TPU v7x, 32 devices: a whole 2x2x4 slice. The times are simulated.
32 devices in a mesh: batch: 2 (over x), row: 4 (over y, core), col: 4 (over z).
Axes of the slice: x: 2, y: 2, z: 4, core: 2. Of those that a mesh axis runs over, the one named last changes fastest.
Arguments:
- tokens_in: bfloat16 [4, 32, 32, 1152], P('batch', 'row', 'col'), may hold values from -6 to 6
- timesteps: int32 [4], replicated, may hold values from 0 to 999
- ada_weight: bfloat16 [2, 1152, 6912], P(None, 'batch'), may hold values from -0.1875 to 0.1875
- ada_bias: bfloat16 [2, 6912], P(None, 'batch'), may hold values from -3 to 3
- conv_taps: bfloat16 [2, 9, 1152], P(None, None, 'batch'), may hold values from -2 to 2
- qkv_weight: bfloat16 [2, 1152, 3456], P(None, 'batch'), may hold values from -0.1875 to 0.1875
- decay_weight: bfloat16 [2, 1152, 16], P(None, 'batch'), may hold values from -0.75 to 0.75
- decay_bias: bfloat16 [2, 16], P(None, 'batch'), may hold values from 1 to 5
- proj_weight: bfloat16 [2, 1152, 1152], P(None, 'batch'), may hold values from -0.1875 to 0.1875
- expand_weight: bfloat16 [2, 1152, 4608], P(None, 'batch'), may hold values from -0.1875 to 0.1875
- shrink_weight: bfloat16 [2, 4608, 1152], P(None, 'batch'), may hold values from -0.09375 to 0.09375
- cotangent: bfloat16 [4, 32, 32, 1152], P('batch', 'row', 'col'), may hold values from -6 to 6
Outputs:
- block_out: bfloat16 [4, 32, 32, 1152], P('batch', 'row', 'col')
- grad_tokens: bfloat16 [4, 32, 32, 1152], P('batch', 'row', 'col')
- grad_ada_weight: float32 [2, 1152, 6912], P(None, 'batch')
- grad_ada_bias: float32 [2, 6912], P(None, 'batch')
- grad_conv_taps: float32 [2, 9, 1152], P(None, None, 'batch')
- grad_qkv_weight: float32 [2, 1152, 3456], P(None, 'batch')
- grad_decay_weight: float32 [2, 1152, 16], P(None, 'batch')
- grad_decay_bias: float32 [2, 16], P(None, 'batch')
- grad_proj_weight: float32 [2, 1152, 1152], P(None, 'batch')
- grad_expand_weight: float32 [2, 1152, 4608], P(None, 'batch')
- grad_shrink_weight: float32 [2, 4608, 1152], P(None, 'batch')
All inputs are finite; a program needn't handle non-finite values.
Results may differ from a plain program's by a relative error of at most 0.025.
The roundings to bfloat16 on the way count: a program that leaves them out, or rounds other values in their place, can miss the bound.
Values may be sent and summed in bfloat16 or wider, within the bound.
No kernel may reach another device: no remote copies, remote signals or barrier semaphores. Data moves between devices by JAX's collectives and lax.ppermute only.
A program may use at most 576 MiB of HBM per device.

v0:
```python
from functools import partial

import jax
import jax.numpy as jnp
from jax import lax
from jax.sharding import PartitionSpec as P

D = 1152
H = 16
HD = 72
LAYERS = 2
ITEMS_DEV = 2


EPS = 1e-06
ACCURATE = lax.Precision.HIGHEST
FLOAT = jnp.float32
BFLOAT = jnp.bfloat16


def extended(cells, sides, width):
    for axis, dim in sides:
        count = lax.axis_size(axis)
        ends = count - 1
        head = lax.slice_in_dim(cells, 0, width, axis=dim)
        tail = lax.slice_in_dim(cells, cells.shape[dim] - width, cells.shape[dim], axis=dim)
        cells = jnp.concatenate(
            [
                lax.ppermute(tail, axis, [(i, (i + 1) % count) for i in range(ends)]),
                cells,
                lax.ppermute(head, axis, [((i + 1) % count, i) for i in range(ends)]),
            ],
            axis=dim,
        )
    return cells


def prefix_2(value, axis, combine, identity, reverse):
    count, position = (lax.axis_size(axis), lax.axis_index(axis))
    everything = jax.tree.map(lambda part: lax.all_gather(part, axis), value)
    start = jax.tree.map(
        lambda part, zero: jnp.broadcast_to(jnp.asarray(zero, part.dtype), part.shape),
        value,
        identity,
    )

    def turn(k, before):
        at = count - 1 - k if reverse else k
        reached = at > position if reverse else at < position
        new = combine(before, jax.tree.map(lambda part: part[at], everything))
        return jax.tree.map(lambda a, b: jnp.where(reached, a, b), new, before)

    return lax.fori_loop(0, count, turn, start)


def contract_rows(left, right):
    return lax.dot_general(left, right, (((0,), (0,)), ((), ())), preferred_element_type=FLOAT)


def contract_cols(left, right):
    return lax.dot_general(left, right, (((1,), (1,)), ((), ())), preferred_element_type=FLOAT)


def flatten_rows(values):
    return values.reshape(-1, values.shape[-1])


def embed_steps(steps):
    half = D // 2
    freqs = jnp.exp(-jnp.log(10000.0) * jnp.arange(half, dtype=FLOAT) / half)
    angles = steps.astype(FLOAT)[:, None] * freqs[None, :]
    return jnp.concatenate([jnp.cos(angles), jnp.sin(angles)], axis=1)


def layer_norm(values):
    center = values - jnp.mean(values, axis=-1, keepdims=True)
    spread = jnp.mean(center * center, axis=-1, keepdims=True)
    return center * lax.rsqrt(spread + EPS)


def split_parts(modulation):
    return modulation.reshape(modulation.shape[0], 6, 1, 1, D)


def pre_mixer(tokens, modulation):
    parts = split_parts(modulation)
    return layer_norm(tokens) * (1.0 + parts[:, 1]) + parts[:, 0]


def post_mixer(tokens, branch, modulation):
    return tokens + split_parts(modulation)[:, 2] * branch


def pre_feed(middle, modulation):
    parts = split_parts(modulation)
    return layer_norm(middle) * (1.0 + parts[:, 4]) + parts[:, 3]


def post_feed(middle, outer, modulation):
    return middle + split_parts(modulation)[:, 5] * outer


def orient_tile(array, layer):
    if layer % 2 == 1:
        return jnp.swapaxes(array, 1, 2)
    return array


def chain_combine(earlier, later):
    return (earlier[0] * later[0], later[0][..., None, None] * earlier[1] + later[1])


def tile_output(queries, keys_in, values_in, logdecay, state_in):
    scale = HD ** (-0.5)
    cumul = jnp.cumsum(logdecay, axis=2)
    trans = jnp.transpose(cumul, (0, 1, 3, 2))
    gap = trans[..., :, None] - trans[..., None, :]
    length = logdecay.shape[2]
    lower = jnp.arange(length)[:, None] >= jnp.arange(length)[None, :]
    weights = jnp.where(lower, jnp.exp(jnp.minimum(gap, 0.0)), 0.0)
    scores = jnp.einsum("irthd,irshd->irhts", queries, keys_in, precision=ACCURATE) * scale
    inside = jnp.einsum("irhts,irshe->irthe", scores * weights, values_in, precision=ACCURATE)
    scaled = queries * (scale * jnp.exp(cumul))[..., None]
    carried = jnp.einsum("irthd,irhde->irthe", scaled, state_in, precision=ACCURATE)
    return inside + carried


def tile_summary(keys_in, values_in, logdecay):
    cumul = jnp.cumsum(logdecay, axis=2)
    total = cumul[:, :, -1]
    weight = jnp.exp(total[:, :, None, :] - cumul)
    state = jnp.einsum("irch,irchd,irche->irhde", weight, keys_in, values_in, precision=ACCURATE)
    return (jnp.exp(total), state)


def conv_apply(padded, taps, rows, cols):
    total = jnp.zeros((padded.shape[0], rows, cols, padded.shape[3]), FLOAT)
    for row_tap in range(3):
        for col_tap in range(3):
            window = padded[:, row_tap : row_tap + rows, col_tap : col_tap + cols].astype(FLOAT)
            total = total + taps[3 * row_tap + col_tap] * window
    return total


def fetch_layer(shards, layer):
    pieces = tuple((piece[layer] for piece in shards))
    others = (
        lax.all_gather(pieces[1], "batch", axis=0, tiled=True),
        lax.all_gather(pieces[2], "batch", axis=1, tiled=True),
        lax.all_gather(pieces[3], "batch", axis=0, tiled=True),
        lax.all_gather(pieces[4], "batch", axis=0, tiled=True),
        lax.all_gather(pieces[5], "batch", axis=0, tiled=True),
        lax.all_gather(pieces[6], "batch", axis=0, tiled=True),
        lax.all_gather(pieces[7], "batch", axis=0, tiled=True),
        lax.all_gather(pieces[8], "batch", axis=0, tiled=True),
    )
    return (pieces[0],) + tuple(others)


def modulate(context, ada_weight, ada_bias, items):
    cond_low, cond_slice = context
    partial_mod = jnp.dot(cond_slice, ada_weight, preferred_element_type=FLOAT)
    every_mod = lax.psum(partial_mod, "batch")
    product = lax.dynamic_slice_in_dim(every_mod, lax.axis_index("batch") * items, items, 0)
    return product + ada_bias.astype(FLOAT)[None, :]


def forward_layer(tokens, context, fetched, layer):
    (
        ada_weight,
        ada_bias,
        conv_taps,
        qkv_weight,
        decay_weight,
        decay_bias,
        proj_weight,
        expand_weight,
        shrink_weight,
    ) = fetched
    items, rows, cols = (tokens.shape[0], tokens.shape[1], tokens.shape[2])
    modulation = modulate(context, ada_weight, ada_bias, items)
    hidden = pre_mixer(tokens, modulation).astype(BFLOAT)
    padded = extended(hidden, (("row", 1), ("col", 2)), 1)
    convolved = conv_apply(padded, conv_taps.astype(FLOAT), rows, cols)
    mixed_rows = jax.nn.silu(convolved).astype(BFLOAT).reshape(-1, D)
    project = jnp.dot(mixed_rows, qkv_weight, preferred_element_type=FLOAT)
    logit = (
        jnp.dot(mixed_rows, decay_weight, preferred_element_type=FLOAT)
        + decay_bias.astype(FLOAT)[None, :]
    )
    logdecay = orient_tile(jax.nn.log_sigmoid(logit).reshape(items, rows, cols, H), layer)
    heads = project.reshape(items, rows, cols, 3, H, HD)
    queries = orient_tile(heads[:, :, :, 0], layer)
    keys_in = orient_tile(heads[:, :, :, 1], layer)
    values_in = orient_tile(heads[:, :, :, 2], layer)
    decay, state = tile_summary(keys_in, values_in, logdecay)
    starting = (jnp.ones_like(decay), jnp.zeros_like(state))
    if layer % 2 == 0:
        prefix = prefix_2((decay, state), "col", chain_combine, starting, False)
    else:
        prefix = prefix_2((decay, state), "row", chain_combine, starting, False)
    state_in = prefix[1]
    attend = orient_tile(tile_output(queries, keys_in, values_in, logdecay, state_in), layer)
    attend_low = attend.reshape(-1, D).astype(BFLOAT)
    branch = jnp.dot(attend_low, proj_weight, preferred_element_type=FLOAT).reshape(
        items, rows, cols, D
    )
    middle = post_mixer(tokens, branch, modulation)
    second = pre_feed(middle, modulation).astype(BFLOAT).reshape(-1, D)
    inner = jnp.dot(second, expand_weight, preferred_element_type=FLOAT)
    active = jax.nn.gelu(inner, approximate=True).astype(BFLOAT)
    outer = jnp.dot(active, shrink_weight, preferred_element_type=FLOAT).reshape(
        items, rows, cols, D
    )
    result = post_feed(middle, outer, modulation)
    saved = (
        tokens,
        modulation,
        padded,
        convolved,
        mixed_rows,
        logit,
        queries,
        keys_in,
        values_in,
        logdecay,
        state_in,
        decay,
        attend_low,
        branch,
        middle,
        second,
        inner,
        active,
        outer,
    )
    return (result, saved)


def backward_layer(delta, saved, fetched, context, layer):
    (
        ada_weight,
        ada_bias,
        conv_taps,
        qkv_weight,
        decay_weight,
        decay_bias,
        proj_weight,
        expand_weight,
        shrink_weight,
    ) = fetched
    (
        tokens,
        modulation,
        padded,
        convolved,
        mixed_rows,
        logit,
        queries,
        keys_in,
        values_in,
        logdecay,
        state_in,
        decay,
        attend_low,
        branch,
        middle,
        second,
        inner,
        active,
        outer,
    ) = saved
    cond_low, cond_slice = context
    items, rows, cols = (tokens.shape[0], tokens.shape[1], tokens.shape[2])
    grid_shape = (items, rows, cols)
    whole = (items, rows, cols, D)
    group_size = lax.axis_size("batch")
    own_index = lax.axis_index("batch")
    columns = (
        lax.all_to_all(second.reshape(whole), "batch", split_axis=3, concat_axis=0, tiled=True),
        lax.all_to_all(mixed_rows.reshape(whole), "batch", split_axis=3, concat_axis=0, tiled=True),
        lax.all_to_all(attend_low.reshape(whole), "batch", split_axis=3, concat_axis=0, tiled=True),
        lax.all_to_all(
            active.reshape(grid_shape + (-1,)), "batch", split_axis=3, concat_axis=0, tiled=True
        ),
        lax.all_to_all(padded, "batch", split_axis=3, concat_axis=0, tiled=True),
    )
    _, feed_out_back = jax.vjp(post_feed, middle, outer, modulation)
    delta_mid_a, delta_outer, delta_mod_a = feed_out_back(delta)
    outer_low = delta_outer.reshape(-1, D).astype(BFLOAT)
    delta_active = contract_cols(outer_low, shrink_weight)
    _, gelu_back = jax.vjp(partial(jax.nn.gelu, approximate=True), inner)
    inner_low = gelu_back(delta_active)[0].astype(BFLOAT)
    delta_second = contract_cols(inner_low, expand_weight)
    _, feed_in_back = jax.vjp(pre_feed, middle, modulation)
    delta_mid_b, delta_mod_b = feed_in_back(delta_second.reshape(whole))
    delta_middle = delta_mid_a + delta_mid_b
    _, mixer_out_back = jax.vjp(post_mixer, tokens, branch, modulation)
    delta_tok_a, delta_branch, delta_mod_c = mixer_out_back(delta_middle)
    branch_low = delta_branch.reshape(-1, D).astype(BFLOAT)
    delta_attend = contract_cols(branch_low, proj_weight)
    delta_attend = orient_tile(delta_attend.reshape(items, rows, cols, H, HD), layer)
    _, output_back = jax.vjp(tile_output, queries, keys_in, values_in, logdecay, state_in)
    delta_query, delta_key_a, delta_value_a, delta_decay_a, delta_state = output_back(delta_attend)
    ending = (jnp.ones_like(decay), jnp.zeros_like(delta_state))
    if layer % 2 == 0:
        later = prefix_2((decay, delta_state), "col", chain_combine, ending, True)
    else:
        later = prefix_2((decay, delta_state), "row", chain_combine, ending, True)
    carried = later[1]
    delta_total = jnp.sum(carried * state_in, axis=(-2, -1))
    _, summary_back = jax.vjp(tile_summary, keys_in, values_in, logdecay)
    delta_key_b, delta_value_b, delta_decay_b = summary_back((delta_total, carried))
    stacked = jnp.stack(
        [
            orient_tile(delta_query, layer),
            orient_tile(delta_key_a + delta_key_b, layer),
            orient_tile(delta_value_a + delta_value_b, layer),
        ],
        axis=3,
    )
    delta_project = stacked.reshape(-1, 3 * D).astype(BFLOAT)
    delta_logdecay = orient_tile(delta_decay_a + delta_decay_b, layer).reshape(-1, H)
    delta_logit = (delta_logdecay * jax.nn.sigmoid(-logit)).astype(BFLOAT)
    delta_mixed = contract_cols(delta_project, qkv_weight) + contract_cols(
        delta_logit, decay_weight
    )
    _, silu_back = jax.vjp(jax.nn.silu, convolved)
    delta_conv = silu_back(delta_mixed.reshape(whole))[0].astype(BFLOAT)
    delta_pad = extended(delta_conv, (("row", 1), ("col", 2)), 1)
    taps = conv_taps.astype(FLOAT)
    delta_hidden = jnp.zeros(whole, FLOAT)
    for row_tap in range(3):
        for col_tap in range(3):
            beside_all = delta_pad[
                :, 2 - row_tap : 2 - row_tap + rows, 2 - col_tap : 2 - col_tap + cols
            ].astype(FLOAT)
            delta_hidden = delta_hidden + taps[3 * row_tap + col_tap] * beside_all
    _, mixer_in_back = jax.vjp(pre_mixer, tokens, modulation)
    delta_tok_b, delta_mod_d = mixer_in_back(delta_hidden)
    delta_tokens = delta_tok_a + delta_tok_b
    delta_mod = delta_mod_a + delta_mod_b + delta_mod_c + delta_mod_d
    spread = (
        lax.all_gather(outer_low.reshape(whole), "batch", axis=0, tiled=True),
        lax.all_gather(inner_low.reshape(grid_shape + (-1,)), "batch", axis=0, tiled=True),
        lax.all_gather(branch_low.reshape(whole), "batch", axis=0, tiled=True),
        lax.all_gather(delta_project.reshape(grid_shape + (3 * D,)), "batch", axis=0, tiled=True),
        lax.all_gather(delta_logit.reshape(grid_shape + (H,)), "batch", axis=0, tiled=True),
        lax.all_gather(delta_conv, "batch", axis=0, tiled=True),
    )
    second_cols, mixed_cols, attend_cols, active_cols, padded_cols = columns
    outer_every, inner_every, branch_every, project_every, logit_every, conv_every = spread
    grad_shrink = contract_rows(flatten_rows(active_cols), flatten_rows(outer_every))
    grad_expand = contract_rows(flatten_rows(second_cols), flatten_rows(inner_every))
    grad_proj = contract_rows(flatten_rows(attend_cols), flatten_rows(branch_every))
    grad_qkv = contract_rows(flatten_rows(mixed_cols), flatten_rows(project_every))
    grad_decay = contract_rows(flatten_rows(mixed_cols), flatten_rows(logit_every))
    head_width = H // group_size
    logit_totals = jnp.sum(logit_every.astype(FLOAT), axis=(0, 1, 2))
    grad_decay_bias = lax.dynamic_slice_in_dim(logit_totals, own_index * head_width, head_width, 0)
    own_width = D // group_size
    conv_own = lax.dynamic_slice_in_dim(conv_every, own_index * own_width, own_width, 3).astype(
        FLOAT
    )
    tap_grads = []
    for row_tap in range(3):
        for col_tap in range(3):
            window = padded_cols[:, row_tap : row_tap + rows, col_tap : col_tap + cols].astype(
                FLOAT
            )
            tap_grads.append(jnp.sum(window * conv_own, axis=(0, 1, 2)))
    grad_taps = jnp.stack(tap_grads)
    every_delta = lax.all_gather(delta_mod, "batch", axis=0, tiled=True)
    grad_rows = lax.dot_general(
        cond_slice.astype(FLOAT), every_delta, (((0,), (0,)), ((), ())), precision=ACCURATE
    )
    width = ada_bias.shape[0] // group_size
    bias_rows = lax.dynamic_slice_in_dim(jnp.sum(every_delta, axis=0), own_index * width, width, 0)
    totals = lax.psum(
        (
            grad_rows,
            bias_rows,
            grad_taps,
            grad_qkv,
            grad_decay,
            grad_decay_bias,
            grad_proj,
            grad_expand,
            grad_shrink,
        ),
        ("row", "col"),
    )
    return (delta_tokens, totals)


def per_device(
    tokens_in,
    timesteps,
    ada_weight,
    ada_bias,
    conv_taps,
    qkv_weight,
    decay_weight,
    decay_bias,
    proj_weight,
    expand_weight,
    shrink_weight,
    cotangent,
):
    shards = (
        ada_weight,
        ada_bias,
        conv_taps,
        qkv_weight,
        decay_weight,
        decay_bias,
        proj_weight,
        expand_weight,
        shrink_weight,
    )
    cond_every = jax.nn.silu(embed_steps(timesteps)).astype(BFLOAT)
    cond_low = lax.dynamic_slice_in_dim(
        cond_every, lax.axis_index("batch") * ITEMS_DEV, ITEMS_DEV, 0
    )
    width = ada_weight.shape[1]
    cond_slice = lax.dynamic_slice_in_dim(cond_every, lax.axis_index("batch") * width, width, 1)
    context = (cond_low, cond_slice)
    tokens = tokens_in.astype(FLOAT)
    inputs = []
    stored = []
    latest = None
    for layer in range(LAYERS):
        fetched = fetch_layer(shards, layer)
        inputs.append(tokens)
        tokens, saved = forward_layer(tokens, context, fetched, layer)
        latest = (fetched, saved)
        stored.append((fetched, saved))
    block_out = tokens.astype(BFLOAT)
    delta = cotangent.astype(FLOAT)
    layer_sums = [None] * LAYERS
    for layer in reversed(range(LAYERS)):
        if layer == LAYERS - 1:
            fetched, saved = latest
        else:
            fetched, saved = stored[layer]
        delta, layer_sums[layer] = backward_layer(delta, saved, fetched, context, layer)
    stacks = [jnp.stack([sums[member] for sums in layer_sums]) for member in range(9)]
    return (
        block_out,
        delta.astype(BFLOAT),
        stacks[0],
        stacks[1],
        stacks[2],
        stacks[3],
        stacks[4],
        stacks[5],
        stacks[6],
        stacks[7],
        stacks[8],
    )


def solution(mesh):
    return jax.shard_map(
        per_device,
        mesh=mesh,
        in_specs=(
            P("batch", "row", "col", None),
            P(),
            P(None, "batch", None),
            P(None, "batch"),
            P(None, None, "batch"),
            P(None, "batch", None),
            P(None, "batch", None),
            P(None, "batch"),
            P(None, "batch", None),
            P(None, "batch", None),
            P(None, "batch", None),
            P("batch", "row", "col", None),
        ),
        out_specs=(
            P("batch", "row", "col", None),
            P("batch", "row", "col", None),
            P(None, "batch", None),
            P(None, "batch"),
            P(None, None, "batch"),
            P(None, "batch", None),
            P(None, "batch", None),
            P(None, "batch"),
            P(None, "batch", None),
            P(None, "batch", None),
            P(None, "batch", None),
        ),
        check_vma=False,
    )
```

profile of v0, /device:TPU:0, one launch (start us, length us, event | category | flops | bytes accessed | tf_op | source)
XLA Modules:
  0.0 4820.1 jit_solution(11661264211182220092)
XLA Ops:
  47.6 35.3 slice_reduce_fusion.17
  125.4 27.0 all-gather.49.cloned.1.call-done
  223.6 40.5 all-gather.5
  272.2 548.3 %all-gather.51.cloned.1.call-done = f32[8,8,16,72,72]{4,3,2,1,0:T(8,128)} async-done(((f32[2,8,16,72,72]{4,3,2,1,0:T(8,128)}), f32[8,8,16,72,72]{4,3,2,1,0:T(8,128)}) %all-gather.51.cloned.1.call-update) | async-done | bytes 21233680 | tf_op jit(solution)/shard_map/all_gather | solution.py:40
  820.5 43.1 while.60
  879.5 113.4 %all-gather.55.cloned.1.call-done = bf16[1,1152,4608]{2,1,0:T(8,128)(2,1)} async-done(((bf16[1,576,4608]{2,1,0:T(8,128)(2,1)}), bf16[1,1152,4608]{2,1,0:T(8,128)(2,1)}) %all-gather.55.cloned.1.call-update) | async-done | bytes 10616848 | tf_op jit(solution)/shard_map/all_gather | solution.py:154
  1000.4 125.5 %all-gather.57.cloned.1.call-done = bf16[1,4608,1152]{2,1,0:T(8,128)(2,1)} async-done(((bf16[1,2304,1152]{2,1,0:T(8,128)(2,1)}), bf16[1,4608,1152]{2,1,0:T(8,128)(2,1)}) %all-gather.57.cloned.1.call-update) | async-done | bytes 10616848 | tf_op jit(solution)/shard_map/all_gather | solution.py:155
  1155.9 35.5 slice_reduce_fusion.8
  1208.6 29.9 all-gather.59.cloned.1.call-done
  1304.0 209.7 %all-gather.61.cloned.1.call-done = f32[8,8,16,72,72]{4,3,2,1,0:T(8,128)} async-done(((f32[2,8,16,72,72]{4,3,2,1,0:T(8,128)}), f32[8,8,16,72,72]{4,3,2,1,0:T(8,128)}) %all-gather.61.cloned.1.call-update) | async-done | bytes 21233680 | tf_op jit(solution)/shard_map/all_gather | solution.py:40
  1513.7 43.7 while.61
  1573.9 113.7 %all-gather.65.cloned.1.call-done = bf16[1,1152,4608]{2,1,0:T(8,128)(2,1)} async-done(((bf16[1,576,4608]{2,1,0:T(8,128)(2,1)}), bf16[1,1152,4608]{2,1,0:T(8,128)(2,1)}) %all-gather.65.cloned.1.call-update) | async-done | bytes 10616848 | tf_op jit(solution)/shard_map/all_gather | solution.py:154
  1695.7 125.0 %all-gather.67.cloned.1.call-done = bf16[1,4608,1152]{2,1,0:T(8,128)(2,1)} async-done(((bf16[1,2304,1152]{2,1,0:T(8,128)(2,1)}), bf16[1,4608,1152]{2,1,0:T(8,128)(2,1)}) %all-gather.67.cloned.1.call-update) | async-done | bytes 10616848 | tf_op jit(solution)/shard_map/all_gather | solution.py:155
  1906.0 187.5 %all-gather.69.cloned.1.call-done = f32[8,8,16,72,72]{4,3,2,1,0:T(8,128)} async-done(((f32[2,8,16,72,72]{4,3,2,1,0:T(8,128)}), f32[8,8,16,72,72]{4,3,2,1,0:T(8,128)}) %all-gather.69.cloned.1.call-update) | async-done | bytes 21233680 | tf_op jit(solution)/shard_map/all_gather | solution.py:40
  2093.5 43.9 while.62
  2394.3 30.0 reshape.692
  2479.4 29.9 reshape.690
  2513.9 21.9 all_gather.165
  2652.4 31.6 reshape.693
  2745.3 31.5 reshape.691
  2917.6 45.0 while.63
  3070.0 87.7 %all-reduce.24.cloned.1.call-done = (f32[1,3456]{1,0:T(1,128)}, f32[1,3456]{1,0:T(1,128)}, f32[1,9,576]{2,1,0:T(8,128)}, f32[1,9,576]{2,1,0:T(8,128)}, f32[1,576...) async-done(((f32[1,3456]{1,0:T(1,128)}, f32[1,3456]{1,0:T(1,128)}, f32[1,9,576]{2,1,0:T(8,128)}, f32[1,9,576]{2,1,0:T(8,128)}, ...) | async-done | bytes 142928 | tf_op jit(solution)/shard_map/psum | solution.py:379
  3163.2 1587.7 %all-reduce.26.cloned.1.call-done = (f32[1,576,6912]{2,1,0:T(8,128)}, f32[1,576,6912]{2,1,0:T(8,128)}, f32[1,576,3456]{2,1,0:T(8,128)}, f32[1,576,3456]{2,1,0:T(...) async-done(((f32[1,576,6912]{2,1,0:T(8,128)}, ...) | async-done | bytes 95551504 | tf_op jit(solution)/shard_map/psum | solution.py:379
  4750.9 24.4 pad_maximum_fusion
  (930 shorter events, 1365.3 us)
Async XLA Ops:
  7.2 75.9 %all-reduce.28.cloned.1.call-start = ((), (), s32[]{:S(2)}) async-start(), calls=%async_computation.28 | async-start | bytes 442368 | tf_op jit(solution)/shard_map/psum | solution.py:163
  18.3 134.1 %all-gather.49.cloned.1.call-start = ((), (), s32[]{:S(2)}) async-start(), calls=%async_computation.14 | async-start | bytes 11943936 | tf_op jit(solution)/shard_map/all_gather | solution.py:150
  24.1 796.4 %all-gather.51.cloned.1.call-start = ((), (), s32[]{:S(2)}) async-start(), calls=%async_computation.15 | async-start | bytes 47185920 | tf_op jit(solution)/shard_map/all_gather | solution.py:40
  188.4 686.7 %all-gather.53.cloned.1.call-start = ((), (), s32[]{:S(2)}) async-start(), calls=%async_computation.16 | async-start | bytes 3981312 | tf_op jit(solution)/shard_map/all_gather | solution.py:153
  191.9 801.0 %all-gather.55.cloned.1.call-start = ((), (), s32[]{:S(2)}) async-start(), calls=%async_computation.17 | async-start | bytes 15925248 | tf_op jit(solution)/shard_map/all_gather | solution.py:154
  205.0 920.9 %all-gather.57.cloned.1.call-start = ((), (), s32[]{:S(2)}) async-start(), calls=%async_computation.18 | async-start | bytes 15925248 | tf_op jit(solution)/shard_map/all_gather | solution.py:155
  215.6 1022.9 %all-gather.59.cloned.1.call-start = ((), (), s32[]{:S(2)}) async-start(), calls=%async_computation.19 | async-start | bytes 11943936 | tf_op jit(solution)/shard_map/all_gather | solution.py:150
  216.3 1297.4 %all-gather.61.cloned.1.call-start = ((), (), s32[]{:S(2)}) async-start(), calls=%async_computation.20 | async-start | bytes 47185920 | tf_op jit(solution)/shard_map/all_gather | solution.py:40
  1151.3 98.7 %collective-permute-start.6 = (bf16[2,10,1,1152]{3,2,1,0:T(2,128)(2,1)S(1)}, bf16[2,10,1,1152]{3,2,1,0:T(2,128)(2,1)S(1)}, u32[]{:S(2)}, u32[]{:S(2)}) collective-permute-start(bf16[2,10,1,1152]{3,2,1,0:T(2,128)(2,1)S(1)} %get-tuple-element.770), channel_id=1, source_target_pairs={{0,1},{1,2},{2,3},{4,5},{5,6},{6,7},{8,9},{9,10},{10,11},{12,13},{... | collective-permute-start | bytes 138248 | tf_op jit(solution)/shard_map/ppermute | solution.py:29
  1154.6 95.3 %collective-permute-start.7 = (bf16[2,10,1,1152]{3,2,1,0:T(2,128)(2,1)S(1)}, bf16[2,10,1,1152]{3,2,1,0:T(2,128)(2,1)S(1)}, u32[]{:S(2)}, u32[]{:S(2)}) collective-permute-start(bf16[2,10,1,1152]{3,2,1,0:T(2,128)(2,1)S(1)} %get-tuple-element.771), channel_id=1, source_target_pairs={{1,0},{2,1},{3,2},{5,4},{6,5},{7,6},{9,8},{10,9},{11,10},{13,12},{... | collective-permute-start | bytes 138248 | tf_op jit(solution)/shard_map/ppermute | solution.py:31
  1286.0 283.2 %all-gather.63.cloned.1.call-start = ((), (), s32[]{:S(2)}) async-start(), calls=%async_computation.21 | async-start | bytes 3981312 | tf_op jit(solution)/shard_map/all_gather | solution.py:153
  1286.7 400.9 %all-gather.65.cloned.1.call-start = ((), (), s32[]{:S(2)}) async-start(), calls=%async_computation.22 | async-start | bytes 15925248 | tf_op jit(solution)/shard_map/all_gather | solution.py:154
  1287.3 533.4 %all-gather.67.cloned.1.call-start = ((), (), s32[]{:S(2)}) async-start(), calls=%async_computation.23 | async-start | bytes 15925248 | tf_op jit(solution)/shard_map/all_gather | solution.py:155
  1288.1 805.4 %all-gather.69.cloned.1.call-start = ((), (), s32[]{:S(2)}) async-start(), calls=%async_computation.24 | async-start | bytes 47185920 | tf_op jit(solution)/shard_map/all_gather | solution.py:40
  1866.1 938.6 %all-gather.47.cloned.1.call-start = ((), (), s32[]{:S(2)}) async-start(), calls=%async_computation.13 | async-start | bytes 3538944 | tf_op jit(solution)/shard_map/all_gather | solution.py:345
  1900.6 1003.6 %all-gather.43.cloned.1.call-start = ((), (), s32[]{:S(2)}) async-start(), calls=%async_computation.11 | async-start | bytes 2654208 | tf_op jit(solution)/shard_map/all_gather | solution.py:347
  2202.2 708.0 %all-gather.45.cloned.1.call-start = ((), (), s32[]{:S(2)}) async-start(), calls=%async_computation.12 | async-start | bytes 3538944 | tf_op jit(solution)/shard_map/all_gather | solution.py:345
  2214.7 703.0 %all-gather.71.cloned.1.call-start = ((), (), s32[]{:S(2)}) async-start(), calls=%async_computation.25 | async-start | bytes 47185920 | tf_op jit(solution)/shard_map/all_gather | solution.py:40
  2373.8 50.4 %all-to-all-start.1 = ((bf16[2,2,57600]{2,1,0:T(2,128)(2,1)}), bf16[2,2,57600]{2,1,0:T(2,128)(2,1)}, u32[]{:S(2)}, u32[]{:S(2)}) async-start(bf16[2,2,57600]{2,1,0:T(2,128)(2,1)} %reshape.674), calls=%async_computation.1 | async-start | bytes 921600 | tf_op jit(solution)/shard_map/all_to_all | solution.py:286
  2459.5 49.9 %all-to-all-start.7 = ((bf16[2,2,36864]{2,1,0:T(2,128)(2,1)}), bf16[2,2,36864]{2,1,0:T(2,128)(2,1)S(1)}, u32[]{:S(2)}, u32[]{:S(2)}) async-start(bf16[2,2,36864]{2,1,0:T(2,128)(2,1)} %reshape.686), calls=%async_computation.7 | async-start | bytes 589824 | tf_op jit(solution)/shard_map/all_to_all | solution.py:280
  2509.4 236.0 %all-to-all-start.9 = ((bf16[2,2,147456]{2,1,0:T(2,128)(2,1)}), bf16[2,2,147456]{2,1,0:T(2,128)(2,1)}, u32[]{:S(2)}, u32[]{:S(2)}) async-start(bf16[2,2,147456]{2,1,0:T(2,128)(2,1)} %reshape.690), calls=%async_computation.9 | async-start | bytes 2359296 | tf_op jit(solution)/shard_map/all_to_all | solution.py:283
  2513.8 548.2 %all-gather.41.cloned.1.call-start = ((), (), s32[]{:S(2)}) async-start(), calls=%async_computation.10 | async-start | bytes 2654208 | tf_op jit(solution)/shard_map/all_gather | solution.py:347
  3031.0 126.7 %all-reduce.24.cloned.1.call-start = ((), (), s32[]{:S(2)}) async-start(), calls=%async_computation.26 | async-start | bytes 385024 | tf_op jit(solution)/shard_map/psum | solution.py:379
  3058.4 1692.5 %all-reduce.26.cloned.1.call-start = ((), (), s32[]{:S(2)}) async-start(), calls=%async_computation.27 | async-start | bytes 191102976 | tf_op jit(solution)/shard_map/psum | solution.py:379
  (242 other events, 6418.1 us)
Sparse Core Ops, SparseCore 0:
  18.5 25.8 all-reduce.27
  46.5 105.8 all-gather.48
  188.5 631.9 all-gather.50
  821.9 37.9 all-gather.52
  861.9 130.9 all-gather.54
  994.9 130.9 all-gather.56
  1127.4 111.0 all-gather.58
  1286.1 227.5 all-gather.60
  1515.2 39.3 all-gather.62
  1556.6 130.9 all-gather.64
  1689.7 130.9 all-gather.66
  1866.2 227.2 all-gather.68
  2095.0 36.0 all-gather.46
  2202.3 30.6 all-gather.42
  2235.0 38.8 all-gather.44
  2275.3 631.8 all-gather.70
  3031.1 30.9 all-gather.40
  3066.9 90.7 all-reduce.23
  3165.3 1585.5 all-reduce.25
where the time goes:
time: 4840 us; the launch traced here: 4820 us
  waiting for transfers between devices  3170 us (65%)
  local copies, waits for them, and re-layouts  651 us (13%)
  matrix products  407 us (8%)
  other arithmetic  294 us (6%)
  blocking collectives  206 us (4%)
  starting transfers between devices  75.8 us (2%)
    psum x2, waiting for transfers between devices, backward_layer(): lax.psum((grad_rows, bias_rows, grad_taps, grad_qkv, grad_decay, grad_dec...  1680 us
    all_gather x4, waiting for transfers between devices, prefix_2(): everything = jax.tree.map(lambda part: lax.all_gather(part, axis), value)  945 us
    unnamed x491, local copies, waits for them, and re-layouts  298 us
    all_gather x2, waiting for transfers between devices, fetch_layer(): lax.all_gather(pieces[8], 'batch', axis=0, tiled=True)  250 us
    all_gather x2, waiting for transfers between devices, fetch_layer(): lax.all_gather(pieces[7], 'batch', axis=0, tiled=True)  227 us
    select_n x16, other arithmetic, turn(): return jax.tree.map(lambda a, b: jnp.where(reached, a, b), new, before)  173 us
  transfers between devices with their start and end apart: 45, of which 16 were waited for; matrix products, arithmetic and copies ran while one was open for 22% of the time, Pallas kernels for 0%

commit v1 on v0

v1 whole, which is shorter than its diff:
```python
import jax
import jax.numpy as jnp
from jax import lax
from jax.experimental import pallas as pl
from jax.experimental.pallas import tpu as pltpu
from jax.sharding import PartitionSpec as P

D = 1152
H = 16
HD = 72
LAYERS = 2
EPS = 1e-06
ACCURATE = lax.Precision.HIGHEST
FLOAT = jnp.float32
BFLOAT = jnp.bfloat16
LANES = 128
VMEM_LIMIT = 48 * 1024 * 1024
GRID_AXES = ("row", "col")


def params():
    return pltpu.CompilerParams(vmem_limit_bytes=VMEM_LIMIT)


def padded_width(width):
    return -(-width // LANES) * LANES


def swap(value, axis="batch", bit=1):
    count = lax.axis_size(axis)
    return lax.ppermute(value, axis, [(i, i ^ bit) for i in range(count)])


def gather_items(own):
    if lax.axis_size("batch") == 2:
        return jnp.concatenate([own, swap(own)], axis=0)
    return lax.all_gather(own, "batch", axis=0, tiled=True)


def reduce_items(partial):
    if lax.axis_size("batch") == 2:
        items = partial.shape[0] // 2
        return partial[:items] + swap(partial[items:].astype(BFLOAT)).astype(FLOAT)
    return lax.psum_scatter(partial, "batch", scatter_dimension=0, tiled=True)


def lines_out(values, axis):
    count, place = lax.axis_size(axis), lax.axis_index(axis)
    groups = values.reshape((count, -1) + values.shape[1:])
    blocks = []
    for k in range(count):
        block = lax.dynamic_index_in_dim(groups, place ^ k, 0, keepdims=False)
        blocks.append(block if k == 0 else swap(block, axis, k))
    return blocks


def lines_back(blocks, axis):
    count, place = lax.axis_size(axis), lax.axis_index(axis)
    received = [blocks[0]] + [swap(blocks[k], axis, k) for k in range(1, count)]
    stacked = jnp.stack(received)
    return jnp.concatenate(
        [lax.dynamic_index_in_dim(stacked, place ^ j, 0, keepdims=False) for j in range(count)]
    )


def halo(cells):
    rows, cols = lax.axis_size("row"), lax.axis_size("col")
    down = [(i, i + 1) for i in range(rows - 1)]
    up = [(i + 1, i) for i in range(rows - 1)]
    top = lax.ppermute(cells[:, -1], "row", down)
    bottom = lax.ppermute(cells[:, 0], "row", up)
    edge = lambda at: jnp.concatenate([top[:, at][:, None], cells[:, :, at], bottom[:, at][:, None]], 1)
    left = lax.ppermute(edge(-1), "col", [(i, i + 1) for i in range(cols - 1)])
    right = lax.ppermute(edge(0), "col", [(i + 1, i) for i in range(cols - 1)])
    return top, bottom, left, right


def beside(cells, top, bottom, left, right, item):
    count = cells.shape[1]
    lefts, rights = left[item].astype(FLOAT), right[item].astype(FLOAT)
    width = cells.shape[2]
    at = lax.broadcasted_iota(jnp.int32, (width, cells.shape[3]), 0)
    rows = []
    for row in range(count + 2):
        if row == 0:
            here = top[item]
        elif row == count + 1:
            here = bottom[item]
        else:
            here = cells[item, row - 1]
        here = here.astype(FLOAT)
        before = jnp.where(at == 0, lefts[row : row + 1], pltpu.roll(here, 1, 0))
        after = jnp.where(at == width - 1, rights[row : row + 1], pltpu.roll(here, width - 1, 0))
        rows.append((before, here, after))
    return rows


def conv_forward_kernel(cells, top, bottom, left, right, taps, convolved, mixed):
    weights = taps[...].astype(FLOAT)
    for item in range(cells.shape[0]):
        rows = beside(cells, top, bottom, left, right, item)
        for row in range(cells.shape[1]):
            total = jnp.zeros(rows[0][1].shape, FLOAT)
            for a in range(3):
                for b in range(3):
                    total += weights[3 * a + b : 3 * a + b + 1] * rows[row + a][b]
            convolved[item, row] = total
            mixed[item, row] = (total * jax.nn.sigmoid(total)).astype(BFLOAT)


def conv_backward_kernel(
    cells, top, bottom, left, right, delta, dtop, dbottom, dleft, dright, taps, hidden, grads
):
    weights = taps[...].astype(FLOAT)
    sums = [jnp.zeros((cells.shape[2], cells.shape[3]), FLOAT) for _ in range(9)]
    for item in range(cells.shape[0]):
        rows = beside(cells, top, bottom, left, right, item)
        for row in range(cells.shape[1]):
            here = delta[item, row].astype(FLOAT)
            for a in range(3):
                for b in range(3):
                    sums[3 * a + b] += rows[row + a][b] * here
        rows = beside(delta, dtop, dbottom, dleft, dright, item)
        for row in range(cells.shape[1]):
            total = jnp.zeros(rows[0][1].shape, FLOAT)
            for a in range(3):
                for b in range(3):
                    total += weights[3 * a + b : 3 * a + b + 1] * rows[row + 2 - a][2 - b]
            hidden[item, row] = total
    for tap in range(9):
        grads[tap : tap + 1] = jnp.sum(sums[tap], axis=0, keepdims=True)


def conv_specs(items, rows, cols, block):
    cells = pl.BlockSpec((items, rows, cols, block), lambda i: (0, 0, 0, i))
    flat = pl.BlockSpec((items, cols, block), lambda i: (0, 0, i))
    side = pl.BlockSpec((items, rows + 2, block), lambda i: (0, 0, i))
    taps = pl.BlockSpec((9, block), lambda i: (0, i))
    return [cells, flat, flat, side, side], taps


def conv_forward(cells, sides, taps):
    items, rows, cols, width = cells.shape
    block = 3 * LANES
    specs, tap_spec = conv_specs(items, rows, cols, block)
    return pl.pallas_call(
        conv_forward_kernel,
        grid=(width // block,),
        in_specs=specs + [tap_spec],
        out_specs=[specs[0], specs[0]],
        out_shape=[
            jax.ShapeDtypeStruct(cells.shape, FLOAT),
            jax.ShapeDtypeStruct(cells.shape, BFLOAT),
        ],
        compiler_params=params(),
    )(cells, *sides, taps)


def conv_backward(cells, sides, delta, delta_sides, taps):
    items, rows, cols, width = cells.shape
    block = 3 * LANES
    specs, tap_spec = conv_specs(items, rows, cols, block)
    return pl.pallas_call(
        conv_backward_kernel,
        grid=(width // block,),
        in_specs=specs + specs + [tap_spec],
        out_specs=[specs[0], tap_spec],
        out_shape=[
            jax.ShapeDtypeStruct(cells.shape, FLOAT),
            jax.ShapeDtypeStruct((9, width), FLOAT),
        ],
        compiler_params=params(),
    )(cells, *sides, delta, *delta_sides, taps)


def scan_mask(place, rows, cols, along_cols, blocks):
    cells = rows * cols
    shape = (blocks * cells, blocks * cells)

    def line_and_position(index):
        block = index // cells
        inside = index - block * cells
        row = inside // cols
        col = inside - row * cols
        source = place ^ block
        if along_cols:
            return row, source * cols + col
        return col, source * rows + row

    line_t, at_t = line_and_position(lax.broadcasted_iota(jnp.int32, shape, 0))
    line_s, at_s = line_and_position(lax.broadcasted_iota(jnp.int32, shape, 1))
    return (line_t == line_s) & (at_s <= at_t)


def dot(left, right, contract=((1,), (0,)), precision=None):
    return lax.dot_general(
        left, right, (contract, ((), ())), precision=precision, preferred_element_type=FLOAT
    )


class Scan:
    def __init__(self, parts, mask, width):
        self.width = width
        self.padded = padded_width(width + 3 * (width // HD))
        self.heads = width // HD
        joined = jnp.concatenate([part[0] for part in parts], axis=0)
        size = self.padded
        self.queries = joined[:, :size]
        self.keys = joined[:, size : 2 * size]
        self.values = joined[:, 2 * size :]
        self.start = width - width // LANES * LANES
        self.block = width // LANES * LANES
        extra = self.queries[:, self.block : self.block + LANES].astype(FLOAT)
        logit = (
            extra
            + pltpu.roll(extra, LANES - self.heads, 1)
            + pltpu.roll(extra, LANES - 2 * self.heads, 1)
        )
        self.lane = lax.broadcasted_iota(jnp.int32, extra.shape, 1)
        self.is_logit = (self.lane >= self.start) & (self.lane < self.start + self.heads)
        self.logit = jnp.where(self.is_logit, logit, 0.0)
        small = jnp.exp(-jnp.abs(self.logit))
        logdecay = jnp.where(self.is_logit, jnp.minimum(self.logit, 0.0) - jnp.log(1.0 + small), 0.0)
        self.lower = jnp.where(mask, 1.0, 0.0).astype(FLOAT)
        self.mask = mask
        self.cumul = dot(self.lower, logdecay, precision=ACCURATE)
        self.cumul_rows = jnp.transpose(self.cumul)
        self.feature = lax.broadcasted_iota(jnp.int32, (1, size), 1)

    def of_head(self, head, array):
        inside = (self.feature >= head * HD) & (self.feature < head * HD + HD)
        return jnp.where(inside, array, jnp.zeros_like(array))

    def weights(self, head):
        at = self.start + head
        gap = self.cumul[:, at : at + 1] - self.cumul_rows[at : at + 1, :]
        return jnp.where(self.mask, jnp.exp(jnp.minimum(gap, 0.0)), 0.0)


SCALE = HD ** (-0.5)


def scan_forward_kernel(place, *refs, rows, cols, along_cols, width):
    count = len(refs) // 2
    parts, outs = refs[:count], refs[count:]
    mask = scan_mask(place[0], rows, cols, along_cols, count)
    scan = Scan(parts, mask, width)
    total = jnp.zeros(scan.queries.shape, FLOAT)
    for head in range(scan.heads):
        scores = dot(scan.of_head(head, scan.queries), scan.keys, ((1,), (1,))) * SCALE
        scores = (scores * scan.weights(head)).astype(BFLOAT)
        total += dot(scores, scan.of_head(head, scan.values))
    cells = rows * cols
    low = total.astype(BFLOAT)
    for k in range(count):
        outs[k][0] = low[k * cells : (k + 1) * cells, :width]


def scan_backward_kernel(place, *refs, rows, cols, along_cols, width):
    count = len(refs) // 3
    parts, deltas, outs = refs[:count], refs[count : 2 * count], refs[2 * count :]
    mask = scan_mask(place[0], rows, cols, along_cols, count)
    scan = Scan(parts, mask, width)
    joined = jnp.concatenate([part[0] for part in deltas], axis=0)
    short = scan.padded - width
    if short:
        joined = jnp.concatenate([joined, jnp.zeros((joined.shape[0], short), BFLOAT)], axis=1)
    shape = scan.queries.shape
    delta_query = jnp.zeros(shape, FLOAT)
    delta_key = jnp.zeros(shape, FLOAT)
    delta_value = jnp.zeros(shape, FLOAT)
    gap_rows = jnp.zeros(scan.lane.shape, FLOAT)
    gap_cols = jnp.zeros(scan.cumul_rows.shape, FLOAT)
    place_row = lax.broadcasted_iota(jnp.int32, gap_cols.shape, 0)
    for head in range(scan.heads):
        query = scan.of_head(head, scan.queries)
        delta = scan.of_head(head, joined)
        weights = scan.weights(head)
        scores = dot(query, scan.keys, ((1,), (1,))) * SCALE * weights
        delta_scores = dot(delta, scan.values, ((1,), (1,)))
        gap = delta_scores * scores
        at = scan.start + head
        gap_rows += jnp.where(scan.lane == at, jnp.sum(gap, axis=1, keepdims=True), 0.0)
        gap_cols += jnp.where(place_row == at, jnp.sum(gap, axis=0, keepdims=True), 0.0)
        inner = (delta_scores * weights * SCALE).astype(BFLOAT)
        delta_query += dot(inner, scan.of_head(head, scan.keys))
        delta_key += dot(inner, query, ((0,), (0,)))
        delta_value += dot(scores.astype(BFLOAT), delta, ((0,), (0,)))
    delta_cumul = gap_rows - jnp.transpose(gap_cols)
    delta_decay = dot(scan.lower, delta_cumul, ((0,), (0,)), ACCURATE)
    small = jnp.exp(-jnp.abs(scan.logit))
    keep = jnp.where(scan.logit >= 0.0, small, 1.0) / (1.0 + small)
    delta_logit = delta_decay * keep
    block = scan.block
    mixed = jnp.where(scan.is_logit, delta_logit, delta_query[:, block : block + LANES])
    pieces = [delta_query[:, :block]] if block else []
    pieces.append(mixed)
    if block + LANES < scan.padded:
        pieces.append(delta_query[:, block + LANES :])
    whole = jnp.concatenate(pieces + [delta_key, delta_value], axis=1).astype(BFLOAT)
    cells = rows * cols
    for k in range(count):
        outs[k][0] = whole[k * cells : (k + 1) * cells]


def scan_call(kernel, place, inputs, out_width, rows, cols, along_cols, width):
    count = lax.axis_size("col") if along_cols else lax.axis_size("row")
    items, cells = inputs[0].shape[:2]
    spec = lambda last: pl.BlockSpec((1, cells, last), lambda i, place: (i, 0, 0))

    def body(*refs):
        kernel(*refs, rows=rows, cols=cols, along_cols=along_cols, width=width)

    return pl.pallas_call(
        body,
        grid_spec=pltpu.PrefetchScalarGridSpec(
            num_scalar_prefetch=1,
            grid=(items,),
            in_specs=[spec(v.shape[2]) for v in inputs],
            out_specs=[spec(out_width)] * count,
        ),
        out_shape=[jax.ShapeDtypeStruct((items, cells, out_width), BFLOAT)] * count,
        compiler_params=params(),
    )(place.reshape(1).astype(jnp.int32), *inputs)


def pick(values, index):
    chosen = values[0]
    for k in range(1, len(values)):
        chosen = jnp.where(index == k, values[k], chosen)
    return chosen


def fetch_columns(pieces):
    count, place = lax.axis_size("batch"), lax.axis_index("batch")
    if count != 2:
        stacked = jnp.stack(pieces)
        return lax.all_to_all(stacked, "batch", 0, 0).reshape((-1,) + pieces[0].shape[1:])
    own, other = pick(pieces, place), pick(pieces, 1 - place)
    rows = own.shape[0]
    half = rows // 2
    core = lax.axis_index("row") % 2
    first = swap(lax.dynamic_slice_in_dim(other, core * half, half, 0))
    second = swap(first, "row", 1)
    whole = jnp.zeros((2 * rows,) + own.shape[1:], own.dtype)
    whole = lax.dynamic_update_slice_in_dim(whole, own, place * rows, 0)
    base = (1 - place) * rows
    whole = lax.dynamic_update_slice_in_dim(whole, first, base + core * half, 0)
    return lax.dynamic_update_slice_in_dim(whole, second, base + (1 - core) * half, 0)


def head_columns(qkv, decay, group, width):
    size = padded_width(width + 3 * (width // HD))
    heads = width // HD
    parts = []
    for j in range(3):
        piece = qkv[:, j * D + group * width : j * D + (group + 1) * width]
        filled = width
        parts.append(piece)
        if j == 0:
            parts.append(decay[:, group * heads : (group + 1) * heads])
            filled += heads
        if size > filled:
            parts.append(jnp.zeros((qkv.shape[0], size - filled), qkv.dtype))
    return jnp.concatenate(parts, axis=1)


def normalize(values):
    center = values - jnp.mean(values, axis=-1, keepdims=True)
    inverse = lax.rsqrt(jnp.mean(center * center, axis=-1, keepdims=True) + EPS)
    return center * inverse, inverse


def normalize_back(delta, normal, inverse):
    first = jnp.mean(delta, axis=-1, keepdims=True)
    second = jnp.mean(delta * normal, axis=-1, keepdims=True)
    return inverse * (delta - first - normal * second)


def embed_steps(steps):
    half = D // 2
    freqs = jnp.exp(-jnp.log(10000.0) * jnp.arange(half, dtype=FLOAT) / half)
    angles = steps.astype(FLOAT)[:, None] * freqs[None, :]
    return jnp.concatenate([jnp.cos(angles), jnp.sin(angles)], axis=1)


GELU_A = 0.7978845608028654
GELU_B = 0.044715


def gelu(z):
    return 0.5 * z * (1.0 + jnp.tanh(GELU_A * (z + GELU_B * z * z * z)))


def gelu_slope(z):
    t = jnp.tanh(GELU_A * (z + GELU_B * z * z * z))
    return 0.5 * (1.0 + t) + 0.5 * z * (1.0 - t * t) * GELU_A * (1.0 + 3.0 * GELU_B * z * z)


def matmul(left, right):
    return lax.dot_general(left, right, (((2,), (0,)), ((), ())), preferred_element_type=FLOAT)


def matmul_back(left, right):
    return lax.dot_general(left, right, (((2,), (1,)), ((), ())), preferred_element_type=FLOAT)


def weight_grad(left, right):
    return lax.dot_general(
        left, right, (((0, 1), (0, 1)), ((), ())), preferred_element_type=FLOAT
    )


def forward_layer(tokens, modulation, weights, layer, tile):
    taps, qkv, decay_bias, proj, expand, shrink = weights
    rows, cols = tile
    items, cells = tokens.shape[:2]
    width = proj.shape[0]
    heads = width // HD
    size = padded_width(width + 3 * heads)
    axis = "col" if layer % 2 == 0 else "row"
    mod = [modulation[:, k][:, None] for k in range(6)]
    normal, inverse = normalize(tokens)
    hidden = (normal * (1.0 + mod[1]) + mod[0]).astype(BFLOAT).reshape(items, rows, cols, D)
    sides = halo(hidden)
    convolved, mixed = conv_forward(hidden, sides, taps)
    mixed = gather_items(mixed.reshape(items, cells, D))
    project = matmul(mixed, qkv)
    logit = project[:, :, width : width + heads] + decay_bias.astype(FLOAT)
    high = logit.astype(BFLOAT)
    rest = logit - high.astype(FLOAT)
    middle_part = rest.astype(BFLOAT)
    low = (rest - middle_part.astype(FLOAT)).astype(BFLOAT)
    project = project.astype(BFLOAT)
    project = jnp.concatenate(
        [project[:, :, :width], high, middle_part, low, project[:, :, width + 3 * heads :]], axis=2
    )
    parts = lines_out(project, axis)
    place = lax.axis_index(axis)
    attends = scan_call(
        scan_forward_kernel, place, parts, width, rows, cols, layer % 2 == 0, width
    )
    attend = lines_back(attends, axis)
    branch = reduce_items(matmul(attend, proj))
    middle = tokens + mod[2] * branch
    normal2, inverse2 = normalize(middle)
    second = gather_items((normal2 * (1.0 + mod[4]) + mod[3]).astype(BFLOAT))
    inner = matmul(second, expand)
    active = gelu(inner).astype(BFLOAT)
    outer = reduce_items(matmul(active, shrink))
    result = middle + mod[5] * outer
    saved = (
        normal, inverse, hidden, sides, convolved, mixed, parts, attend, branch,
        normal2, inverse2, second, inner, active, outer,
    )
    return result, saved


def backward_layer(delta, saved, modulation, weights, layer, tile):
    taps, qkv, decay_bias, proj, expand, shrink = weights
    (
        normal, inverse, hidden, sides, convolved, mixed, parts, attend, branch,
        normal2, inverse2, second, inner, active, outer,
    ) = saved
    rows, cols = tile
    items, cells = delta.shape[:2]
    width = proj.shape[0]
    heads = width // HD
    size = padded_width(width + 3 * heads)
    axis = "col" if layer % 2 == 0 else "row"
    mod = [modulation[:, k][:, None] for k in range(6)]
    over = lambda v: jnp.sum(v, axis=1)
    delta_gate2 = over(delta * outer)
    outer_low = gather_items((mod[5] * delta).astype(BFLOAT))
    grad_shrink = weight_grad(active, outer_low)
    inner_low = (matmul_back(outer_low, shrink) * gelu_slope(inner)).astype(BFLOAT)
    grad_expand = weight_grad(second, inner_low)
    delta_second = reduce_items(matmul_back(inner_low, expand))
    delta_shift2 = over(delta_second)
    delta_scale2 = over(delta_second * normal2)
    delta_middle = delta + normalize_back(delta_second * (1.0 + mod[4]), normal2, inverse2)
    delta_gate1 = over(delta_middle * branch)
    branch_low = gather_items((mod[2] * delta_middle).astype(BFLOAT))
    grad_proj = weight_grad(attend, branch_low)
    delta_attend = matmul_back(branch_low, proj).astype(BFLOAT)
    delta_parts = lines_out(delta_attend, axis)
    place = lax.axis_index(axis)
    projects = scan_call(
        scan_backward_kernel, place, list(parts) + delta_parts, 3 * size, rows, cols,
        layer % 2 == 0, width,
    )
    delta_project = lines_back(projects, axis)
    grad_qkv = weight_grad(mixed, delta_project)
    grad_decay_bias = jnp.sum(delta_project[:, :, width : width + heads].astype(FLOAT), axis=(0, 1))
    delta_mixed = reduce_items(matmul_back(delta_project, qkv)).reshape(convolved.shape)
    gate = jax.nn.sigmoid(convolved)
    delta_conv = (delta_mixed * gate * (1.0 + convolved * (1.0 - gate))).astype(BFLOAT)
    delta_sides = halo(delta_conv)
    delta_hidden, grad_taps = conv_backward(hidden, sides, delta_conv, delta_sides, taps)
    delta_hidden = delta_hidden.reshape(items, cells, D)
    delta_shift1 = over(delta_hidden)
    delta_scale1 = over(delta_hidden * normal)
    delta_tokens = delta_middle + normalize_back(delta_hidden * (1.0 + mod[1]), normal, inverse)
    delta_mod = jnp.stack(
        [delta_shift1, delta_scale1, delta_gate1, delta_shift2, delta_scale2, delta_gate2], axis=1
    )
    return delta_tokens, (grad_shrink, grad_expand, grad_proj, grad_qkv), (
        delta_mod, grad_taps, grad_decay_bias,
    )


def sum_rows_here(grad):
    return lax.psum(grad.astype(BFLOAT), GRID_AXES).astype(FLOAT)


def sum_columns(grad):
    count = lax.axis_size("batch")
    low = grad.astype(BFLOAT).reshape((count, -1, grad.shape[1]))
    shares = lax.axis_size("row") * lax.axis_size("col")
    if count == 2 and low.shape[1] % shares == 0:
        share = lax.psum_scatter(low, GRID_AXES, scatter_dimension=1, tiled=True)
        place = lax.axis_index("batch")
        own = lax.dynamic_index_in_dim(share, place, 0, keepdims=False)
        other = swap(lax.dynamic_index_in_dim(share, 1 - place, 0, keepdims=False))
        both = jnp.stack([jnp.where(place == 0, own, other), jnp.where(place == 0, other, own)])
        return lax.all_gather(both, GRID_AXES, axis=1, tiled=True)
    total = lax.psum(low, GRID_AXES)
    return lax.all_to_all(total, "batch", 0, 0)


def per_device(
    tokens_in, timesteps, ada_weight, ada_bias, conv_taps, qkv_weight, decay_weight, decay_bias,
    proj_weight, expand_weight, shrink_weight, cotangent,
):
    count, place = lax.axis_size("batch"), lax.axis_index("batch")
    items, rows, cols = tokens_in.shape[:3]
    tile = (rows, cols)
    rows_here = ada_weight.shape[1]
    width = proj_weight.shape[1]
    heads = width // HD
    size = padded_width(width + 3 * heads)
    cond = jax.nn.silu(embed_steps(timesteps)).astype(BFLOAT)
    cond_slice = lax.dynamic_slice_in_dim(cond, place * rows_here, rows_here, 1)
    order = [0] if count != 2 else None
    if count == 2:
        cond_first = jnp.where(
            place == 0, cond_slice, jnp.concatenate([cond_slice[items:], cond_slice[:items]])
        )
    else:
        cond_first = cond_slice
    biases = lax.all_gather(ada_bias, "batch", axis=1, tiled=True).astype(FLOAT)
    taps_all = lax.all_gather(conv_taps, "batch", axis=2, tiled=True)
    weights, modulations = [], []
    partial = jnp.stack(
        [
            jnp.dot(cond_first, ada_weight[layer], preferred_element_type=FLOAT)
            for layer in range(LAYERS)
        ],
        axis=1,
    )
    if count == 2:
        total = partial[:items] + swap(partial[items:])
    else:
        total = lax.psum_scatter(partial, "batch", scatter_dimension=0, tiled=True)
    for layer in range(LAYERS):
        modulations.append((total[:, layer] + biases[layer]).reshape(items, 6, D))
    for layer in range(LAYERS):
        qkv = fetch_columns(
            [head_columns(qkv_weight[layer], decay_weight[layer], g, width) for g in range(count)]
        )
        inner = expand_weight.shape[2] // count
        expand = fetch_columns(
            [expand_weight[layer][:, g * inner : (g + 1) * inner] for g in range(count)]
        )
        weights.append(
            (taps_all[layer], qkv, decay_bias[layer], proj_weight[layer], expand, shrink_weight[layer])
        )
    tokens = tokens_in.astype(FLOAT).reshape(items, rows * cols, D)
    stored = []
    for layer in range(LAYERS):
        tokens, saved = forward_layer(tokens, modulations[layer], weights[layer], layer, tile)
        stored.append(saved)
    block_out = tokens.astype(BFLOAT).reshape(tokens_in.shape)
    delta = cotangent.astype(FLOAT).reshape(tokens.shape)
    bigs, smalls = [None] * LAYERS, [None] * LAYERS
    for layer in reversed(range(LAYERS)):
        delta, big, small = backward_layer(
            delta, stored[layer], modulations[layer], weights[layer], layer, tile
        )
        grad_shrink, grad_expand, grad_proj, grad_qkv = big
        bigs[layer] = (
            sum_rows_here(grad_shrink),
            sum_columns(grad_expand),
            sum_rows_here(grad_proj),
            sum_columns(grad_qkv),
        )
        smalls[layer] = small
    grad_tokens = delta.astype(BFLOAT).reshape(tokens_in.shape)
    delta_mods, taps_grads, bias_grads = lax.psum(
        tuple(jnp.stack([smalls[layer][k] for layer in range(LAYERS)]) for k in range(3)), GRID_AXES
    )
    every_mod = gather_items(delta_mods.transpose(1, 0, 2, 3)).reshape(count * items, LAYERS, 6 * D)
    if count == 2:
        taps_every = taps_grads + swap(taps_grads)
    else:
        taps_every = lax.psum(taps_grads, "batch")
    grad_taps = lax.dynamic_slice_in_dim(taps_every, place * width, width, 2)
    grad_ada = jnp.zeros((LAYERS, rows_here, 6 * D), FLOAT)
    for item in range(count * items):
        grad_ada += (
            cond_first[item].astype(FLOAT)[None, :, None] * every_mod[item][:, None, :]
        )
    bias_width = ada_bias.shape[1]
    grad_ada_bias = lax.dynamic_slice_in_dim(
        jnp.sum(every_mod, axis=0), place * bias_width, bias_width, 1
    )
    stack = lambda k: jnp.stack([bigs[layer][k] for layer in range(LAYERS)])
    grad_shrink, grad_proj = stack(0), stack(2)
    expand_parts, qkv_parts = stack(1), stack(3)
    grad_expand = jnp.concatenate([expand_parts[:, g] for g in range(count)], 2).astype(FLOAT)
    grad_qkv = jnp.concatenate(
        [
            qkv_parts[:, g, :, j * size : j * size + width]
            for j in range(3)
            for g in range(count)
        ],
        axis=2,
    ).astype(FLOAT)
    grad_decay = jnp.concatenate(
        [qkv_parts[:, g, :, width : width + heads] for g in range(count)], axis=2
    ).astype(FLOAT)
    return (
        block_out,
        grad_tokens,
        grad_ada,
        grad_ada_bias,
        grad_taps,
        grad_qkv,
        grad_decay,
        bias_grads,
        grad_proj,
        grad_expand,
        grad_shrink,
    )


def solution(mesh):
    return jax.shard_map(
        per_device,
        mesh=mesh,
        in_specs=(
            P("batch", "row", "col", None),
            P(),
            P(None, "batch", None),
            P(None, "batch"),
            P(None, None, "batch"),
            P(None, "batch", None),
            P(None, "batch", None),
            P(None, "batch"),
            P(None, "batch", None),
            P(None, "batch", None),
            P(None, "batch", None),
            P("batch", "row", "col", None),
        ),
        out_specs=(
            P("batch", "row", "col", None),
            P("batch", "row", "col", None),
            P(None, "batch", None),
            P(None, "batch"),
            P(None, None, "batch"),
            P(None, "batch", None),
            P(None, "batch", None),
            P(None, "batch"),
            P(None, "batch", None),
            P(None, "batch", None),
            P(None, "batch", None),
        ),
        check_vma=False,
    )
```

time: 4840 us -> 1480 us (0.31)
  waiting for transfers between devices: 3170 us -> 867 us
  local copies, waits for them, and re-layouts: 651 us -> 192 us
  matrix products: 407 us -> 78.6 us
  other arithmetic: 294 us -> 93.8 us
  blocking collectives: 206 us -> 87.8 us
    psum x3 -> x1, waiting for transfers between devices: 1680 us -> 25.6 us  [per_device(): lax.psum(tuple((jnp.stack([smalls[layer][k] for layer in range(LAYERS)])...]
    all_gather x16 -> x4, waiting for transfers between devices: 1480 us -> 140 us  [sum_columns(): return lax.all_gather(both, GRID_AXES, axis=1, tiled=True)]
    unnamed x19 -> x7, waiting for transfers between devices: 2.84 us -> 530 us
    dot_general x58 -> x26, matrix products: 407 us -> 78.6 us  [the longest x8 25.8 us: weight_grad(): lax.dot_general(left, right, (((0, 1), (0, 1)), ((), ())), preferred_elem...]
    unnamed x491 -> x390, local copies, waits for them, and re-layouts: 298 us -> 23.4 us
    ppermute x16 -> x71, waiting for transfers between devices: 4.62 us -> 171 us  [the longest x55 153 us: swap(): return lax.ppermute(value, axis, [(i, i ^ bit) for i in range(count)])]
    select_n x16 -> x5, other arithmetic: 173 us -> 7.9 us  [the longest x4 7.89 us: pick(): chosen = jnp.where(index == k, values[k], chosen)]
    all_gather x18 -> x2, blocking collectives: 200 us -> 56.1 us  [the longest x1 47.5 us: per_device(): biases = lax.all_gather(ada_bias, 'batch', axis=1, tiled=True).astype(FLOAT)]
  transfers between devices with their start and end apart: 45 -> 77, of which waited for: 16 -> 46; matrix products, arithmetic and copies ran while one was open for 22% -> 19% of each run, Pallas kernels for 0% -> 1%
where the time goes in v1:
time: 1480 us; the launch traced here: 1470 us
  waiting for transfers between devices  867 us (59%)
  local copies, waits for them, and re-layouts  192 us (13%)
  starting transfers between devices  105 us (7%)
  other arithmetic  93.8 us (6%)
  blocking collectives  87.8 us (6%)
  matrix products  78.6 us (5%)
  Pallas kernels  24.9 us (2%)
  between operations  18.2 us (1%)
    unnamed x7, waiting for transfers between devices  530 us
    ppermute x55, waiting for transfers between devices, swap(): return lax.ppermute(value, axis, [(i, i ^ bit) for i in range(count)])  153 us
    all_gather x4, waiting for transfers between devices, sum_columns(): return lax.all_gather(both, GRID_AXES, axis=1, tiled=True)  140 us
    ppermute x55, starting transfers between devices, swap(): return lax.ppermute(value, axis, [(i, i ^ bit) for i in range(count)])  59.2 us
    reshape x4, local copies, waits for them, and re-layouts, sum_columns(): low = grad.astype(BFLOAT).reshape((count, -1, grad.shape[1]))  49.7 us
    all_gather x1, blocking collectives, per_device(): biases = lax.all_gather(ada_bias, 'batch', axis=1, tiled=True).astype(FLOAT)  47.5 us
    psum x1, blocking collectives, per_device(): lax.psum(tuple((jnp.stack([smalls[layer][k] for layer in range(LAYERS)])...  31.7 us
  transfers between devices with their start and end apart: 77, of which 46 were waited for; matrix products, arithmetic and copies ran while one was open for 19% of the time, Pallas kernels for 1%

profile of v1, /device:TPU:0, one launch (start us, length us, event | category | flops | bytes accessed | tf_op | source)
XLA Modules:
  0.0 1468.0 jit_solution(11817446791962162314)
XLA Ops:
  60.1 8.9 slice_bitcast_fusion
  76.9 47.5 %all_gather.18 = bf16[2,6912]{1,0:T(2,128)(2,1)S(1)} all-gather(bf16[2,3456]{1,0:T(2,128)(2,1)S(1)} %copy-done.139), channel_id=1, replica_groups=mesh['batch'=2,'row'=4,'col'=4] {'batch'}, dimensions={1}, use_global_device_ids=true | all-gather | bytes 41472 | tf_op jit(solution)/shard_map/all_gather | solution.py:551
  125.3 8.6 all_gather.19
  191.8 11.6 collective-permute-done.9.refs_3_
  221.6 26.0 %collective-permute-done.14 = bf16[2,64,1152]{2,1,0:T(8,128)(2,1)S(1)} collective-permute-done((bf16[2,64,1152]{2,1,0:T(8,128)(2,1)S(1)}, bf16[2,64,1152]{2,1,0:T(8,128)(2,1)S(1)}, u32[]{:S(2)}, u32[]{:S(2)}) %collective-permute-start.14) | collective-permute-done | bytes 294944 | tf_op jit(solution)/shard_map/ppermute | solution.py:31
  275.1 12.9 collective-permute-start.21
  328.4 7.7 collective-permute-done.27.refs_3_
  433.4 8.8 collective-permute-done.46
  481.5 15.8 %copy.346 = bf16[2,576,2304]{2,0,1:T(2,128)(2,1)} copy(bf16[2,576,2304]{2,1,0:T(8,128)(2,1)S(1)} %bitcast.469) | data formatting | bytes 10616832 | tf_op jit(solution)/shard_map/reshape | solution.py:518
  505.3 8.9 copy.333
  539.2 16.0 %copy.341 = bf16[2,576,2304]{2,0,1:T(2,128)(2,1)} copy(bf16[2,576,2304]{2,1,0:T(8,128)(2,1)S(1)} %bitcast.470) | data formatting | bytes 10616832 | tf_op jit(solution)/shard_map/reshape | solution.py:518
  562.5 9.0 copy.327
  602.8 529.6 %all-reduce.11.cloned.1.call-done = (bf16[2,576,1920]{2,0,1:T(2,128)(2,1)}, bf16[2,576,1920]{2,0,1:T(2,128)(2,1)}, bf16[1,576,1152]{2,1,0:T(8,128)(2,1)}, bf16[1...) async-done(((bf16[2,576,1920]{2,0,1:T(2,128)(2,1)}, ...) | async-done | bytes 32735248
  1169.0 31.7 %psum.51 = f32[2,8]{1,0:T(2,128)} all-reduce(f32[2,8]{1,0:T(2,128)S(1)} %pad_maximum_fusion.56), channel_id=1, replica_groups=mesh['batch'=2,'row'=4,'col'=4] {'row','col'}, use_global_device_ids=true, to_apply=%region_36.37 | all-reduce | flops 16 | bytes 128 | tf_op jit(solution)/shard_map/psum | solution.py:599
  1202.0 25.6 %all-reduce.9.cloned.1.call-done = (f32[2,2,6,1152]{3,2,1,0:T(8,128)}, f32[2,9,1152]{2,1,0:T(8,128)}) async-done(((f32[2,2,6,1152]{3,2,1,0:T(8,128)}, f32[2,9,1152]{2,1,0:T(8,128)}), (f32[2,2,6,1152]{3,2,1,0:T(8,128)}, f32[2,9,1152]{2,1,0:T(8,128)})) %all-reduce.9.cloned.1.call-update) | async-done | bytes 193552 | tf_op jit(solution)/shard_map/psum | solution.py:599
  1237.2 13.7 multiply_add_fusion
  1253.6 7.6 maximum_convert_fusion.1
  1261.2 20.0 %all-gather.5.cloned.1.call-done = bf16[2,576,1920]{2,0,1:T(2,128)(2,1)} async-done(((bf16[2,36,1920]{2,0,1:T(2,128)(2,1)}), bf16[2,576,1920]{2,0,1:T(2,128)(2,1)}) %all-gather.5.cloned.1.call-update) | async-done | bytes 4423696 | tf_op jit(solution)/shard_map/all_gather | solution.py:526
  1286.0 48.2 %all-gather.7.cloned.1.call-done = bf16[2,576,1920]{2,0,1:T(2,128)(2,1)} async-done(((bf16[2,36,1920]{2,0,1:T(2,128)(2,1)}), bf16[2,576,1920]{2,0,1:T(2,128)(2,1)}) %all-gather.7.cloned.1.call-update) | async-done | bytes 4423696 | tf_op jit(solution)/shard_map/all_gather | solution.py:526
  1345.7 14.0 concatenate.122
  1359.7 10.2 convert_element_type.295
  1370.6 20.5 %all-gather.9.cloned.1.call-done = bf16[2,576,2304]{2,0,1:T(2,128)(2,1)} async-done(((bf16[2,36,2304]{2,0,1:T(2,128)(2,1)}), bf16[2,576,2304]{2,0,1:T(2,128)(2,1)}) %all-gather.9.cloned.1.call-update) | async-done | bytes 5308432 | tf_op jit(solution)/shard_map/all_gather | solution.py:526
  1396.6 51.5 %all-gather.11.cloned.1.call-done = bf16[2,576,2304]{2,0,1:T(2,128)(2,1)} async-done(((bf16[2,36,2304]{2,0,1:T(2,128)(2,1)}), bf16[2,576,2304]{2,0,1:T(2,128)(2,1)}) %all-gather.11.cloned.1.call-update) | async-done | bytes 5308432 | tf_op jit(solution)/shard_map/all_gather | solution.py:526
  1453.1 7.8 maximum_convert_fusion
  (802 shorter events, 487.7 us)
Async XLA Ops:
  7.2 1125.3 %all-reduce.11.cloned.1.call-start = ((), (), s32[]{:S(2)}) async-start(), calls=%async_computation.5 | async-start | bytes 65470464
  17.8 127.2 %collective-permute-start = (f32[2,2,6912]{2,0,1:T(2,128)}, f32[2,2,6912]{2,0,1:T(2,128)}, u32[]{:S(2)}, u32[]{:S(2)}) collective-permute-start(f32[2,2,6912]{2,0,1:T(2,128)} %pad_maximum_fusion.43), channel_id=1, source_target_pairs={{0,16},{16,0},{1,17},{17,1},{2,18},{18,2},{3,19},{19,3},{4,20},{20... | collective-permute-start | bytes 331784 | tf_op jit(solution)/shard_map/ppermute | solution.py:31
  45.9 216.2 %collective-permute-start.24 = (bf16[288,1920]{1,0:T(8,128)(2,1)}, bf16[288,1920]{1,0:T(8,128)(2,1)}, u32[]{:S(2)}, u32[]{:S(2)}) collective-permute-start(bf16[288,1920]{1,0:T(8,128)(2,1)} %dynamic-slice_select_fusion.2), channel_id=1, source_target_pairs={{0,16},{16,0},{1,17},{17,1},{2,18},{18,2},{3,19},{19,3},{4,20},{20... | collective-permute-start | bytes 3317768 | tf_op jit(solution)/shard_map/ppermute | solution.py:31
  58.1 94.4 %collective-permute-start.6 = (bf16[288,1920]{1,0:T(8,128)(2,1)}, bf16[288,1920]{1,0:T(8,128)(2,1)}, u32[]{:S(2)}, u32[]{:S(2)}) collective-permute-start(bf16[288,1920]{1,0:T(8,128)(2,1)} %dynamic-slice_select_fusion.3), channel_id=1, source_target_pairs={{0,16},{16,0},{1,17},{17,1},{2,18},{18,2},{3,19},{19,3},{4,20},{20... | collective-permute-start | bytes 3317768 | tf_op jit(solution)/shard_map/ppermute | solution.py:31
  75.5 136.2 %collective-permute-start.16 = (bf16[288,2304]{1,0:T(8,128)(2,1)}, bf16[288,2304]{1,0:T(8,128)(2,1)}, u32[]{:S(2)}, u32[]{:S(2)}) collective-permute-start(bf16[288,2304]{1,0:T(8,128)(2,1)} %dynamic-slice_select_fusion.1), channel_id=1, source_target_pairs={{0,16},{16,0},{1,17},{17,1},{2,18},{18,2},{3,19},{19,3},{4,20},{20... | collective-permute-start | bytes 3981320 | tf_op jit(solution)/shard_map/ppermute | solution.py:31
  152.5 15.0 %collective-permute-start.7 = (bf16[288,1920]{1,0:T(8,128)(2,1)}, bf16[288,1920]{1,0:T(8,128)(2,1)S(1)}, u32[]{:S(2)}, u32[]{:S(2)}) collective-permute-start(bf16[288,1920]{1,0:T(8,128)(2,1)} %collective-permute-done.6), channel_id=1, source_target_pairs={{0,4},{4,0},{8,12},{12,8},{1,5},{5,1},{9,13},{13,9},{2,6},{6,2},{1... | collective-permute-start | bytes 3317768 | tf_op jit(solution)/shard_map/ppermute | solution.py:31
  183.0 20.4 %collective-permute-start.9 = (bf16[1,64,1920]{2,1,0:T(8,128)(2,1)S(1)}, bf16[1,64,1920]{2,1,0:T(8,128)(2,1)S(1)}, u32[]{:S(2)}, u32[]{:S(2)}) collective-permute-start(bf16[1,64,1920]{2,1,0:T(8,128)(2,1)S(1)} %get-tuple-element.229), channel_id=1, source_target_pairs={{0,2},{1,3},{2,0},{3,1},{4,6},{5,7},{6,4},{7,5},{8,10},{9,11},{10,... | collective-permute-start | bytes 737288 | tf_op jit(solution)/shard_map/ppermute | solution.py:31
  184.1 19.3 %collective-permute-start.8 = (bf16[1,64,1920]{2,1,0:T(8,128)(2,1)S(1)}, bf16[1,64,1920]{2,1,0:T(8,128)(2,1)S(1)}, u32[]{:S(2)}, u32[]{:S(2)}) collective-permute-start(bf16[1,64,1920]{2,1,0:T(8,128)(2,1)S(1)} %get-tuple-element.230), channel_id=1, source_target_pairs={{0,1},{1,0},{2,3},{3,2},{4,5},{5,4},{6,7},{7,6},{8,9},{9,8},{10,11... | collective-permute-start | bytes 737288 | tf_op jit(solution)/shard_map/ppermute | solution.py:31
  211.8 130.1 %collective-permute-start.34 = (bf16[288,2304]{1,0:T(8,128)(2,1)}, bf16[288,2304]{1,0:T(8,128)(2,1)}, u32[]{:S(2)}, u32[]{:S(2)}) collective-permute-start(bf16[288,2304]{1,0:T(8,128)(2,1)} %dynamic-slice_select_fusion), channel_id=1, source_target_pairs={{0,16},{16,0},{1,17},{17,1},{2,18},{18,2},{3,19},{19,3},{4,20},{20... | collective-permute-start | bytes 3981320 | tf_op jit(solution)/shard_map/ppermute | solution.py:31
  212.4 36.6 %collective-permute-start.17 = (bf16[288,2304]{1,0:T(8,128)(2,1)}, bf16[288,2304]{1,0:T(8,128)(2,1)S(1)}, u32[]{:S(2)}, u32[]{:S(2)}) collective-permute-start(bf16[288,2304]{1,0:T(8,128)(2,1)} %collective-permute-done.16), channel_id=1, source_target_pairs={{0,4},{4,0},{8,12},{12,8},{1,5},{5,1},{9,13},{13,9},{2,6},{6,2},{1... | collective-permute-start | bytes 3981320 | tf_op jit(solution)/shard_map/ppermute | solution.py:31
  218.2 29.5 %collective-permute-start.14 = (bf16[2,64,1152]{2,1,0:T(8,128)(2,1)S(1)}, bf16[2,64,1152]{2,1,0:T(8,128)(2,1)S(1)}, u32[]{:S(2)}, u32[]{:S(2)}) collective-permute-start(bf16[2,64,1152]{2,1,0:T(8,128)(2,1)S(1)} %slice.921), channel_id=1, source_target_pairs={{0,16},{16,0},{1,17},{17,1},{2,18},{18,2},{3,19},{19,3},{4,20},{20... | collective-permute-start | bytes 884744 | tf_op jit(solution)/shard_map/ppermute | solution.py:31
  262.1 41.7 %collective-permute-start.25 = (bf16[288,1920]{1,0:T(8,128)(2,1)}, bf16[288,1920]{1,0:T(8,128)(2,1)}, u32[]{:S(2)}, u32[]{:S(2)}) collective-permute-start(bf16[288,1920]{1,0:T(8,128)(2,1)} %collective-permute-done.24), channel_id=1, source_target_pairs={{0,4},{4,0},{8,12},{12,8},{1,5},{5,1},{9,13},{13,9},{2,6},{6,2},{1... | collective-permute-start | bytes 3317768 | tf_op jit(solution)/shard_map/ppermute | solution.py:31
  275.1 20.4 %collective-permute-start.21 = (bf16[2,10,1152]{2,1,0:T(8,128)(2,1)S(1)}, bf16[2,10,1152]{2,1,0:T(8,128)(2,1)S(1)}, u32[]{:S(2)}, u32[]{:S(2)}) collective-permute-start(bf16[2,10,1152]{2,1,0:T(8,128)(2,1)S(1)} %pad_maximum_fusion.46), channel_id=1, source_target_pairs={{0,1},{1,2},{2,3},{4,5},{5,6},{6,7},{8,9},{9,10},{10,11},{12,13},{... | collective-permute-start | bytes 138248 | tf_op jit(solution)/shard_map/ppermute | solution.py:73
  327.8 43.2 %collective-permute-start.37 = (bf16[2,64,1152]{2,1,0:T(8,128)(2,1)S(1)}, bf16[2,64,1152]{2,1,0:T(8,128)(2,1)S(1)}, u32[]{:S(2)}, u32[]{:S(2)}) collective-permute-start(bf16[2,64,1152]{2,1,0:T(8,128)(2,1)S(1)} %fusion.105), channel_id=1, source_target_pairs={{0,16},{16,0},{1,17},{17,1},{2,18},{18,2},{3,19},{19,3},{4,20},{20... | collective-permute-start | bytes 884744 | tf_op jit(solution)/shard_map/ppermute | solution.py:31
  341.9 16.3 %collective-permute-start.35 = (bf16[288,2304]{1,0:T(8,128)(2,1)}, bf16[288,2304]{1,0:T(8,128)(2,1)S(1)}, u32[]{:S(2)}, u32[]{:S(2)}) collective-permute-start(bf16[288,2304]{1,0:T(8,128)(2,1)} %collective-permute-done.34), channel_id=1, source_target_pairs={{0,4},{4,0},{8,12},{12,8},{1,5},{5,1},{9,13},{13,9},{2,6},{6,2},{1... | collective-permute-start | bytes 3981320 | tf_op jit(solution)/shard_map/ppermute | solution.py:31
  479.2 20.0 %collective-permute-start.52 = (bf16[2,64,1152]{2,1,0:T(8,128)(2,1)S(1)}, bf16[2,64,1152]{2,1,0:T(8,128)(2,1)S(1)}, u32[]{:S(2)}, u32[]{:S(2)}) collective-permute-start(bf16[2,64,1152]{2,1,0:T(8,128)(2,1)S(1)} %slice.915), channel_id=1, source_target_pairs={{0,16},{16,0},{1,17},{17,1},{2,18},{18,2},{3,19},{19,3},{4,20},{20... | collective-permute-start | bytes 884744 | tf_op jit(solution)/shard_map/ppermute | solution.py:31
  533.1 24.9 %collective-permute-start.57 = (bf16[1,64,1920]{2,1,0:T(8,128)(2,1)S(1)}, bf16[1,64,1920]{2,1,0:T(8,128)(2,1)S(1)}, u32[]{:S(2)}, u32[]{:S(2)}) collective-permute-start(bf16[1,64,1920]{2,1,0:T(8,128)(2,1)S(1)} %get-tuple-element.52), channel_id=1, source_target_pairs={{0,1},{1,0},{2,3},{3,2},{4,5},{5,4},{6,7},{7,6},{8,9},{9,8},{10,11... | collective-permute-start | bytes 737288 | tf_op jit(solution)/shard_map/ppermute | solution.py:31
  533.4 24.6 %collective-permute-start.58 = (bf16[1,64,1920]{2,1,0:T(8,128)(2,1)S(1)}, bf16[1,64,1920]{2,1,0:T(8,128)(2,1)S(1)}, u32[]{:S(2)}, u32[]{:S(2)}) collective-permute-start(bf16[1,64,1920]{2,1,0:T(8,128)(2,1)S(1)} %get-tuple-element.53), channel_id=1, source_target_pairs={{0,2},{1,3},{2,0},{3,1},{4,6},{5,7},{6,4},{7,5},{8,10},{9,11},{10,... | collective-permute-start | bytes 737288 | tf_op jit(solution)/shard_map/ppermute | solution.py:31
  536.3 21.7 %collective-permute-start.59 = (bf16[1,64,1920]{2,1,0:T(8,128)(2,1)S(1)}, bf16[1,64,1920]{2,1,0:T(8,128)(2,1)S(1)}, u32[]{:S(2)}, u32[]{:S(2)}) collective-permute-start(bf16[1,64,1920]{2,1,0:T(8,128)(2,1)S(1)} %get-tuple-element.54), channel_id=1, source_target_pairs={{0,3},{1,2},{2,1},{3,0},{4,7},{5,6},{6,5},{7,4},{8,11},{9,10},{10,... | collective-permute-start | bytes 737288 | tf_op jit(solution)/shard_map/ppermute | solution.py:31
  571.4 656.1 %all-reduce.9.cloned.1.call-start = ((), (), s32[]{:S(2)}) async-start(), calls=%async_computation.4 | async-start | bytes 589824 | tf_op jit(solution)/shard_map/psum | solution.py:599
  1136.4 144.8 %all-gather.5.cloned.1.call-start = ((), (), s32[]{:S(2)}) async-start(), calls=%async_computation | async-start | bytes 4700160 | tf_op jit(solution)/shard_map/all_gather | solution.py:526
  1141.6 192.6 %all-gather.7.cloned.1.call-start = ((), (), s32[]{:S(2)}) async-start(), calls=%async_computation.1 | async-start | bytes 4700160 | tf_op jit(solution)/shard_map/all_gather | solution.py:526
  1150.4 240.7 %all-gather.9.cloned.1.call-start = ((), (), s32[]{:S(2)}) async-start(), calls=%async_computation.2 | async-start | bytes 5640192 | tf_op jit(solution)/shard_map/all_gather | solution.py:526
  1159.1 289.0 %all-gather.11.cloned.1.call-start = ((), (), s32[]{:S(2)}) async-start(), calls=%async_computation.3 | async-start | bytes 5640192 | tf_op jit(solution)/shard_map/all_gather | solution.py:526
  (235 other events, 2507.7 us)
Sparse Core Ops, SparseCore 0:
  571.6 560.8 all-reduce.10
  1137.0 90.5 all-reduce.8
  1230.4 50.6 all-gather.4
  1283.8 50.3 all-gather.6
  1336.2 54.8 all-gather.8
  1393.1 54.9 all-gather.10

commit v2 on v1

--- a/solution.py
+++ b/solution.py
@@ -16,6 +16,7 @@
 LANES = 128
 VMEM_LIMIT = 48 * 1024 * 1024
 GRID_AXES = ("row", "col")
+SMALL = pl.CostEstimate(flops=1, bytes_accessed=1, transcendentals=0)
 
 
 def params():
@@ -35,6 +36,14 @@
     if lax.axis_size("batch") == 2:
         return jnp.concatenate([own, swap(own)], axis=0)
     return lax.all_gather(own, "batch", axis=0, tiled=True)
+
+
+def gather_last(own):
+    if lax.axis_size("batch") == 2:
+        other = swap(own)
+        first = lax.axis_index("batch") == 0
+        return jnp.concatenate([jnp.where(first, own, other), jnp.where(first, other, own)], -1)
+    return lax.all_gather(own, "batch", axis=own.ndim - 1, tiled=True)
 
 
 def reduce_items(partial):
@@ -64,21 +73,13 @@
 
 
 def halo(cells):
-    rows, cols = lax.axis_size("row"), lax.axis_size("col")
-    down = [(i, i + 1) for i in range(rows - 1)]
-    up = [(i + 1, i) for i in range(rows - 1)]
-    top = lax.ppermute(cells[:, -1], "row", down)
-    bottom = lax.ppermute(cells[:, 0], "row", up)
-    edge = lambda at: jnp.concatenate([top[:, at][:, None], cells[:, :, at], bottom[:, at][:, None]], 1)
-    left = lax.ppermute(edge(-1), "col", [(i, i + 1) for i in range(cols - 1)])
-    right = lax.ppermute(edge(0), "col", [(i + 1, i) for i in range(cols - 1)])
-    return top, bottom, left, right
-
-
-def beside(cells, top, bottom, left, right, item):
-    count = cells.shape[1]
+    return halo_edges([cells[:, 0], cells[:, -1], cells[:, :, 0], cells[:, :, -1]])
+
+
+def beside(cells, sides, item):
+    top, bottom, left, right = sides
+    count, width = cells.shape[1], cells.shape[2]
     lefts, rights = left[item].astype(FLOAT), right[item].astype(FLOAT)
-    width = cells.shape[2]
     at = lax.broadcasted_iota(jnp.int32, (width, cells.shape[3]), 0)
     rows = []
     for row in range(count + 2):
@@ -95,10 +96,11 @@
     return rows
 
 
-def conv_forward_kernel(cells, top, bottom, left, right, taps, convolved, mixed):
+def conv_forward_kernel(cells, *refs):
+    sides, (taps, convolved, mixed) = refs[:4], refs[4:]
     weights = taps[...].astype(FLOAT)
     for item in range(cells.shape[0]):
-        rows = beside(cells, top, bottom, left, right, item)
+        rows = beside(cells, sides, item)
         for row in range(cells.shape[1]):
             total = jnp.zeros(rows[0][1].shape, FLOAT)
             for a in range(3):
@@ -108,19 +110,18 @@
             mixed[item, row] = (total * jax.nn.sigmoid(total)).astype(BFLOAT)
 
 
-def conv_backward_kernel(
-    cells, top, bottom, left, right, delta, dtop, dbottom, dleft, dright, taps, hidden, grads
-):
+def conv_backward_kernel(cells, *refs):
+    sides, delta, delta_sides, (taps, hidden, grads) = refs[:4], refs[4], refs[5:9], refs[9:]
     weights = taps[...].astype(FLOAT)
     sums = [jnp.zeros((cells.shape[2], cells.shape[3]), FLOAT) for _ in range(9)]
     for item in range(cells.shape[0]):
-        rows = beside(cells, top, bottom, left, right, item)
+        rows = beside(cells, sides, item)
         for row in range(cells.shape[1]):
             here = delta[item, row].astype(FLOAT)
             for a in range(3):
                 for b in range(3):
                     sums[3 * a + b] += rows[row + a][b] * here
-        rows = beside(delta, dtop, dbottom, dleft, dright, item)
+        rows = beside(delta, delta_sides, item)
         for row in range(cells.shape[1]):
             total = jnp.zeros(rows[0][1].shape, FLOAT)
             for a in range(3):
@@ -133,10 +134,9 @@
 
 def conv_specs(items, rows, cols, block):
     cells = pl.BlockSpec((items, rows, cols, block), lambda i: (0, 0, 0, i))
-    flat = pl.BlockSpec((items, cols, block), lambda i: (0, 0, i))
-    side = pl.BlockSpec((items, rows + 2, block), lambda i: (0, 0, i))
+    side = lambda size: pl.BlockSpec((items, size, block), lambda i: (0, 0, i))
     taps = pl.BlockSpec((9, block), lambda i: (0, i))
-    return [cells, flat, flat, side, side], taps
+    return [cells] + [side(size) for size in (cols, cols, rows + 2, rows + 2)], taps
 
 
 def conv_forward(cells, sides, taps):
@@ -152,6 +152,7 @@
             jax.ShapeDtypeStruct(cells.shape, FLOAT),
             jax.ShapeDtypeStruct(cells.shape, BFLOAT),
         ],
+        cost_estimate=SMALL,
         compiler_params=params(),
     )(cells, *sides, taps)
 
@@ -169,6 +170,7 @@
             jax.ShapeDtypeStruct(cells.shape, FLOAT),
             jax.ShapeDtypeStruct((9, width), FLOAT),
         ],
+        cost_estimate=SMALL,
         compiler_params=params(),
     )(cells, *sides, delta, *delta_sides, taps)
 
@@ -320,6 +322,7 @@
             out_specs=[spec(out_width)] * count,
         ),
         out_shape=[jax.ShapeDtypeStruct((items, cells, out_width), BFLOAT)] * count,
+        cost_estimate=SMALL,
         compiler_params=params(),
     )(place.reshape(1).astype(jnp.int32), *inputs)
 
@@ -409,6 +412,1213 @@
     return lax.dot_general(
         left, right, (((0, 1), (0, 1)), ((), ())), preferred_element_type=FLOAT
     )
+
+
+SHARES = 16
+SHARE_ROWS = 144
+STAGES = (("row", 1), ("row", 2), ("col", 1), ("col", 2))
+
+
+def share_place(stages):
+    number = jnp.int32(0)
+    for axis, bit in stages:
+        number = 2 * number + (lax.axis_index(axis) // bit) % 2
+    return number.reshape(1).astype(jnp.int32)
+
+
+def product(act, delta):
+    return lax.dot_general(act, delta, (((1,), (0,)), ((), ())), preferred_element_type=FLOAT)
+
+
+def grad_send_kernel(place, act, delta, out):
+    out[0] = product(act[0], delta[0]).astype(BFLOAT)
+
+
+def grad_keep_kernel(place, act, delta, received, send, keep):
+    value = (product(act[0], delta[0]) + received[0].astype(FLOAT)).astype(BFLOAT)
+    first = pl.program_id(0) < SHARES // 4
+
+    @pl.when(first)
+    def _():
+        send[0] = value
+
+    @pl.when(jnp.logical_not(first))
+    def _():
+        keep[0] = value
+
+
+class GradSum:
+    def __init__(self, act, delta, act_index, delta_index, stages):
+        self.act, self.delta, self.stages = act, delta, stages
+        self.act_index, self.delta_index = act_index, delta_index
+        self.place = share_place(stages)
+
+    def call(self, kernel, position, extra, extra_specs, out_specs, out_shapes, through):
+        tokens = self.act.shape[2]
+        act_spec = pl.BlockSpec(
+            (1, SHARE_ROWS, tokens), lambda i, m: self.act_index(position(i) ^ m[0])
+        )
+        delta_spec = pl.BlockSpec(
+            (1, tokens, D), lambda i, m: self.delta_index(position(i) ^ m[0])
+        )
+        inputs = 3 + len(extra)
+
+        def body(*refs):
+            kernel(*refs[:inputs], *refs[inputs + 1 : -1])
+
+        return pl.pallas_call(
+            body,
+            grid_spec=pltpu.PrefetchScalarGridSpec(
+                num_scalar_prefetch=1,
+                grid=(SHARES // 2,),
+                in_specs=[act_spec, delta_spec] + extra_specs + [ANYWHERE],
+                out_specs=out_specs + [ANYWHERE],
+            ),
+            out_shape=out_shapes + [jax.ShapeDtypeStruct(through.shape, through.dtype)],
+            input_output_aliases={inputs: len(out_shapes)},
+            cost_estimate=SMALL,
+            compiler_params=params(),
+        )(self.place, self.act, self.delta, *extra, through)
+
+    def start(self, through):
+        half = SHARES // 2
+        block = (1, SHARE_ROWS, D)
+        send, through = self.call(
+            grad_send_kernel,
+            lambda i: i + half,
+            [],
+            [],
+            [pl.BlockSpec(block, lambda i, m: (i, 0, 0))],
+            [jax.ShapeDtypeStruct((half, SHARE_ROWS, D), BFLOAT)],
+            through,
+        )
+        self.flight = self.move(send, 0)
+        return through
+
+    def move(self, value, stage):
+        axis, bit = self.stages[stage]
+        return swap(value, axis, bit)
+
+    def second(self, through):
+        quarter = SHARES // 4
+        block = (1, SHARE_ROWS, D)
+        position = lambda i: i ^ quarter
+        send, self.keep, through = self.call(
+            grad_keep_kernel,
+            position,
+            [self.flight],
+            [pl.BlockSpec(block, lambda i, m: (position(i), 0, 0))],
+            [
+                pl.BlockSpec(block, lambda i, m: (jnp.minimum(i, quarter - 1), 0, 0)),
+                pl.BlockSpec(block, lambda i, m: (jnp.maximum(i - quarter, 0), 0, 0)),
+            ],
+            [jax.ShapeDtypeStruct((quarter, SHARE_ROWS, D), BFLOAT)] * 2,
+            through,
+        )
+        self.flight = self.move(send, 1)
+        self.state = 0
+        return through
+
+    works = ("halve", "halve", "add", "join", "join", "pass")
+    own_state = 3
+    offload = False
+
+    def advanced(self, outs):
+        work = self.works[self.state]
+        self.state += 1
+        if work == "pass":
+            self.keep, self.flight = outs
+            self.pieces = [self.keep, self.flight]
+            self.pieces += [self.move(piece, 0) for piece in self.pieces]
+            return
+        self.keep = outs[0]
+        if not (self.offload and self.state == self.own_state):
+            self.flight = self.onward(self.state, outs[-1])
+
+    def onward(self, state, value):
+        return self.move(value, (None, 2, 3, 3, 2, 1)[state])
+
+    def done(self):
+        return self.state == len(self.works)
+
+
+class CrossGradSum(GradSum):
+    works = ("halve", "halve", "add", "take", "join", "join", "pass")
+    own_state = 4
+
+    def onward(self, state, value):
+        if state == 3:
+            return self.cross(value)
+        return self.move(value, (None, 2, 3, None, 3, 2, 1)[state])
+
+    def cross(self, value):
+        rows, cols = lax.axis_size("row"), lax.axis_size("col")
+        pairs = []
+        for x in range(2):
+            for r in range(rows):
+                for z in range(cols):
+                    stays = r % 2 == x
+                    to_x, to_r = (x, r) if stays else (1 - x, r ^ 1)
+                    pairs.append(((x * rows + r) * cols + z, (to_x * rows + to_r) * cols + z))
+        return lax.ppermute(value, ("batch", "row", "col"), pairs)
+
+
+class Gathered:
+    def __init__(self, sums):
+        self.sums = sums
+
+    def gather(self):
+        self.collect(jnp.concatenate([one.keep for one in self.sums]))
+
+    def collect(self, shares):
+        whole = lax.all_gather(shares, GRID_AXES)
+        for slot, one in enumerate(self.sums):
+            one.whole, one.slot = whole, slot
+
+    @staticmethod
+    def finish(sums, kinds, previous, layer, shapes, through):
+        block = (1, SHARE_ROWS, D)
+        scalar = lax.axis_index("batch").reshape(1).astype(jnp.int32)
+
+        def source(slot):
+            def index(i, m):
+                core, y, low, high = i // 8, i // 4 % 2, i // 2 % 2, i % 2
+                return ((y * 2 + core) * 4 + high * 2 + low, slot, 0, 0)
+
+            return pl.BlockSpec((None,) + block, index)
+
+        def expand(i, m):
+            own = jnp.where(i // 8 == m[0], m[0], 1 - m[0])
+            return (layer, i % 4, own * 2 + i // 4 % 2)
+
+        indices = (
+            lambda i, m: (layer, i, 0),
+            expand,
+            lambda i, m: (layer, i // 4, jnp.minimum(i % 4, 2)),
+            lambda i, m: (layer, i // 4, 0),
+        )
+        targets = [k for kind in kinds for k in ((0,), (1,), (2, 3))["ABC".index(kind)]]
+        earlier = [previous[k] for k in targets] if previous else []
+        count, outs, given = len(earlier), len(targets), len(sums)
+
+        def body(m, *refs):
+            where = dict(zip(targets, refs[-1 - outs : -1]))
+            last = pl.program_id(0) % 4 == 3
+            for kind, ref in zip(kinds, refs):
+                if kind != "C":
+                    where["AB".index(kind)][0] = ref[0].astype(FLOAT)
+                    continue
+
+                @pl.when(last)
+                def _(ref=ref):
+                    where[3][0] = ref[0].astype(FLOAT)
+
+                @pl.when(jnp.logical_not(last))
+                def _(ref=ref):
+                    where[2][0] = ref[0].astype(FLOAT)
+
+        *results, through = pl.pallas_call(
+            body,
+            grid_spec=pltpu.PrefetchScalarGridSpec(
+                num_scalar_prefetch=1,
+                grid=(SHARES,),
+                in_specs=[source(one.slot) for one in sums] + [ANYWHERE] * (count + 1),
+                out_specs=[pl.BlockSpec(block, indices[k]) for k in targets] + [ANYWHERE],
+            ),
+            out_shape=[jax.ShapeDtypeStruct(shapes[k], FLOAT) for k in targets]
+            + [jax.ShapeDtypeStruct(through.shape, through.dtype)],
+            input_output_aliases={1 + given + k: k for k in range(count)}
+            | {1 + given + count: outs},
+            cost_estimate=SMALL,
+            compiler_params=params(),
+        )(scalar, *[one.whole for one in sums], *earlier, through)
+        return dict(zip(targets, results)), through
+
+
+class Scattered(Gathered):
+    def __init__(self):
+        self.sums, self.group, self.shares = [], [], []
+
+    def add(self, one, through):
+        slot, tokens, dim = len(self.group), one.act.shape[2], len(self.shares) % 2
+        one.offload = True
+        earlier = [self.buffer] if slot else []
+        self.sums.append(one)
+        self.group.append(one)
+        count = len(earlier)
+        width = 1 if dim else 2
+        place = lambda d: (slot, d, 0, 0) if dim else (d, slot, 0, 0)
+        shape = (width, SHARES) if dim else (SHARES, width)
+
+        def share(d):
+            row, col = d // 4, d % 4
+            return row % 2 * 8 + row // 2 * 4 + col % 2 * 2 + col // 2
+
+        def body(act, delta, *refs):
+            refs[count + 1][0, 0] = product(act[0], delta[0]).astype(BFLOAT)
+
+        self.buffer, through = pl.pallas_call(
+            body,
+            grid=(SHARES,),
+            in_specs=[
+                pl.BlockSpec((1, SHARE_ROWS, tokens), lambda d: one.act_index(share(d))),
+                pl.BlockSpec((1, tokens, D), lambda d: one.delta_index(share(d))),
+            ]
+            + [ANYWHERE] * (count + 1),
+            out_specs=[pl.BlockSpec((1, 1, SHARE_ROWS, D), place), ANYWHERE],
+            out_shape=[
+                jax.ShapeDtypeStruct(shape + (SHARE_ROWS, D), BFLOAT),
+                jax.ShapeDtypeStruct(through.shape, through.dtype),
+            ],
+            input_output_aliases={2 + k: k for k in range(count)} | {2 + count: 1},
+            cost_estimate=SMALL,
+            compiler_params=params(),
+        )(one.act, one.delta, *earlier, through)
+        return through
+
+    def reduce(self):
+        dim = len(self.shares) % 2
+        summed = lax.psum_scatter(self.buffer, GRID_AXES, scatter_dimension=dim, tiled=True)
+        self.shares.append(summed.reshape(-1, SHARE_ROWS, D))
+        self.group = []
+
+    def gather(self, after):
+        shares = passed_by(self.shares, [after])
+        shares = [part[slot] for part in shares for slot in range(part.shape[0])]
+        for slot, one in enumerate(self.sums):
+            if isinstance(one, CrossGradSum):
+                shares[slot] = one.cross(shares[slot])
+        self.collect(jnp.stack(shares))
+
+
+class SmallSum:
+    works = ("sum",) * 4
+
+    def __init__(self, value):
+        self.value, self.state = value, 0
+
+    def start(self, through):
+        self.keep, self.flight = self.value, self.move(0, self.value)
+        return through
+
+    def move(self, stage, value):
+        return swap(value, *STAGES[stage])
+
+    def advanced(self, outs):
+        self.state += 1
+        (self.keep,) = outs
+        self.flight = None if self.done() else self.move(self.state, self.keep)
+
+    def done(self):
+        return self.state == len(self.works)
+
+
+def tick_kernel(*refs, works):
+    at, out = 0, 2 * len(works)
+    for work in works:
+        keep, flight = refs[at], refs[at + 1]
+        at += 2
+        count = keep.shape[0]
+        if work == "sum":
+            refs[out][...] = keep[...] + flight[...]
+            out += 1
+            continue
+        if work == "join":
+            refs[out][:count] = keep[...]
+            refs[out][count:] = flight[...]
+            out += 1
+            continue
+        for row in range(count):
+            value = (keep[row].astype(FLOAT) + flight[row].astype(FLOAT)).astype(BFLOAT)
+            if work == "add":
+                refs[out][row] = value
+            elif row < count // 2:
+                refs[out][row] = value
+            else:
+                refs[out + 1][row - count // 2] = value
+        out += 1 if work == "add" else 2
+
+
+def tick(sums, through):
+    if not sums:
+        return through
+    light = ("pass", "take")
+    working = [one for one in sums if one.works[one.state] not in light]
+    passing = [one for one in sums if one.works[one.state] in light]
+    operands, shapes, counts, works = [], [], [], []
+    for one in working:
+        operands += [one.keep, one.flight]
+        work, count = one.works[one.state], one.keep.shape[0]
+        works.append(work)
+        sizes = {"halve": [count // 2] * 2, "join": [2 * count]}.get(work, [count])
+        counts.append(len(sizes))
+        shapes += [
+            jax.ShapeDtypeStruct((k,) + one.keep.shape[1:], one.keep.dtype) for k in sizes
+        ]
+    kept = lambda one: [one.flight] if one.works[one.state] == "take" else [one.keep, one.flight]
+    passed = [value for one in passing for value in kept(one)] + [through]
+
+    def body(*refs):
+        ins, outs = refs[: len(operands)], refs[len(operands) + len(passed) :]
+        tick_kernel(*ins, *outs, works=works)
+
+    outs = pl.pallas_call(
+        body,
+        in_specs=[WHOLE] * len(operands) + [ANYWHERE] * len(passed),
+        out_specs=[WHOLE] * len(shapes) + [ANYWHERE] * len(passed),
+        out_shape=shapes + [jax.ShapeDtypeStruct(v.shape, v.dtype) for v in passed],
+        input_output_aliases={
+            len(operands) + k: len(shapes) + k for k in range(len(passed))
+        },
+        cost_estimate=SMALL,
+        compiler_params=params(),
+    )(*operands, *passed)
+    at = 0
+    for one, count in zip(working, counts):
+        one.advanced(outs[at : at + count])
+        at += count
+    for one in passing:
+        count = len(kept(one))
+        one.advanced(outs[at : at + count])
+        at += count
+    return outs[-1]
+
+
+def sum_small(value):
+    for axis, bit in STAGES:
+        value = value + swap(value, axis, bit)
+    return value
+
+
+def turned(values):
+    return jnp.transpose(values.reshape(-1, values.shape[2]))
+
+
+def own_half(values):
+    half = values.shape[-1] // 2
+    return jnp.where(lax.axis_index("batch") == 0, values[..., :half], values[..., half:])
+
+
+def spread(values):
+    items = values.shape[0] // 2
+    other = swap(values)
+    return jnp.concatenate([other[items:], other[:items]], axis=0)
+
+
+def shrink_sum(active, outer_low):
+    act = turned(active)[None]
+    delta = outer_low.reshape(1, -1, D)
+    return GradSum(act, delta, lambda s: (0, s, 0), lambda s: (0, 0, 0), STAGES)
+
+
+def expand_sum(second, inner_low):
+    act = turned(second)[None]
+    delta = inner_low.reshape(1, -1, inner_low.shape[-1])
+    return CrossGradSum(
+        act, delta, lambda s: (0, s // 8 * 4 + s % 4, 0), lambda s: (0, 0, s // 4 % 2), STAGES
+    )
+
+
+def mixer_delta(own, other, branch, branch_other, places, width, size):
+    tokens = own.shape[0]
+    block = tokens // 4
+    heads = width // HD
+
+    def body(places, mine, theirs, low, low_other, out, logits):
+        first = places[0] == 0
+        values = mine[...].astype(FLOAT), theirs[...].astype(FLOAT)
+        left = jnp.where(first, values[0], values[1])
+        right = jnp.where(first, values[1], values[0])
+        for j in range(3):
+            part = slice(j * size, j * size + width)
+            out[:, j * D : (j + 1) * D] = jnp.concatenate(
+                [left[:, part], right[:, part]], axis=1
+            ).astype(BFLOAT)
+        half = pl.program_id(0) < 2
+
+        @pl.when(half)
+        def _():
+            out[:, 3 * D :] = low[...]
+
+        @pl.when(jnp.logical_not(half))
+        def _():
+            out[:, 3 * D :] = low_other[...]
+
+        part = slice(width, width + heads)
+        rest = jnp.zeros((block, LANES - 2 * heads), FLOAT)
+        logits[...] = jnp.concatenate([left[:, part], right[:, part], rest], axis=1).astype(BFLOAT)
+
+    return pl.pallas_call(
+        body,
+        grid_spec=pltpu.PrefetchScalarGridSpec(
+            num_scalar_prefetch=1,
+            grid=(4,),
+            in_specs=[
+                pl.BlockSpec((block, 3 * size), lambda i, m: (i, 0)),
+                pl.BlockSpec((block, 3 * size), lambda i, m: (i ^ 2, 0)),
+                pl.BlockSpec((block, D), lambda i, m: (jnp.minimum(i, 1), 0)),
+                pl.BlockSpec((block, D), lambda i, m: (jnp.maximum(i - 2, 0), 0)),
+            ],
+            out_specs=[
+                pl.BlockSpec((block, 4 * D), lambda i, m: (i, 0)),
+                pl.BlockSpec((block, LANES), lambda i, m: (i, 0)),
+            ],
+        ),
+        out_shape=[
+            jax.ShapeDtypeStruct((tokens, 4 * D), BFLOAT),
+            jax.ShapeDtypeStruct((tokens, LANES), BFLOAT),
+        ],
+        cost_estimate=SMALL,
+        compiler_params=params(),
+    )(places, own, other, branch, branch_other)
+
+
+def mixer_sum(mixed, delta_project, attend, branch, branch_other, places, width, size):
+    act = jnp.stack([turned(own_half(mixed)[None]), turned(attend[None])])
+    delta, logits = mixer_delta(
+        delta_project, swap(delta_project), branch, branch_other, places, width, size
+    )
+    return (
+        GradSum(
+            act,
+            delta[None],
+            lambda s: (jnp.where(s % 4 == 3, 1, 0), s // 4, 0),
+            lambda s: (0, 0, s % 4),
+            STAGES,
+        ),
+        logits,
+    )
+
+
+ITEMS = 2
+ANYWHERE = pl.BlockSpec(memory_space=pl.ANY)
+WHOLE = pl.BlockSpec(memory_space=pltpu.VMEM)
+
+
+def call(body, shapes, arrays, places=None, held=(), after=(), scratch=()):
+    first = 0 if places is None else 1
+    count, kept, tied = len(arrays), len(held), len(after)
+
+    def whole(*refs):
+        ins = refs[first : first + count]
+        far = refs[first + count : first + count + kept]
+        at = first + count + kept + tied
+        outs = refs[at : at + len(shapes)]
+        body(refs[0] if first else None, ins, far, outs, refs[at + len(shapes) :])
+
+    return pl.pallas_call(
+        whole,
+        in_specs=[pl.BlockSpec(memory_space=pltpu.SMEM)] * first
+        + [WHOLE] * count
+        + [ANYWHERE] * (kept + tied),
+        out_specs=[WHOLE] * len(shapes),
+        out_shape=[jax.ShapeDtypeStruct(*shape) for shape in shapes],
+        scratch_shapes=list(scratch),
+        cost_estimate=SMALL,
+        compiler_params=params(),
+    )(*([] if places is None else [places]), *arrays, *held, *after)
+
+
+def edge_shapes(tile):
+    rows, cols = tile
+    sizes = [cols, cols, rows, rows]
+    return [((ITEMS, size, D), BFLOAT) for size in sizes]
+
+
+def put_edges(value, item, refs, tile):
+    rows, cols = tile
+    lines = [value[0], value[rows - 1]]
+    for at in (0, cols - 1):
+        lines.append(jnp.concatenate([value[r][at : at + 1] for r in range(rows)], axis=0))
+    for ref, line in zip(refs, lines):
+        ref[item] = line.astype(BFLOAT)
+
+
+def halo_edges(edges):
+    rows, cols = lax.axis_size("row"), lax.axis_size("col")
+    first_row, last_row, first_col, last_col = edges
+    top = lax.ppermute(last_row, "row", [(i, i + 1) for i in range(rows - 1)])
+    bottom = lax.ppermute(first_row, "row", [(i + 1, i) for i in range(rows - 1)])
+    to_right = jnp.concatenate([top[:, -1:], last_col, bottom[:, -1:]], axis=1)
+    to_left = jnp.concatenate([top[:, :1], first_col, bottom[:, :1]], axis=1)
+    left = lax.ppermute(to_right, "col", [(i, i + 1) for i in range(cols - 1)])
+    right = lax.ppermute(to_left, "col", [(i + 1, i) for i in range(cols - 1)])
+    return top, bottom, left, right
+
+
+def modulated(value, mod, shift, scale):
+    normal, inverse = normalize(value)
+    return normal * (1.0 + mod[scale : scale + 1]) + mod[shift : shift + 1]
+
+
+def enter_first(tokens, mod, tile):
+    cells = (ITEMS,) + tile + (D,)
+
+    def body(_, ins, far, outs, scratch):
+        for i in range(ITEMS):
+            hidden = modulated(ins[0][i].astype(FLOAT), ins[1][i], 0, 1).reshape(cells[1:])
+            outs[0][i] = hidden.astype(BFLOAT)
+            put_edges(hidden, i, outs[1:], tile)
+
+    hidden, *edges = call(body, [(cells, BFLOAT)] + edge_shapes(tile), [tokens, mod])
+    return hidden, edges
+
+
+def enter_next(middle, own, received, mod_before, mod, tile):
+    cells = (ITEMS,) + tile + (D,)
+    count = middle.shape[1]
+
+    def body(_, ins, far, outs, scratch):
+        for i in range(ITEMS):
+            at = slice(i * count, (i + 1) * count)
+            outer = ins[1][at] + ins[2][at].astype(FLOAT)
+            outs[1][i] = outer
+            value = ins[0][i] + ins[3][i][5:6] * outer
+            outs[0][i] = value
+            hidden = modulated(value, ins[4][i], 0, 1).reshape(cells[1:])
+            outs[2][i] = hidden.astype(BFLOAT)
+            put_edges(hidden, i, outs[3:], tile)
+
+    shapes = [(middle.shape, FLOAT), (middle.shape, FLOAT), (cells, BFLOAT)] + edge_shapes(tile)
+    value, outer, hidden, *edges = call(body, shapes, [middle, own, received, mod_before, mod])
+    return value, outer, hidden, edges
+
+
+def leave(middle, own, received, mod):
+    count = middle.shape[1]
+
+    def body(_, ins, far, outs, scratch):
+        for i in range(ITEMS):
+            at = slice(i * count, (i + 1) * count)
+            outer = ins[1][at] + ins[2][at].astype(FLOAT)
+            outs[1][i] = outer
+            outs[0][i] = (ins[0][i] + ins[3][i][5:6] * outer).astype(BFLOAT)
+
+    return call(
+        body, [(middle.shape, BFLOAT), (middle.shape, FLOAT)], [middle, own, received, mod]
+    )
+
+
+def gather_weight(far, scratch, sems, places, own):
+    batch, quarter = places[0], places[1]
+    rows = own.shape[0]
+    size = rows // 4
+    base = (1 - batch) * rows
+    parts = [(own, batch * rows, rows)]
+    for k in range(4):
+        parts.append((far[k], base + (quarter ^ k) * size, size))
+    copies = []
+    for k, (source, start, count) in enumerate(parts):
+        target = scratch.at[pl.ds(pl.multiple_of(start, 16), count)]
+        copy = pltpu.make_async_copy(source, target, sems.at[k])
+        copy.start()
+        copies.append(copy)
+    return copies
+
+
+def split_logit(block, start, heads):
+    lane = lax.broadcasted_iota(jnp.int32, block.shape, 1)
+    here = (lane >= start) & (lane < start + heads)
+    high = block.astype(BFLOAT).astype(FLOAT)
+    rest = jnp.where(here, block - high, 0.0)
+    middle = rest.astype(BFLOAT).astype(FLOAT)
+    low = rest - middle
+    return (
+        jnp.where(here, high, block) + pltpu.roll(middle, heads, 1) + pltpu.roll(low, 2 * heads, 1)
+    )
+
+
+def project_call(own, other, weight, bias, places, cells, width):
+    size = weight[0].shape[1] // 3
+    block = width // LANES * LANES
+    total = 2 * own.shape[0]
+    count = total // cells
+
+    def body(places, ins, far, outs, scratch):
+        whole, joined, result, sems = scratch
+        copies = gather_weight(far[1:], whole, sems, places, far[0])
+        joined[: total // 2] = ins[0][...]
+        joined[total // 2 :] = ins[1][...]
+        for copy in copies:
+            copy.wait()
+        for part in range(3):
+            columns = slice(part * size, (part + 1) * size)
+            value = dot(joined[...], whole[:, columns])
+            if part == 0:
+                last = split_logit(
+                    value[:, block : block + LANES] + ins[2][...], width - block, width // HD
+                )
+                result[:, :block] = value[:, :block].astype(BFLOAT)
+                result[:, block : block + LANES] = last.astype(BFLOAT)
+            else:
+                result[:, columns] = value.astype(BFLOAT)
+        for k in range(count):
+            start = pl.multiple_of((places[2] ^ k) * cells, cells)
+            outs[k][0] = result[pl.ds(start, cells)]
+
+    return call(
+        body,
+        [((1, cells, 3 * size), BFLOAT)] * count,
+        [own, other, bias],
+        places,
+        weight,
+        scratch=[
+            pltpu.VMEM((D, 3 * size), BFLOAT),
+            pltpu.VMEM((total, D), BFLOAT),
+            pltpu.VMEM((total, 3 * size), BFLOAT),
+            pltpu.SemaphoreType.DMA((5,)),
+        ],
+    )
+
+
+def halves_out(value, outs, columns, items_here):
+    outs[0][:, columns] = value[:items_here]
+    outs[1][:, columns] = value[items_here:].astype(BFLOAT)
+
+
+COLUMNS = 384
+
+
+def attend_out_call(blocks, weight, layer, places, cells, width):
+    count = len(blocks)
+    total = count * cells
+
+    def body(places, ins, far, outs, scratch):
+        whole, sems = scratch
+        copy = pltpu.make_async_copy(far[0].at[layer], whole, sems.at[0])
+        copy.start()
+        for k in range(count):
+            start = pl.multiple_of((places[2] ^ k) * cells, cells)
+            outs[2][pl.ds(start, cells)] = ins[k][0]
+        copy.wait()
+        for at in range(0, D, COLUMNS):
+            columns = slice(at, at + COLUMNS)
+            halves_out(dot(outs[2][...], whole[:, columns]), outs, columns, total // 2)
+
+    return call(
+        body,
+        [((total // 2, D), FLOAT), ((total // 2, D), BFLOAT), ((total, width), BFLOAT)],
+        blocks,
+        places,
+        [weight],
+        scratch=[pltpu.VMEM((width, D), BFLOAT), pltpu.SemaphoreType.DMA((1,))],
+    )
+
+
+def middle_call(tokens, own, received, mod):
+    count = tokens.shape[1]
+
+    def body(_, ins, far, outs, scratch):
+        for i in range(ITEMS):
+            at = slice(i * count, (i + 1) * count)
+            branch = ins[1][at] + ins[2][at].astype(FLOAT)
+            outs[0][i] = branch
+            middle = ins[0][i].astype(FLOAT) + ins[3][i][2:3] * branch
+            outs[1][i] = middle
+            outs[2][at] = modulated(middle, ins[3][i], 3, 4).astype(BFLOAT)
+
+    shape = tokens.shape
+    return call(
+        body,
+        [(shape, FLOAT), (shape, FLOAT), ((ITEMS * count, D), BFLOAT)],
+        [tokens, own, received, mod],
+    )
+
+
+def feed_call(own, other, expand, shrink, layer, places):
+    total = 2 * own.shape[0]
+    inner = shrink.shape[1]
+    rows = expand[0].shape[1]
+    tile = 256
+
+    def body(places, ins, far, outs, scratch):
+        wide, back, joined, sems = scratch
+        start = pl.multiple_of(places[0] * inner, LANES)
+        source = far[0].at[layer, :, pl.ds(start, inner)]
+        copies = gather_weight(far[1:5], wide, sems, places, source)
+        last = pltpu.make_async_copy(far[5].at[layer], back, sems.at[5])
+        last.start()
+        joined[: total // 2] = ins[0][...]
+        joined[total // 2 :] = ins[1][...]
+        for copy in copies:
+            copy.wait()
+        for at in range(0, inner, tile):
+            columns = slice(at, at + tile)
+            value = dot(joined[...], wide[:, columns])
+            outs[2][:, columns] = value
+            outs[3][:, columns] = gelu(value).astype(BFLOAT)
+        last.wait()
+        for at in range(0, D, COLUMNS):
+            columns = slice(at, at + COLUMNS)
+            halves_out(dot(outs[3][...], back[:, columns]), outs, columns, total // 2)
+
+    return call(
+        body,
+        [
+            ((total // 2, D), FLOAT),
+            ((total // 2, D), BFLOAT),
+            ((total, inner), FLOAT),
+            ((total, inner), BFLOAT),
+        ],
+        [own, other],
+        places,
+        list(expand) + [shrink],
+        scratch=[
+            pltpu.VMEM((2 * rows, inner), BFLOAT),
+            pltpu.VMEM((inner, D), BFLOAT),
+            pltpu.VMEM((total, D), BFLOAT),
+            pltpu.SemaphoreType.DMA((6,)),
+        ],
+    )
+
+
+def feed_back_call(own, other, inner_value, expand, shrink, layer, places):
+    total = 2 * own.shape[0]
+    inner = shrink.shape[1]
+    rows = expand[0].shape[1]
+    tile = 256
+
+    def body(places, ins, far, outs, scratch):
+        wide, back, joined, sems = scratch
+        last = pltpu.make_async_copy(far[5].at[layer], back, sems.at[5])
+        last.start()
+        start = pl.multiple_of(places[0] * inner, LANES)
+        source = far[0].at[layer, :, pl.ds(start, inner)]
+        copies = gather_weight(far[1:5], wide, sems, places, source)
+        joined[: total // 2] = ins[0][...]
+        joined[total // 2 :] = ins[1][...]
+        last.wait()
+        for at in range(0, inner, tile):
+            columns = slice(at, at + tile)
+            value = dot(joined[...], back[at : at + tile], ((1,), (1,)))
+            outs[2][:, columns] = (value * gelu_slope(ins[2][:, columns])).astype(BFLOAT)
+        for copy in copies:
+            copy.wait()
+        for at in range(0, D, COLUMNS):
+            columns = slice(at, at + COLUMNS)
+            value = dot(outs[2][...], wide[at : at + COLUMNS], ((1,), (1,)))
+            halves_out(value, outs, columns, total // 2)
+
+    return call(
+        body,
+        [((total // 2, D), FLOAT), ((total // 2, D), BFLOAT), ((total, inner), BFLOAT)],
+        [own, other, inner_value],
+        places,
+        list(expand) + [shrink],
+        scratch=[
+            pltpu.VMEM((2 * rows, inner), BFLOAT),
+            pltpu.VMEM((inner, D), BFLOAT),
+            pltpu.VMEM((total, D), BFLOAT),
+            pltpu.SemaphoreType.DMA((6,)),
+        ],
+    )
+
+
+def middle_back_call(delta, own, received, middle, branch, outer, mod):
+    count = middle.shape[1]
+    over = lambda v: jnp.sum(v, axis=0, keepdims=True)
+
+    def body(_, ins, far, outs, scratch):
+        for i in range(ITEMS):
+            at = slice(i * count, (i + 1) * count)
+            here = ins[0][i].astype(FLOAT)
+            mod_here = ins[6][i]
+            outs[2][i, 3:4] = over(here * ins[5][i])
+            second = ins[1][at] + ins[2][at].astype(FLOAT)
+            normal, inverse = normalize(ins[3][i])
+            outs[2][i, 1:2] = over(second)
+            outs[2][i, 2:3] = over(second * normal)
+            total = here + normalize_back(second * (1.0 + mod_here[4:5]), normal, inverse)
+            outs[0][i] = total
+            outs[2][i, 0:1] = over(total * ins[4][i])
+            outs[1][at] = (mod_here[2:3] * total).astype(BFLOAT)
+
+    return call(
+        body,
+        [(middle.shape, FLOAT), ((ITEMS * count, D), BFLOAT), ((ITEMS, 4, D), FLOAT)],
+        [delta, own, received, middle, branch, outer, mod],
+    )
+
+
+def attend_back_call(own, other, weight, layer, places, cells, width):
+    total = 2 * own.shape[0]
+    count = total // cells
+
+    def body(places, ins, far, outs, scratch):
+        whole, joined, result, sems = scratch
+        copy = pltpu.make_async_copy(far[0].at[layer], whole, sems.at[0])
+        copy.start()
+        joined[: total // 2] = ins[0][...]
+        joined[total // 2 :] = ins[1][...]
+        copy.wait()
+        result[...] = dot(joined[...], whole[...], ((1,), (1,))).astype(BFLOAT)
+        for k in range(count):
+            start = pl.multiple_of((places[2] ^ k) * cells, cells)
+            outs[k][0] = result[pl.ds(start, cells)]
+
+    return call(
+        body,
+        [((1, cells, width), BFLOAT)] * count,
+        [own, other],
+        places,
+        [weight],
+        scratch=[
+            pltpu.VMEM((width, D), BFLOAT),
+            pltpu.VMEM((total, D), BFLOAT),
+            pltpu.VMEM((total, width), BFLOAT),
+            pltpu.SemaphoreType.DMA((1,)),
+        ],
+    )
+
+
+def project_back_call(blocks, weight, places, cells, width):
+    count = len(blocks)
+    total = count * cells
+    wide = blocks[0].shape[2]
+
+    def body(places, ins, far, outs, scratch):
+        whole, sems = scratch
+        copies = gather_weight(far[1:], whole, sems, places, far[0])
+        for k in range(count):
+            start = pl.multiple_of((places[2] ^ k) * cells, cells)
+            outs[2][pl.ds(start, cells)] = ins[k][0]
+        at = width // LANES * LANES
+        logits = outs[2][:, at : at + LANES].astype(FLOAT)
+        outs[3][...] = jnp.sum(logits, axis=0, keepdims=True)
+        for copy in copies:
+            copy.wait()
+        for at in range(0, D, COLUMNS):
+            columns = slice(at, at + COLUMNS)
+            value = dot(outs[2][...], whole[at : at + COLUMNS], ((1,), (1,)))
+            halves_out(value, outs, columns, total // 2)
+
+    return call(
+        body,
+        [
+            ((total // 2, D), FLOAT),
+            ((total // 2, D), BFLOAT),
+            ((total, wide), BFLOAT),
+            ((1, LANES), FLOAT),
+        ],
+        blocks,
+        places,
+        weight,
+        scratch=[pltpu.VMEM((D, wide), BFLOAT), pltpu.SemaphoreType.DMA((5,))],
+    )
+
+
+def conv_delta_call(own, received, convolved, tile):
+    cells = convolved.shape
+    count = tile[0] * tile[1]
+
+    def body(_, ins, far, outs, scratch):
+        for i in range(ITEMS):
+            at = slice(i * count, (i + 1) * count)
+            delta = (ins[0][at] + ins[1][at].astype(FLOAT)).reshape(cells[1:])
+            value = ins[2][i]
+            gate = jax.nn.sigmoid(value)
+            delta = delta * gate * (1.0 + value * (1.0 - gate))
+            outs[0][i] = delta.astype(BFLOAT)
+            put_edges(delta, i, outs[1:], tile)
+
+    delta, *edges = call(
+        body, [(cells, BFLOAT)] + edge_shapes(tile), [own, received, convolved]
+    )
+    return delta, edges
+
+
+def enter_back_call(delta_hidden, tokens, delta_middle, mod, mod_before):
+    count = tokens.shape[1]
+    over = lambda v: jnp.sum(v, axis=0, keepdims=True)
+    lower = mod_before is not None
+
+    def body(_, ins, far, outs, scratch):
+        for i in range(ITEMS):
+            at = slice(i * count, (i + 1) * count)
+            here = ins[0][i].reshape(count, D)
+            normal, inverse = normalize(ins[1][i].astype(FLOAT))
+            outs[0][i, 0:1] = over(here)
+            outs[0][i, 1:2] = over(here * normal)
+            total = ins[2][i] + normalize_back(here * (1.0 + ins[3][i][1:2]), normal, inverse)
+            if lower:
+                outs[2][i] = total
+                outs[1][at] = (ins[4][i][5:6] * total).astype(BFLOAT)
+            else:
+                outs[1][at] = total.astype(BFLOAT)
+
+    shapes = [((ITEMS, 2, D), FLOAT), ((ITEMS * count, D), BFLOAT)]
+    arrays = [delta_hidden, tokens, delta_middle, mod]
+    if lower:
+        shapes.append((tokens.shape, FLOAT))
+        arrays.append(mod_before)
+    return call(body, shapes, arrays)
+
+
+def pack_kernel(places, qkv, decay, own, other, *, width):
+    heads = width // HD
+    size = padded_width(width + 3 * heads)
+    value, extra = qkv[0].astype(FLOAT), decay[0].astype(FLOAT)
+    rows = value.shape[0]
+    pieces = []
+    for group in range(2):
+        parts = []
+        for j in range(3):
+            start = j * D + group * width
+            parts.append(value[:, start : start + width])
+            filled = width
+            if j == 0:
+                parts.append(extra[:, group * heads : (group + 1) * heads])
+                filled += heads
+            parts.append(jnp.zeros((rows, size - filled), FLOAT))
+        pieces.append(jnp.concatenate(parts, axis=1).astype(BFLOAT))
+    first = places[0] == 0
+    own[...] = jnp.where(first, pieces[0], pieces[1])
+    other[...] = jnp.where(first, pieces[1], pieces[0])
+
+
+def pack_call(qkv, decay, layer, places, width):
+    rows = qkv.shape[1]
+    size = padded_width(width + 3 * (width // HD))
+
+    def body(*refs):
+        pack_kernel(*refs, width=width)
+
+    out = pl.BlockSpec((SHARE_ROWS, 3 * size), lambda i, m: (i, 0))
+    return pl.pallas_call(
+        body,
+        grid_spec=pltpu.PrefetchScalarGridSpec(
+            num_scalar_prefetch=1,
+            grid=(rows // SHARE_ROWS,),
+            in_specs=[
+                pl.BlockSpec((1, SHARE_ROWS, qkv.shape[2]), lambda i, m: (layer, i, 0)),
+                pl.BlockSpec((1, SHARE_ROWS, decay.shape[2]), lambda i, m: (layer, i, 0)),
+            ],
+            out_specs=[out, out],
+        ),
+        out_shape=[jax.ShapeDtypeStruct((rows, 3 * size), BFLOAT)] * 2,
+        cost_estimate=SMALL,
+        compiler_params=params(),
+    )(places, qkv, decay)
+
+
+def passed_by(values, after):
+    count = len(values)
+    return pl.pallas_call(
+        lambda *refs: None,
+        in_specs=[ANYWHERE] * (count + len(after)),
+        out_specs=[ANYWHERE] * count,
+        out_shape=[jax.ShapeDtypeStruct(v.shape, v.dtype) for v in values],
+        input_output_aliases={k: k for k in range(count)},
+        cost_estimate=SMALL,
+        compiler_params=params(),
+    )(*values, *after)
+
+
+def lines_swapped(blocks, axis):
+    return [blocks[0]] + [swap(blocks[k], axis, k) for k in range(1, len(blocks))]
+
+
+class Pair:
+    def __init__(self, args, modulations, taps, tile):
+        self.args, self.modulations, self.taps, self.tile = args, modulations, taps, tile
+        self.cells = tile[0] * tile[1]
+        self.width = args["proj"].shape[1]
+        self.heads = self.width // HD
+        self.size = padded_width(self.width + 3 * self.heads)
+        batch, row = lax.axis_index("batch"), lax.axis_index("row")
+        quarter = row % 2 * 2 + row // 2
+        self.places = [
+            jnp.stack([batch, quarter, lax.axis_index(axis)]).astype(jnp.int32)
+            for axis in ("col", "row")
+        ]
+        self.qkv, self.expand, self.bias = [], [], []
+        self.pieces = {}
+        for layer in range(LAYERS):
+            own, other = pack_call(
+                args["qkv"], args["decay"], layer, self.places[0], self.width
+            )
+            part = own.shape[0] // 4
+            piece = lax.dynamic_slice_in_dim(other, quarter * part, part, 0)
+            self.pieces["qkv", layer] = piece
+            self.qkv.append([own])
+            inner = args["shrink"].shape[1]
+            piece = lax.dynamic_slice(
+                args["expand"], (layer, quarter * part, (1 - batch) * inner), (1, part, inner)
+            )
+            self.pieces["expand", layer] = piece[0]
+            self.expand.append([args["expand"]])
+            start = self.width - self.width // LANES * LANES
+            self.bias.append(
+                jnp.pad(
+                    args["decay_bias"][layer].astype(FLOAT)[None],
+                    ((0, 0), (start, LANES - start - self.heads)),
+                )
+            )
+        for stage in range(3):
+            self.fetch("qkv", 0, stage, [])
+
+    def fetch(self, name, layer, stage, after):
+        held = self.pieces[name, layer]
+        if stage == 0:
+            if after:
+                (held,) = passed_by([held], after)
+            self.pieces[name, layer] = [swap(held)]
+        elif stage == 1:
+            if after:
+                held = passed_by(held, after)
+            self.pieces[name, layer] = [held[0], swap(held[0], "row", 2)]
+        else:
+            if after:
+                held = passed_by(held, after)
+            into = self.qkv if name == "qkv" else self.expand
+            into[layer] += list(held) + [swap(part, "row", 1) for part in held]
+
+    def axis(self, layer):
+        return "col" if layer % 2 == 0 else "row"
+
+    def scan(self, kernel, layer, inputs, out_width):
+        place = self.places[layer % 2][2]
+        rows, cols = self.tile
+        return scan_call(
+            kernel, place, inputs, out_width, rows, cols, layer % 2 == 0, self.width
+        )
+
+    def forward(self, layer, hidden, edges, tokens):
+        places, axis = self.places[layer % 2], self.axis(layer)
+        mod = self.modulations[layer]
+        sides = halo_edges(edges)
+        convolved, mixed = conv_forward(hidden, sides, self.taps[layer])
+        mixed = mixed.reshape(-1, D)
+        mixed_other = swap(mixed)
+        if layer == 0:
+            self.fetch("expand", 0, 0, [hidden])
+            self.fetch("expand", 0, 1, [mixed])
+        else:
+            self.fetch("expand", 1, 1, [mixed])
+        parts = project_call(
+            mixed, mixed_other, self.qkv[layer], self.bias[layer], places, self.cells, self.width
+        )
+        self.fetch("expand", layer, 2, [parts[0]])
+        if layer + 1 < LAYERS:
+            self.fetch("qkv", layer + 1, 0, [parts[0]])
+        parts = lines_swapped(parts, axis)
+        attends = self.scan(scan_forward_kernel, layer, parts, self.width)
+        own, send, attend = attend_out_call(
+            lines_swapped(attends, axis), self.args["proj"], layer, places, self.cells, self.width
+        )
+        if layer + 1 < LAYERS:
+            self.fetch("qkv", layer + 1, 1, [own])
+        branch, middle, second = middle_call(tokens, own, swap(send), mod)
+        second_other = swap(second)
+        if layer + 1 < LAYERS:
+            self.fetch("qkv", layer + 1, 2, [second])
+        own, send, inner, active = feed_call(
+            second, second_other, self.expand[layer], self.args["shrink"], layer, places
+        )
+        if layer + 1 < LAYERS:
+            self.fetch("expand", layer + 1, 0, [own])
+        saved = dict(
+            tokens=tokens, hidden=hidden, sides=sides, convolved=convolved, mixed=mixed,
+            mixed_other=mixed_other, parts=parts, attend=attend, branch=branch, middle=middle,
+            second=second, second_other=second_other, inner=inner, active=active,
+        )
+        return middle, own, swap(send), saved
+
+    def backward(self, layer, delta, outer_low, outer_other, saved, tick):
+        places, axis = self.places[layer % 2], self.axis(layer)
+        mod = self.modulations[layer]
+        both = lambda own, other: jnp.concatenate([own, other], axis=0)
+        own, send, inner_low = feed_back_call(
+            outer_low, outer_other, saved["inner"], self.expand[layer], self.args["shrink"],
+            layer, places,
+        )
+        received = swap(send)
+        shrink_pipe = shrink_sum(saved["active"][None], both(outer_low, outer_other))
+        own = tick("P1", {"A": shrink_pipe}, own)
+        delta_middle, branch_low, mod_b = middle_back_call(
+            delta, own, received, saved["middle"], saved["branch"], saved["outer"], mod
+        )
+        branch_other = swap(branch_low)
+        paired = lambda v: v.reshape(2, -1, v.shape[-1])
+        expand_pipe = expand_sum(
+            paired(both(saved["second"], saved["second_other"])), paired(inner_low)
+        )
+        branch_low = tick("P2", {"B": expand_pipe}, branch_low)
+        blocks = attend_back_call(
+            branch_low, branch_other, self.args["proj"], layer, places, self.cells, self.width
+        )
+        sent = lines_swapped(blocks, axis)
+        sent[0] = tick("P3", {}, sent[0])
+        projects = self.scan(
+            scan_backward_kernel, layer, list(saved["parts"]) + sent, 3 * self.size
+        )
+        sent = lines_swapped(projects, axis)
+        sent[0] = tick("P4", {}, sent[0])
+        own, send, delta_project, grad_bias = project_back_call(
+            sent, self.qkv[layer], places, self.cells, self.width
+        )
+        received = swap(send)
+        mixed = both(saved["mixed"], saved["mixed_other"])
+
+        def mixer(after):
+            (value,) = passed_by([delta_project], after)
+            pipe, logits = mixer_sum(
+                mixed, value, saved["attend"], branch_low, branch_other, places,
+                self.width, self.size,
+            )
+            return pipe, dot(logits, own_half(mixed), ((0,), (0,)))[: 2 * self.heads]
+
+        if not layer:
+            mixer_pipe, grad_decay = mixer([])
+        own = tick("P5", {}, own)
+        delta_conv, edges = conv_delta_call(own, received, saved["convolved"], self.tile)
+        delta_sides = halo_edges(edges)
+        delta_conv = tick("P6", {}, delta_conv)
+        if layer:
+            mixer_pipe, grad_decay = mixer([delta_conv])
+        top, bottom, left, right = delta_sides
+        left = tick("P8", {"C": mixer_pipe}, left)
+        delta_sides = (top, bottom, left, right)
+        delta_hidden, grad_taps = conv_backward(
+            saved["hidden"], saved["sides"], delta_conv, delta_sides, self.taps[layer]
+        )
+        before = self.modulations[layer - 1] if layer else None
+        mod_a, low, *rest = enter_back_call(
+            delta_hidden, saved["tokens"], delta_middle, mod, before
+        )
+        low_other = swap(low) if rest else None
+
+        small = SmallSum(join_smalls(mod_a, mod_b, grad_taps, grad_decay, grad_bias))
+        low = tick("P7", {"S": small}, low)
+        return rest[0] if rest else None, low, low_other
+
+
+def pair_forward_backward(pair, tokens_in, cotangent, tick):
+    tile = pair.tile
+    shape = (ITEMS, pair.cells, D)
+    tokens = tokens_in.reshape(shape)
+    delta = cotangent.reshape(shape)
+    outer_low = (pair.modulations[-1][:, 5:6] * delta.astype(FLOAT)).astype(BFLOAT)
+    hidden, edges = enter_first(tokens, pair.modulations[0], tile)
+    stored = []
+    for layer in range(LAYERS):
+        middle, own, received, saved = pair.forward(layer, hidden, edges, tokens)
+        stored.append(saved)
+        mod = pair.modulations[layer]
+        if layer + 1 < LAYERS:
+            tokens, saved["outer"], hidden, edges = enter_next(
+                middle, own, received, mod, pair.modulations[layer + 1], tile
+            )
+        else:
+            block_out, saved["outer"] = leave(middle, own, received, mod)
+    outer_low = outer_low.reshape(-1, D)
+    outer_other = swap(outer_low)
+    for layer in reversed(range(LAYERS)):
+        delta, outer_low, outer_other = pair.backward(
+            layer, delta, outer_low, outer_other, stored[layer],
+            lambda point, fresh, through, layer=layer: tick(layer, point, fresh, through),
+        )
+    return block_out, outer_low
 
 
 def forward_layer(tokens, modulation, weights, layer, tile):
@@ -454,6 +1664,12 @@
         normal2, inverse2, second, inner, active, outer,
     )
     return result, saved
+
+
+def pipelined(width):
+    shares = lax.axis_size("row") * lax.axis_size("col")
+    square = lax.axis_size("row") == 4 and lax.axis_size("col") == 4
+    return lax.axis_size("batch") == 2 and square and width == 4 * SHARE_ROWS and shares == SHARES
 
 
 def backward_layer(delta, saved, modulation, weights, layer, tile):
@@ -491,6 +1707,7 @@
     )
     delta_project = lines_back(projects, axis)
     grad_qkv = weight_grad(mixed, delta_project)
+    sums = (grad_shrink, grad_expand, grad_proj, grad_qkv)
     grad_decay_bias = jnp.sum(delta_project[:, :, width : width + heads].astype(FLOAT), axis=(0, 1))
     delta_mixed = reduce_items(matmul_back(delta_project, qkv)).reshape(convolved.shape)
     gate = jax.nn.sigmoid(convolved)
@@ -504,9 +1721,7 @@
     delta_mod = jnp.stack(
         [delta_shift1, delta_scale1, delta_gate1, delta_shift2, delta_scale2, delta_gate2], axis=1
     )
-    return delta_tokens, (grad_shrink, grad_expand, grad_proj, grad_qkv), (
-        delta_mod, grad_taps, grad_decay_bias,
-    )
+    return delta_tokens, sums, (delta_mod, grad_taps, None, grad_decay_bias)
 
 
 def sum_rows_here(grad):
@@ -526,6 +1741,143 @@
         return lax.all_gather(both, GRID_AXES, axis=1, tiled=True)
     total = lax.psum(low, GRID_AXES)
     return lax.all_to_all(total, "batch", 0, 0)
+
+
+def ada_call(cond, mods, previous, layer, through):
+    items, rows = cond.shape
+    wide = mods.shape[1]
+    block = 64
+    previous = [] if previous is None else [previous]
+
+    def body(columns, values, *refs):
+        out = refs[-2]
+        for at in range(0, wide, D):
+            part = slice(at, at + D)
+            total = columns[:, 0:1] * values[0:1, part]
+            for item in range(1, items):
+                total += columns[:, item : item + 1] * values[item : item + 1, part]
+            out[0, :, part] = total
+
+    count = len(previous)
+    return pl.pallas_call(
+        body,
+        grid=(rows // block,),
+        in_specs=[
+            pl.BlockSpec((block, items), lambda i: (i, 0)),
+            pl.BlockSpec((items, wide), lambda i: (0, 0)),
+        ]
+        + [ANYWHERE] * (count + 1),
+        out_specs=[pl.BlockSpec((1, block, wide), lambda i: (layer, i, 0)), ANYWHERE],
+        out_shape=[
+            jax.ShapeDtypeStruct((LAYERS, rows, wide), FLOAT),
+            jax.ShapeDtypeStruct(through.shape, through.dtype),
+        ],
+        input_output_aliases={2 + k: k for k in range(count)} | {2 + count: 1},
+        cost_estimate=SMALL,
+        compiler_params=params(),
+    )(jnp.transpose(cond.astype(FLOAT)), mods, *previous, through)
+
+
+SCHEDULE = {
+    (1, "P1"): "aA1",
+    (1, "P2"): "aB1rL1",
+    (1, "P7"): "sC1sS1",
+    (0, "P1"): "kC1sA0",
+    (0, "P2"): "tS1kA0sB0",
+    (0, "P3"): "gL1kB0",
+    (0, "P4"): "tS1",
+    (0, "P5"): "tC1tS1",
+    (0, "P8"): "tC1tA0tS1sC0",
+    (0, "P7"): "tC1tA0tB0kC0sS0",
+}
+TAIL = (
+    "tA0tB0tS0",
+    "mS1",
+    "tB0tC0tS0",
+    "tB0tC0tS0",
+    "tC0tS0gL0",
+    "fAB1",
+    "mS0",
+    "fC1",
+    "fABC0",
+)
+
+
+SMALL_ROWS = 32
+
+
+def join_smalls(mod_a, mod_b, grad_taps, grad_decay, grad_bias):
+    heads = grad_decay.shape[0] // 2
+
+    def body(_, ins, far, outs, scratch):
+        out = outs[0]
+        for i in range(ITEMS):
+            out[6 * i : 6 * i + 2] = ins[0][i]
+            out[6 * i + 2 : 6 * i + 6] = ins[1][i]
+        out[12:21] = ins[2][...]
+        out[21 : 21 + heads] = jnp.concatenate([ins[3][:heads], ins[3][heads:]], axis=1)
+        bias = jnp.concatenate([ins[4][...], jnp.zeros((1, D - LANES), FLOAT)], axis=1)
+        out[21 + heads : 22 + heads] = bias
+        out[22 + heads :] = jnp.zeros((SMALL_ROWS - 22 - heads, D), FLOAT)
+
+    return call(
+        body, [((SMALL_ROWS, D), FLOAT)], [mod_a, mod_b, grad_taps, grad_decay, grad_bias]
+    )[0]
+
+
+def split_smalls(flat, items, heads, width):
+    start = width - width // LANES * LANES
+    decay = flat[21 : 21 + heads]
+    return (
+        flat[: items * 6].reshape(items, 6 * D),
+        flat[12:21],
+        jnp.concatenate([decay[:, :width], decay[:, width:]], axis=0),
+        flat[21 + heads, start : start + heads],
+    )
+
+
+def general_forward_backward(
+    tokens_in, cotangent, modulations, taps_all, qkv_weight, decay_weight, decay_bias,
+    proj_weight, expand_weight, shrink_weight,
+):
+    count = lax.axis_size("batch")
+    items, rows, cols = tokens_in.shape[:3]
+    tile = (rows, cols)
+    width = proj_weight.shape[1]
+    weights = []
+    for layer in range(LAYERS):
+        qkv = fetch_columns(
+            [head_columns(qkv_weight[layer], decay_weight[layer], g, width) for g in range(count)]
+        )
+        inner = expand_weight.shape[2] // count
+        expand = fetch_columns(
+            [expand_weight[layer][:, g * inner : (g + 1) * inner] for g in range(count)]
+        )
+        weights.append(
+            (taps_all[layer], qkv, decay_bias[layer], proj_weight[layer], expand, shrink_weight[layer])
+        )
+    tokens = tokens_in.astype(FLOAT).reshape(items, rows * cols, D)
+    stored = []
+    for layer in range(LAYERS):
+        tokens, saved = forward_layer(tokens, modulations[layer], weights[layer], layer, tile)
+        stored.append(saved)
+    delta = cotangent.astype(FLOAT).reshape(tokens.shape)
+    bigs, smalls = [None] * LAYERS, [None] * LAYERS
+    for layer in reversed(range(LAYERS)):
+        delta, big, small = backward_layer(
+            delta, stored[layer], modulations[layer], weights[layer], layer, tile
+        )
+        grad_shrink, grad_expand, grad_proj, grad_qkv = big
+        bigs[layer] = (
+            sum_rows_here(grad_shrink),
+            sum_columns(grad_expand),
+            sum_rows_here(grad_proj),
+            sum_columns(grad_qkv),
+        )
+        smalls[layer] = tuple(
+            None if part is None else lax.psum(part, GRID_AXES) for part in small
+        )
+    return tokens.astype(BFLOAT), delta.astype(BFLOAT), bigs, smalls
 
 
 def per_device(
@@ -548,8 +1900,8 @@
         )
     else:
         cond_first = cond_slice
-    biases = lax.all_gather(ada_bias, "batch", axis=1, tiled=True).astype(FLOAT)
-    taps_all = lax.all_gather(conv_taps, "batch", axis=2, tiled=True)
+    biases = gather_last(ada_bias).astype(FLOAT)
+    taps_all = gather_last(conv_taps)
     weights, modulations = [], []
     partial = jnp.stack(
         [
@@ -564,71 +1916,126 @@
         total = lax.psum_scatter(partial, "batch", scatter_dimension=0, tiled=True)
     for layer in range(LAYERS):
         modulations.append((total[:, layer] + biases[layer]).reshape(items, 6, D))
-    for layer in range(LAYERS):
-        qkv = fetch_columns(
-            [head_columns(qkv_weight[layer], decay_weight[layer], g, width) for g in range(count)]
-        )
-        inner = expand_weight.shape[2] // count
-        expand = fetch_columns(
-            [expand_weight[layer][:, g * inner : (g + 1) * inner] for g in range(count)]
-        )
-        weights.append(
-            (taps_all[layer], qkv, decay_bias[layer], proj_weight[layer], expand, shrink_weight[layer])
-        )
-    tokens = tokens_in.astype(FLOAT).reshape(items, rows * cols, D)
-    stored = []
-    for layer in range(LAYERS):
-        tokens, saved = forward_layer(tokens, modulations[layer], weights[layer], layer, tile)
-        stored.append(saved)
-    block_out = tokens.astype(BFLOAT).reshape(tokens_in.shape)
-    delta = cotangent.astype(FLOAT).reshape(tokens.shape)
-    bigs, smalls = [None] * LAYERS, [None] * LAYERS
-    for layer in reversed(range(LAYERS)):
-        delta, big, small = backward_layer(
-            delta, stored[layer], modulations[layer], weights[layer], layer, tile
-        )
-        grad_shrink, grad_expand, grad_proj, grad_qkv = big
-        bigs[layer] = (
-            sum_rows_here(grad_shrink),
-            sum_columns(grad_expand),
-            sum_rows_here(grad_proj),
-            sum_columns(grad_qkv),
-        )
-        smalls[layer] = small
-    grad_tokens = delta.astype(BFLOAT).reshape(tokens_in.shape)
-    delta_mods, taps_grads, bias_grads = lax.psum(
-        tuple(jnp.stack([smalls[layer][k] for layer in range(LAYERS)]) for k in range(3)), GRID_AXES
-    )
-    every_mod = gather_items(delta_mods.transpose(1, 0, 2, 3)).reshape(count * items, LAYERS, 6 * D)
+    fast = pipelined(width) and count * items == 4 and tile == (8, 8)
+    hidden_units = shrink_weight.shape[1]
+    if fast:
+        moving = {}
+        upper_sums = Scattered()
+
+        def act(names, through):
+            names = [names[at : at + 3] for at in range(0, len(names), 3)]
+            steps = [moving[name[1:]] for name in names if name[0] == "t"]
+            through = tick(steps, through)
+            for name in names:
+                one = moving.get(name[1:])
+                if name[0] == "s":
+                    through = one.start(through)
+                elif name[0] == "k":
+                    through = one.second(through)
+                elif name == "gL1":
+                    upper_sums.gather(through)
+                elif name == "gL0":
+                    Gathered([moving[name] for name in ("C1", "A0", "B0", "C0")]).gather()
+                elif name[0] == "a":
+                    through = upper_sums.add(one, through)
+                elif name[0] == "r":
+                    upper_sums.reduce()
+            return through
+
+        def step(layer, point, fresh, through):
+            for name, one in fresh.items():
+                moving[name if len(name) == 2 else name + str(layer)] = one
+                if name in "ABC":
+                    one.offload = True
+            return act(SCHEDULE.get((layer, point), ""), through)
+
+        pair = Pair(
+            dict(
+                qkv=qkv_weight, decay=decay_weight, decay_bias=decay_bias, proj=proj_weight,
+                expand=expand_weight, shrink=shrink_weight,
+            ),
+            modulations,
+            taps_all,
+            tile,
+        )
+        block_out, through = pair_forward_backward(pair, tokens_in, cotangent, step)
+        shapes = [
+            (LAYERS, hidden_units, D),
+            (LAYERS, rows_here, expand_weight.shape[2]),
+            (LAYERS, rows_here, 3 * D),
+            (LAYERS, width, D),
+        ]
+        finished = None
+        grad_ada = None
+        smalls = [None] * LAYERS
+        for names in TAIL:
+            if names[0] == "f":
+                kinds = names[1:-1]
+                layer = int(names[-1])
+                made, through = Gathered.finish(
+                    [moving[kind + names[-1]] for kind in kinds], kinds,
+                    None if layer else finished, layer, shapes, through,
+                )
+                finished = (finished or {}) | made
+            elif names[0] == "m":
+                layer = int(names[2])
+                smalls[layer] = list(split_smalls(moving[names[1:]].keep, items, heads, width))
+                mods = gather_items(smalls[layer][0])
+                smalls[layer][0] = mods
+                grad_ada, through = ada_call(cond_first, mods, grad_ada, layer, through)
+            else:
+                through = act(names, through)
+        grad_tokens = through
+    else:
+        block_out, grad_tokens, bigs, smalls = general_forward_backward(
+            tokens_in, cotangent, modulations, taps_all, qkv_weight, decay_weight, decay_bias,
+            proj_weight, expand_weight, shrink_weight,
+        )
+    block_out = block_out.reshape(tokens_in.shape)
+    grad_tokens = grad_tokens.reshape(tokens_in.shape)
+    delta_mods, taps_grads, bias_grads = (
+        jnp.stack([smalls[layer][k] for layer in range(LAYERS)]) for k in (0, 1, 3)
+    )
+    if fast:
+        every_mod = delta_mods.transpose(1, 0, 2)
+    else:
+        every_mod = gather_items(delta_mods.transpose(1, 0, 2, 3)).reshape(
+            count * items, LAYERS, 6 * D
+        )
     if count == 2:
         taps_every = taps_grads + swap(taps_grads)
     else:
         taps_every = lax.psum(taps_grads, "batch")
     grad_taps = lax.dynamic_slice_in_dim(taps_every, place * width, width, 2)
-    grad_ada = jnp.zeros((LAYERS, rows_here, 6 * D), FLOAT)
-    for item in range(count * items):
-        grad_ada += (
-            cond_first[item].astype(FLOAT)[None, :, None] * every_mod[item][:, None, :]
-        )
+    if not fast:
+        grad_ada = jnp.zeros((LAYERS, rows_here, 6 * D), FLOAT)
+        for item in range(count * items):
+            grad_ada += (
+                cond_first[item].astype(FLOAT)[None, :, None] * every_mod[item][:, None, :]
+            )
     bias_width = ada_bias.shape[1]
     grad_ada_bias = lax.dynamic_slice_in_dim(
         jnp.sum(every_mod, axis=0), place * bias_width, bias_width, 1
     )
-    stack = lambda k: jnp.stack([bigs[layer][k] for layer in range(LAYERS)])
-    grad_shrink, grad_proj = stack(0), stack(2)
-    expand_parts, qkv_parts = stack(1), stack(3)
-    grad_expand = jnp.concatenate([expand_parts[:, g] for g in range(count)], 2).astype(FLOAT)
-    grad_qkv = jnp.concatenate(
-        [
-            qkv_parts[:, g, :, j * size : j * size + width]
-            for j in range(3)
-            for g in range(count)
-        ],
-        axis=2,
-    ).astype(FLOAT)
-    grad_decay = jnp.concatenate(
-        [qkv_parts[:, g, :, width : width + heads] for g in range(count)], axis=2
-    ).astype(FLOAT)
+    if fast:
+        grad_shrink, grad_expand, grad_qkv, grad_proj = (finished[k] for k in range(4))
+        grad_decay = jnp.stack([jnp.transpose(smalls[layer][2]) for layer in range(LAYERS)])
+    else:
+        stack = lambda k: jnp.stack([bigs[layer][k] for layer in range(LAYERS)])
+        grad_shrink, grad_proj = stack(0), stack(2)
+        expand_parts, qkv_parts = stack(1), stack(3)
+        grad_expand = jnp.concatenate([expand_parts[:, g] for g in range(count)], 2).astype(FLOAT)
+        grad_qkv = jnp.concatenate(
+            [
+                qkv_parts[:, g, :, j * size : j * size + width]
+                for j in range(3)
+                for g in range(count)
+            ],
+            axis=2,
+        ).astype(FLOAT)
+        grad_decay = jnp.concatenate(
+            [qkv_parts[:, g, :, width : width + heads] for g in range(count)], axis=2
+        ).astype(FLOAT)
     return (
         block_out,
         grad_tokens,

time: 1480 us -> 900 us (0.61)
  waiting for transfers between devices: 867 us -> 378 us
  Pallas kernels: 24.9 us -> 231 us
  local copies, waits for them, and re-layouts: 192 us -> 87.6 us
  blocking collectives: 87.8 us -> 0 us
  other arithmetic: 93.8 us -> 19.8 us
  matrix products: 78.6 us -> 9.25 us
  starting transfers between devices: 105 us -> 144 us
    unnamed x7 -> x3, waiting for transfers between devices: 530 us -> 0.05 us
    pallas_call x0 -> x65, Pallas kernels: none -> 205 us  [the longest x25 66 us: call(): pl.pallas_call(whole, in_specs=[pl.BlockSpec(memory_space=pltpu.SMEM)] *...]
    ppermute x55 -> x88, waiting for transfers between devices: 153 us -> 230 us  [swap(): return lax.ppermute(value, axis, [(i, i ^ bit) for i in range(count)])]
    dot_general x24 -> x2, matrix products: 69.8 us -> 0.37 us  [dot(): lax.dot_general(left, right, (contract, ((), ())), precision=precision, p...]
    all_gather x2 -> x0, blocking collectives: 56.1 us -> none  [the longest x1 47.5 us: per_device(): biases = lax.all_gather(ada_bias, 'batch', axis=1, tiled=True).astype(FLOAT)]
    all_gather x4 -> x2, waiting for transfers between devices: 140 us -> 84.1 us  [collect(): whole = lax.all_gather(shares, GRID_AXES)]
    ppermute x55 -> x88, starting transfers between devices: 59.2 us -> 112 us  [swap(): return lax.ppermute(value, axis, [(i, i ^ bit) for i in range(count)])]
    ppermute x16 -> x18, waiting for transfers between devices: 18.6 us -> 64.3 us  [the longest x4 30.6 us: halo_edges(): right = lax.ppermute(to_left, 'col', [(i + 1, i) for i in range(cols - 1)])]
  transfers between devices with their start and end apart: 77 -> 109, of which waited for: 46 -> 47; matrix products, arithmetic and copies ran while one was open for 19% -> 7% of each run, Pallas kernels for 1% -> 21%
where the time goes in v2:
time: 900 us; the launch traced here: 886 us
  waiting for transfers between devices  378 us (42%)
  Pallas kernels  231 us (26%)
  starting transfers between devices  144 us (16%)
  local copies, waits for them, and re-layouts  87.6 us (10%)
  other arithmetic  19.8 us (2%)
  between operations  16.1 us (2%)
  matrix products  9.25 us (1%)
    ppermute x88, waiting for transfers between devices, swap(): return lax.ppermute(value, axis, [(i, i ^ bit) for i in range(count)])  230 us
    ppermute x88, starting transfers between devices, swap(): return lax.ppermute(value, axis, [(i, i ^ bit) for i in range(count)])  112 us
    all_gather x2, waiting for transfers between devices, collect(): whole = lax.all_gather(shares, GRID_AXES)  84.1 us
    pallas_call x25, Pallas kernels, call(): pl.pallas_call(whole, in_specs=[pl.BlockSpec(memory_space=pltpu.SMEM)] *...  66 us
    unnamed x350, local copies, waits for them, and re-layouts  56.1 us
    pallas_call x3, Pallas kernels, finish(): pl.pallas_call(body, grid_spec=pltpu.PrefetchScalarGridSpec(num_scalar_pr...  46.3 us
    pallas_call x8, Pallas kernels, call(): pl.pallas_call(body, grid_spec=pltpu.PrefetchScalarGridSpec(num_scalar_pr...  37.6 us
    ppermute x4, waiting for transfers between devices, halo_edges(): right = lax.ppermute(to_left, 'col', [(i + 1, i) for i in range(cols - 1)])  30.6 us
  transfers between devices with their start and end apart: 109, of which 47 were waited for; matrix products, arithmetic and copies ran while one was open for 7% of the time, Pallas kernels for 21%

profile of v2, /device:TPU:0, one launch (start us, length us, event | category | flops | bytes accessed | tf_op | source)
XLA Modules:
  0.0 886.0 jit_solution(14965302358980485892)
XLA Ops:
  65.0 8.8 collective-permute-done.7
  93.5 10.4 %collective-permute-done.13.refs_3_ = bf16[1,64,1920]{2,1,0:T(8,128)(2,1)S(1)} collective-permute-done((bf16[1,64,1920]{2,1,0:T(8,128)(2,1)S(1)}, bf16[1,64,1920]{2,1,0:T(8,128)(2,1)S(1)}, u32[]{:S(2)}, u32[]{:S(2)}) %collective-permute-start.13) | collective-permute-done | bytes 245792 | tf_op jit(solution)/shard_map/ppermute | solution.py:32
  121.4 12.3 %collective-permute-done.18.refs_2_ = bf16[128,1152]{1,0:T(8,128)(2,1)S(1)} collective-permute-done((bf16[128,1152]{1,0:T(8,128)(2,1)S(1)}, bf16[128,1152]{1,0:T(8,128)(2,1)S(1)}, u32[]{:S(2)}, u32[]{:S(2)}) %collective-permute-start.18) | collective-permute-done | bytes 294944 | tf_op jit(solution)/shard_map/ppermute | solution.py:32
  260.0 7.9 shard_map.227
  271.2 9.4 %shard_map.229 = (f32[128,1152]{1,0:T(8,128)S(1)}, bf16[128,1152]{1,0:T(8,128)(2,1)}, bf16[256,2304]{1,0:T(8,128)(2,1)S(1)}) custom-call(s32[3]{0:T(128)S(1)} %pad_add_fusion.2.refs_0_.places, bf16[128,1152]{1,0:T(8,128)(2,1)} %fusion.12.refs_1_, bf16[128,1152]{1,0:T(8,128)(2,1)} %collective-permute-done.47.refs_2_, f32[256,2304]{1,0:T(8,128)} %get-tuple-element.264.refs_3_, ...), custom_call_target="tpu_custom_call" | custom-call | flops 1 | bytes 1 | tf_op jit(solution)/shard_map/pallas_call | solution.py:909
  290.7 8.3 shard_map.230
  311.2 8.5 shard_map.232
  355.8 8.0 collective-permute-done.56.refs_1_
  410.0 8.9 shard_map.242
  431.4 8.9 %collective-permute-done.66.refs_2_ = bf16[128,1152]{1,0:T(8,128)(2,1)S(1)} collective-permute-done((bf16[128,1152]{1,0:T(8,128)(2,1)S(1)}, bf16[128,1152]{1,0:T(8,128)(2,1)S(1)}, u32[]{:S(2)}, u32[]{:S(2)}) %collective-permute-start.66) | collective-permute-done | bytes 294944 | tf_op jit(solution)/shard_map/ppermute | solution.py:32
  504.1 13.5 %collective-permute-done.67.refs_1_ = f32[32,1152]{1,0:T(8,128)S(1)} collective-permute-done((f32[32,1152]{1,0:T(8,128)S(1)}, f32[32,1152]{1,0:T(8,128)S(1)}, u32[]{:S(2)}, u32[]{:S(2)}) %collective-permute-start.67) | collective-permute-done | bytes 147488 | tf_op jit(solution)/shard_map/ppermute | solution.py:32
  520.2 8.8 collective-permute-done.76.refs_3_
  541.2 13.7 %collective-permute-done.74.refs_3_ = f32[32,1152]{1,0:T(8,128)S(1)} collective-permute-done((f32[32,1152]{1,0:T(8,128)S(1)}, f32[32,1152]{1,0:T(8,128)S(1)}, u32[]{:S(2)}, u32[]{:S(2)}) %collective-permute-start.74) | collective-permute-done | bytes 147488 | tf_op jit(solution)/shard_map/ppermute | solution.py:32
  566.3 25.1 %collective-permute-done.83.refs_6_ = bf16[2,8,1152]{2,1,0:T(8,128)(2,1)S(1)} collective-permute-done((bf16[2,8,1152]{2,1,0:T(8,128)(2,1)}, bf16[2,8,1152]{2,1,0:T(8,128)(2,1)S(1)}, u32[]{:S(2)}, u32[]{:S(2)}) %collective-permute-start.83) | collective-permute-done | bytes 36896 | tf_op jit(solution)/shard_map/ppermute | solution.py:941
  614.4 19.8 %collective-permute-done.89.refs_8_ = bf16[2,10,1152]{2,1,0:T(8,128)(2,1)S(1)} collective-permute-done((bf16[2,10,1152]{2,1,0:T(8,128)(2,1)S(1)}, bf16[2,10,1152]{2,1,0:T(8,128)(2,1)S(1)}, u32[]{:S(2)}, u32[]{:S(2)}) %collective-permute-start.89) | collective-permute-done | bytes 46112 | tf_op jit(solution)/shard_map/ppermute | solution.py:945
  657.9 11.7 %collective-permute-done.90.refs_1_ = bf16[1,144,1152]{2,1,0:T(8,128)(2,1)} collective-permute-done((bf16[1,144,1152]{2,1,0:T(8,128)(2,1)}, bf16[1,144,1152]{2,1,0:T(8,128)(2,1)}, u32[]{:S(2)}, u32[]{:S(2)}) %collective-permute-start.90) | collective-permute-done | bytes 331808 | tf_op jit(solution)/shard_map/ppermute | solution.py:32
  672.9 9.1 %shard_map.267 = (f32[2,576,6912]{2,1,0:T(8,128)}, bf16[128,1152]{1,0:T(8,128)(2,1)}) custom-call(f32[576,4]{1,0:T(8,128)S(1)} %copy-done.35, f32[4,6912]{1,0:T(4,128)S(1)} %get-tuple-element.483.values, bf16[128,1152]{1,0:T(8,128)(2,1)} %get-tuple-element.381.refs_0_), custom_call_target="tpu_custom_call", output_to_operand_aliasing={{1}: (2, {})} | custom-call | flops 1 | bytes 1 | tf_op jit(solution)/shard_map/pallas_call | solution.py:1762
  689.6 16.0 %collective-permute-done.99.refs_3_ = f32[32,1152]{1,0:T(8,128)S(1)} collective-permute-done((f32[32,1152]{1,0:T(8,128)S(1)}, f32[32,1152]{1,0:T(8,128)S(1)}, u32[]{:S(2)}, u32[]{:S(2)}) %collective-permute-start.99) | collective-permute-done | bytes 147488 | tf_op jit(solution)/shard_map/ppermute | solution.py:32
  709.3 20.8 %collective-permute-done.102.refs_3_ = f32[32,1152]{1,0:T(8,128)S(1)} collective-permute-done((f32[32,1152]{1,0:T(8,128)S(1)}, f32[32,1152]{1,0:T(8,128)S(1)}, u32[]{:S(2)}, u32[]{:S(2)}) %collective-permute-start.102) | collective-permute-done | bytes 147488 | tf_op jit(solution)/shard_map/ppermute | solution.py:32
  739.7 15.3 %shard_map.272 = (f32[2,2304,1152]{2,1,0:T(8,128)}, f32[2,576,4608]{2,1,0:T(8,128)}, bf16[128,1152]{1,0:T(8,128)(2,1)}) custom-call(s32[1]{0:T(128)} %bitcast.1.m, bf16[16,2,144,1152]{3,2,1,0:T(8,128)(2,1)} %bitcast.132, bf16[16,2,144,1152]{3,2,1,0:T(8,128)(2,1)} %bitcast.133, ...), custom_call_target="tpu_custom_call", output_to_operand_aliasing={{2}: (3, {})} | custom-call | flops 1 | bytes 1 | tf_op jit(solution)/shard_map/pallas_call | solution.py:620
  755.0 9.1 %shard_map.273 = (f32[2,576,6912]{2,1,0:T(8,128)}, bf16[128,1152]{1,0:T(8,128)(2,1)}) custom-call(f32[576,4]{1,0:T(8,128)S(1)} %copy-done.35, f32[4,6912]{1,0:T(4,128)S(1)} %get-tuple-element.481.values, f32[2,576,6912]{2,1,0:T(8,128)} %get-tuple-element.399.refs_0_, ...), custom_call_target="tpu_custom_call", output_to_operand_aliasing={{0}: (2, {}), {1}: (3, {})} | custom-call | flops 1 | bytes 1 | tf_op jit(solution)/shard_map/pallas_call | solution.py:1762
  764.1 84.1 %all-gather.5.cloned.1.call-done = bf16[64,144,1152]{2,1,0:T(8,128)(2,1)} async-done(((bf16[4,144,1152]{2,1,0:T(8,128)(2,1)}), bf16[64,144,1152]{2,1,0:T(8,128)(2,1)}) %all-gather.5.cloned.1.call-update) | async-done | bytes 21233680 | tf_op jit(solution)/shard_map/all_gather | solution.py:574
  848.2 12.0 %shard_map.274 = (f32[2,576,3456]{2,1,0:T(8,128)}, f32[2,576,1152]{2,1,0:T(8,128)}, bf16[128,1152]{1,0:T(8,128)(2,1)}) custom-call(s32[1]{0:T(128)} %bitcast.1.m, bf16[16,4,144,1152]{3,2,1,0:T(8,128)(2,1)} %bitcast.128, bf16[128,1152]{1,0:T(8,128)(2,1)} %get-tuple-element.401.refs_1_), custom_call_target="tpu_custom_call", output_to_operand_aliasing={{2}: (2, {})} | custom-call | flops 1 | bytes 1 | tf_op jit(solution)/shard_map/pallas_call | solution.py:620
  860.2 19.1 %shard_map.275 = (f32[2,2304,1152]{2,1,0:T(8,128)}, f32[2,576,4608]{2,1,0:T(8,128)}, f32[2,576,3456]{2,1,0:T(8,128)}, f32[2,576,1152]{2,1,0:T(8,128)}, bf16[128,1152]{1,0:T(8,128)(2,1)}) custom-call(s32[1]{0:T(128)} %bitcast.1.m, ...), custom_call_target="tpu_custom_call", output_to_operand_aliasing={{0}: (4, {}), {1}: (5, {}), {2}: (6, {}), {3}: (7, {}), {4}... | custom-call | flops 1 | bytes 1 | tf_op jit(solution)/shard_map/pallas_call | solution.py:620
  (716 shorter events, 500.7 us)
Async XLA Ops:
  7.2 458.2 %reduce-scatter.2.cloned.1.call-start = ((), (), s32[]{:S(2)}) async-start(), calls=%async_computation.1 | async-start | bytes 11280384 | tf_op jit(solution)/shard_map/reduce_scatter | solution.py:681
  62.2 29.4 %collective-permute-start.21 = (bf16[144,2304]{1,0:T(8,128)(2,1)S(1)}, bf16[144,2304]{1,0:T(8,128)(2,1)}, u32[]{:S(2)}, u32[]{:S(2)}) collective-permute-start(bf16[144,2304]{1,0:T(8,128)(2,1)S(1)} %shard_map.211.refs_0_), channel_id=1, source_target_pairs={{0,8},{4,12},{8,0},{12,4},{1,9},{5,13},{9,1},{13,5},{2,10},{6,14},... | collective-permute-start | bytes 1990664 | tf_op jit(solution)/shard_map/ppermute | solution.py:32
  91.6 55.6 %collective-permute-start.22 = (bf16[144,2304]{1,0:T(8,128)(2,1)S(1)}, bf16[144,2304]{1,0:T(8,128)(2,1)}, u32[]{:S(2)}, u32[]{:S(2)}) collective-permute-start(bf16[144,2304]{1,0:T(8,128)(2,1)S(1)} %get-tuple-element.231.refs_4_.refs_5_), channel_id=1, source_target_pairs={{0,4},{4,0},{8,12},{12,8},{1,5},{5,1},{9,13},{13,9},{2,6},{6,2},{1... | collective-permute-start | bytes 1990664 | tf_op jit(solution)/shard_map/ppermute | solution.py:32
  91.6 55.6 %collective-permute-start.23 = (bf16[144,2304]{1,0:T(8,128)(2,1)}, bf16[144,2304]{1,0:T(8,128)(2,1)}, u32[]{:S(2)}, u32[]{:S(2)}) collective-permute-start(bf16[144,2304]{1,0:T(8,128)(2,1)} %get-tuple-element.232.refs_5_.refs_6_), channel_id=1, source_target_pairs={{0,4},{4,0},{8,12},{12,8},{1,5},{5,1},{9,13},{13,9},{2,6},{6,2},{1... | collective-permute-start | bytes 1990664 | tf_op jit(solution)/shard_map/ppermute | solution.py:32
  139.9 27.3 %collective-permute-start.31 = (bf16[144,1920]{1,0:T(8,128)(2,1)}, bf16[144,1920]{1,0:T(8,128)(2,1)}, u32[]{:S(2)}, u32[]{:S(2)}) collective-permute-start(bf16[144,1920]{1,0:T(8,128)(2,1)} %shard_map.218.refs_0_), channel_id=1, source_target_pairs={{0,8},{4,12},{8,0},{12,4},{1,9},{5,13},{9,1},{13,5},{2,10},{6,14},... | collective-permute-start | bytes 1658888 | tf_op jit(solution)/shard_map/ppermute | solution.py:32
  167.3 32.0 %collective-permute-start.32 = (bf16[144,1920]{1,0:T(8,128)(2,1)}, bf16[144,1920]{1,0:T(8,128)(2,1)}, u32[]{:S(2)}, u32[]{:S(2)}) collective-permute-start(bf16[144,1920]{1,0:T(8,128)(2,1)} %get-tuple-element.244.refs_5_.refs_6_), channel_id=1, source_target_pairs={{0,4},{4,0},{8,12},{12,8},{1,5},{5,1},{9,13},{13,9},{2,6},{6,2},{1... | collective-permute-start | bytes 1658888 | tf_op jit(solution)/shard_map/ppermute | solution.py:32
  169.4 29.9 %collective-permute-start.33 = (bf16[144,1920]{1,0:T(8,128)(2,1)}, bf16[144,1920]{1,0:T(8,128)(2,1)}, u32[]{:S(2)}, u32[]{:S(2)}) collective-permute-start(bf16[144,1920]{1,0:T(8,128)(2,1)} %get-tuple-element.245.refs_6_.refs_7_), channel_id=1, source_target_pairs={{0,4},{4,0},{8,12},{12,8},{1,5},{5,1},{9,13},{13,9},{2,6},{6,2},{1... | collective-permute-start | bytes 1658888 | tf_op jit(solution)/shard_map/ppermute | solution.py:32
  184.7 41.5 %collective-permute-start.43 = (bf16[144,2304]{1,0:T(8,128)(2,1)}, bf16[144,2304]{1,0:T(8,128)(2,1)}, u32[]{:S(2)}, u32[]{:S(2)}) collective-permute-start(bf16[144,2304]{1,0:T(8,128)(2,1)} %shard_map.225.refs_0_), channel_id=1, source_target_pairs={{0,8},{4,12},{8,0},{12,4},{1,9},{5,13},{9,1},{13,5},{2,10},{6,14},... | collective-permute-start | bytes 1990664 | tf_op jit(solution)/shard_map/ppermute | solution.py:32
  226.2 31.9 %collective-permute-start.44 = (bf16[144,2304]{1,0:T(8,128)(2,1)}, bf16[144,2304]{1,0:T(8,128)(2,1)}, u32[]{:S(2)}, u32[]{:S(2)}) collective-permute-start(bf16[144,2304]{1,0:T(8,128)(2,1)} %get-tuple-element.258.refs_4_.refs_5_), channel_id=1, source_target_pairs={{0,4},{4,0},{8,12},{12,8},{1,5},{5,1},{9,13},{13,9},{2,6},{6,2},{1... | collective-permute-start | bytes 1990664 | tf_op jit(solution)/shard_map/ppermute | solution.py:32
  226.6 31.5 %collective-permute-start.45 = (bf16[144,2304]{1,0:T(8,128)(2,1)}, bf16[144,2304]{1,0:T(8,128)(2,1)}, u32[]{:S(2)}, u32[]{:S(2)}) collective-permute-start(bf16[144,2304]{1,0:T(8,128)(2,1)} %get-tuple-element.259.refs_5_.refs_6_), channel_id=1, source_target_pairs={{0,4},{4,0},{8,12},{12,8},{1,5},{5,1},{9,13},{13,9},{2,6},{6,2},{1... | collective-permute-start | bytes 1990664 | tf_op jit(solution)/shard_map/ppermute | solution.py:32
  269.8 29.2 %collective-permute-start.46 = (bf16[128,1152]{1,0:T(8,128)(2,1)}, bf16[128,1152]{1,0:T(8,128)(2,1)}, u32[]{:S(2)}, u32[]{:S(2)}) collective-permute-start(bf16[128,1152]{1,0:T(8,128)(2,1)} %get-tuple-element.261), channel_id=1, source_target_pairs={{0,16},{16,0},{1,17},{17,1},{2,18},{18,2},{3,19},{19,3},{4,20},{20... | collective-permute-start | bytes 884744 | tf_op jit(solution)/shard_map/ppermute | solution.py:32
  320.4 419.3 %all-gather.7.cloned.1.call-start = ((), (), s32[]{:S(2)}) async-start(), calls=%async_computation.3 | async-start | bytes 11280384 | tf_op jit(solution)/shard_map/all_gather | solution.py:574
  469.2 379.0 %all-gather.5.cloned.1.call-start = ((), (), s32[]{:S(2)}) async-start(), calls=%async_computation.2 | async-start | bytes 22560768 | tf_op jit(solution)/shard_map/all_gather | solution.py:574
  476.0 65.3 %collective-permute-start.64 = (bf16[4,144,1152]{2,1,0:T(8,128)(2,1)}, bf16[4,144,1152]{2,1,0:T(8,128)(2,1)S(1)}, u32[]{:S(2)}, u32[]{:S(2)}) collective-permute-start(bf16[4,144,1152]{2,1,0:T(8,128)(2,1)} %copy-done.148), channel_id=1, source_target_pairs={{0,8},{4,12},{8,0},{12,4},{1,9},{5,13},{9,1},{13,5},{2,10},{6,14},... | collective-permute-start | bytes 3981320 | tf_op jit(solution)/shard_map/ppermute | solution.py:32
  500.4 28.6 %collective-permute-start.76 = (bf16[1,64,1920]{2,1,0:T(8,128)(2,1)S(1)}, bf16[1,64,1920]{2,1,0:T(8,128)(2,1)S(1)}, u32[]{:S(2)}, u32[]{:S(2)}) collective-permute-start(bf16[1,64,1920]{2,1,0:T(8,128)(2,1)S(1)} %get-tuple-element.331), channel_id=1, source_target_pairs={{0,2},{1,3},{2,0},{3,1},{4,6},{5,7},{6,4},{7,5},{8,10},{9,11},{10,... | collective-permute-start | bytes 737288 | tf_op jit(solution)/shard_map/ppermute | solution.py:32
  540.2 55.1 %collective-permute-start.79 = (bf16[4,144,1152]{2,1,0:T(8,128)(2,1)}, bf16[4,144,1152]{2,1,0:T(8,128)(2,1)}, u32[]{:S(2)}, u32[]{:S(2)}) collective-permute-start(bf16[4,144,1152]{2,1,0:T(8,128)(2,1)} %get-tuple-element.337), channel_id=1, source_target_pairs={{0,8},{4,12},{8,0},{12,4},{1,9},{5,13},{9,1},{13,5},{2,10},{6,14},... | collective-permute-start | bytes 3981320 | tf_op jit(solution)/shard_map/ppermute | solution.py:32
  560.1 35.2 %collective-permute-start.80 = (f32[32,1152]{1,0:T(8,128)S(1)}, f32[32,1152]{1,0:T(8,128)S(1)}, u32[]{:S(2)}, u32[]{:S(2)}) collective-permute-start(f32[32,1152]{1,0:T(8,128)S(1)} %get-tuple-element.338.refs_4_), channel_id=1, source_target_pairs={{0,2},{1,3},{2,0},{3,1},{4,6},{5,7},{6,4},{7,5},{8,10},{9,11},{10,... | collective-permute-start | bytes 442376 | tf_op jit(solution)/shard_map/ppermute | solution.py:32
  560.3 37.5 %collective-permute-start.78 = (bf16[2,144,1152]{2,1,0:T(8,128)(2,1)}, bf16[2,144,1152]{2,1,0:T(8,128)(2,1)S(1)}, u32[]{:S(2)}, u32[]{:S(2)}) collective-permute-start(bf16[2,144,1152]{2,1,0:T(8,128)(2,1)} %copy-done.149), channel_id=1, source_target_pairs={{0,1},{1,0},{2,3},{3,2},{4,5},{5,4},{6,7},{7,6},{8,9},{9,8},{10,11... | collective-permute-start | bytes 1990664 | tf_op jit(solution)/shard_map/ppermute | solution.py:32
  563.1 37.4 %collective-permute-start.88 = (bf16[256,1920]{1,0:T(8,128)(2,1)S(1)}, bf16[256,1920]{1,0:T(8,128)(2,1)S(1)}, u32[]{:S(2)}, u32[]{:S(2)}) collective-permute-start(bf16[256,1920]{1,0:T(8,128)(2,1)S(1)} %shard_map.258.mine), channel_id=1, source_target_pairs={{0,16},{16,0},{1,17},{17,1},{2,18},{18,2},{3,19},{19,3},{4,20},{20... | collective-permute-start | bytes 2949128 | tf_op jit(solution)/shard_map/ppermute | solution.py:32
  604.8 39.1 %collective-permute-start.93 = (bf16[8,144,1152]{2,1,0:T(8,128)(2,1)S(1)}, bf16[8,144,1152]{2,1,0:T(8,128)(2,1)}, u32[]{:S(2)}, u32[]{:S(2)}) collective-permute-start(bf16[8,144,1152]{2,1,0:T(8,128)(2,1)S(1)} %get-tuple-element.371), channel_id=1, source_target_pairs={{0,4},{4,0},{8,12},{12,8},{1,5},{5,1},{9,13},{13,9},{2,6},{6,2},{1... | collective-permute-start | bytes 7962632 | tf_op jit(solution)/shard_map/ppermute | solution.py:32
  607.2 31.1 %collective-permute-start.87 = (bf16[4,144,1152]{2,1,0:T(8,128)(2,1)S(1)}, bf16[4,144,1152]{2,1,0:T(8,128)(2,1)S(1)}, u32[]{:S(2)}, u32[]{:S(2)}) collective-permute-start(bf16[4,144,1152]{2,1,0:T(8,128)(2,1)S(1)} %copy-done.147), channel_id=1, source_target_pairs={{0,8},{4,12},{8,0},{12,4},{1,9},{5,13},{9,1},{13,5},{2,10},{6,14},... | collective-permute-start | bytes 3981320 | tf_op jit(solution)/shard_map/ppermute | solution.py:32
  607.6 30.8 %collective-permute-start.86 = (bf16[2,144,1152]{2,1,0:T(8,128)(2,1)}, bf16[2,144,1152]{2,1,0:T(8,128)(2,1)S(1)}, u32[]{:S(2)}, u32[]{:S(2)}) collective-permute-start(bf16[2,144,1152]{2,1,0:T(8,128)(2,1)} %get-tuple-element.348), channel_id=1, source_target_pairs={{0,1},{1,0},{2,3},{3,2},{4,5},{5,4},{6,7},{7,6},{8,9},{9,8},{10,11... | collective-permute-start | bytes 1990664 | tf_op jit(solution)/shard_map/ppermute | solution.py:32
  642.0 27.7 %collective-permute-start.91 = (bf16[2,144,1152]{2,1,0:T(8,128)(2,1)}, bf16[2,144,1152]{2,1,0:T(8,128)(2,1)}, u32[]{:S(2)}, u32[]{:S(2)}) collective-permute-start(bf16[2,144,1152]{2,1,0:T(8,128)(2,1)} %get-tuple-element.365), channel_id=1, source_target_pairs={{0,1},{1,0},{2,3},{3,2},{4,5},{5,4},{6,7},{7,6},{8,9},{9,8},{10,11... | collective-permute-start | bytes 1990664 | tf_op jit(solution)/shard_map/ppermute | solution.py:32
  650.9 35.4 %collective-permute-start.95 = (bf16[4,144,1152]{2,1,0:T(8,128)(2,1)}, bf16[4,144,1152]{2,1,0:T(8,128)(2,1)S(1)}, u32[]{:S(2)}, u32[]{:S(2)}) collective-permute-start(bf16[4,144,1152]{2,1,0:T(8,128)(2,1)} %get-tuple-element.378), channel_id=1, source_target_pairs={{0,8},{4,12},{8,0},{12,4},{1,9},{5,13},{9,1},{13,5},{2,10},{6,14},... | collective-permute-start | bytes 3981320 | tf_op jit(solution)/shard_map/ppermute | solution.py:32
  (257 other events, 3380.8 us)
Sparse Core Ops, SparseCore 0:
  320.5 121.6 reduce-scatter.1
  469.4 133.3 all-gather.6
  731.6 116.5 all-gather.4

commit v3 on v2

--- a/solution.py
+++ b/solution.py
@@ -594,28 +594,33 @@
         indices = (
             lambda i, m: (layer, i, 0),
             expand,
-            lambda i, m: (layer, i // 4, jnp.minimum(i % 4, 2)),
-            lambda i, m: (layer, i // 4, 0),
-        )
-        targets = [k for kind in kinds for k in ((0,), (1,), (2, 3))["ABC".index(kind)]]
-        earlier = [previous[k] for k in targets] if previous else []
+            lambda i, m: (0, i // 4, jnp.minimum(i % 4, 2)),
+            lambda i, m: (0, i // 4, 0),
+        )
+        blocks = (block, block, (LAYERS,) + block[1:], (LAYERS,) + block[1:])
+        targets = [k for kind in kinds[:3] for k in ((0,), (1,), (2, 3))["ABC".index(kind)]]
+        kept = [k for k in targets if previous and k in previous]
+        earlier = [previous[k] for k in kept]
         count, outs, given = len(earlier), len(targets), len(sums)
 
         def body(m, *refs):
             where = dict(zip(targets, refs[-1 - outs : -1]))
             last = pl.program_id(0) % 4 == 3
+            done = 0
             for kind, ref in zip(kinds, refs):
                 if kind != "C":
                     where["AB".index(kind)][0] = ref[0].astype(FLOAT)
                     continue
 
+                at, done = done, done + 1
+
                 @pl.when(last)
-                def _(ref=ref):
-                    where[3][0] = ref[0].astype(FLOAT)
+                def _(ref=ref, at=at):
+                    where[3][at] = ref[0].astype(FLOAT)
 
                 @pl.when(jnp.logical_not(last))
-                def _(ref=ref):
-                    where[2][0] = ref[0].astype(FLOAT)
+                def _(ref=ref, at=at):
+                    where[2][at] = ref[0].astype(FLOAT)
 
         *results, through = pl.pallas_call(
             body,
@@ -623,11 +628,11 @@
                 num_scalar_prefetch=1,
                 grid=(SHARES,),
                 in_specs=[source(one.slot) for one in sums] + [ANYWHERE] * (count + 1),
-                out_specs=[pl.BlockSpec(block, indices[k]) for k in targets] + [ANYWHERE],
+                out_specs=[pl.BlockSpec(blocks[k], indices[k]) for k in targets] + [ANYWHERE],
             ),
             out_shape=[jax.ShapeDtypeStruct(shapes[k], FLOAT) for k in targets]
             + [jax.ShapeDtypeStruct(through.shape, through.dtype)],
-            input_output_aliases={1 + given + k: k for k in range(count)}
+            input_output_aliases={1 + given + j: targets.index(k) for j, k in enumerate(kept)}
             | {1 + given + count: outs},
             cost_estimate=SMALL,
             compiler_params=params(),
@@ -790,32 +795,17 @@
     return value
 
 
-def turned(values):
-    return jnp.transpose(values.reshape(-1, values.shape[2]))
-
-
-def own_half(values):
-    half = values.shape[-1] // 2
-    return jnp.where(lax.axis_index("batch") == 0, values[..., :half], values[..., half:])
-
-
-def spread(values):
-    items = values.shape[0] // 2
-    other = swap(values)
-    return jnp.concatenate([other[items:], other[:items]], axis=0)
-
-
-def shrink_sum(active, outer_low):
-    act = turned(active)[None]
-    delta = outer_low.reshape(1, -1, D)
-    return GradSum(act, delta, lambda s: (0, s, 0), lambda s: (0, 0, 0), STAGES)
-
-
-def expand_sum(second, inner_low):
-    act = turned(second)[None]
-    delta = inner_low.reshape(1, -1, inner_low.shape[-1])
+def shrink_sum(act, outer_low):
+    return GradSum(act[None], outer_low[None], lambda s: (0, s, 0), lambda s: (0, 0, 0), STAGES)
+
+
+def expand_sum(act, inner_low):
     return CrossGradSum(
-        act, delta, lambda s: (0, s // 8 * 4 + s % 4, 0), lambda s: (0, 0, s // 4 % 2), STAGES
+        act[None],
+        inner_low[None],
+        lambda s: (0, s // 8 * 4 + s % 4, 0),
+        lambda s: (0, 0, s // 4 % 2),
+        STAGES,
     )
 
 
@@ -873,8 +863,7 @@
     )(places, own, other, branch, branch_other)
 
 
-def mixer_sum(mixed, delta_project, attend, branch, branch_other, places, width, size):
-    act = jnp.stack([turned(own_half(mixed)[None]), turned(attend[None])])
+def mixer_sum(act, delta_project, branch, branch_other, places, width, size):
     delta, logits = mixer_delta(
         delta_project, swap(delta_project), branch, branch_other, places, width, size
     )
@@ -1170,6 +1159,45 @@
             pltpu.SemaphoreType.DMA((6,)),
         ],
     )
+
+
+def turn_call(mixed, mixed_other, attend, second, second_other, active, places, through):
+    tokens = attend.shape[0]
+    width = attend.shape[1]
+    padded = padded_width(width)
+    inner = active.shape[1]
+    half = mixed.shape[0]
+
+    def turn(value):
+        return jnp.transpose(value.astype(FLOAT)).astype(BFLOAT)
+
+    def body(places, one, two, three, four, five, six, _, mixer, wide, long, __):
+        first = places[0] == 0
+        for ref, at in ((one, 0), (two, half)):
+            value = turn(ref[...])
+            mixer[0, :, at : at + half] = jnp.where(first, value[:width], value[width:])
+        blank = jnp.zeros((tokens, padded - width), FLOAT)
+        value = jnp.concatenate([three[...].astype(FLOAT), blank], axis=1)
+        mixer[1] = jnp.transpose(value)[:width].astype(BFLOAT)
+        wide[:, :half] = turn(four[...])
+        wide[:, half:] = turn(five[...])
+        for at in range(0, inner, 256):
+            long[at : at + 256] = turn(six[:, at : at + 256])
+
+    return pl.pallas_call(
+        body,
+        in_specs=[pl.BlockSpec(memory_space=pltpu.SMEM)] + [WHOLE] * 6 + [ANYWHERE],
+        out_specs=[WHOLE] * 3 + [ANYWHERE],
+        out_shape=[
+            jax.ShapeDtypeStruct((2, width, tokens), BFLOAT),
+            jax.ShapeDtypeStruct((D, tokens), BFLOAT),
+            jax.ShapeDtypeStruct((inner, tokens), BFLOAT),
+            jax.ShapeDtypeStruct(through.shape, through.dtype),
+        ],
+        input_output_aliases={7: 3},
+        cost_estimate=SMALL,
+        compiler_params=params(),
+    )(places, mixed, mixed_other, attend, second, second_other, active, through)
 
 
 def feed_back_call(own, other, inner_value, expand, shrink, layer, places):
@@ -1517,12 +1545,16 @@
         )
         if layer + 1 < LAYERS:
             self.fetch("expand", layer + 1, 0, [own])
+        received = swap(send)
+        mixer_act, second_act, active_act, own = turn_call(
+            mixed, mixed_other, attend, second, second_other, active, places, own
+        )
         saved = dict(
-            tokens=tokens, hidden=hidden, sides=sides, convolved=convolved, mixed=mixed,
-            mixed_other=mixed_other, parts=parts, attend=attend, branch=branch, middle=middle,
-            second=second, second_other=second_other, inner=inner, active=active,
-        )
-        return middle, own, swap(send), saved
+            tokens=tokens, hidden=hidden, sides=sides, convolved=convolved, parts=parts,
+            branch=branch, middle=middle, inner=inner, mixer_act=mixer_act,
+            second_act=second_act, active_act=active_act,
+        )
+        return middle, own, received, saved
 
     def backward(self, layer, delta, outer_low, outer_other, saved, tick):
         places, axis = self.places[layer % 2], self.axis(layer)
@@ -1533,16 +1565,13 @@
             layer, places,
         )
         received = swap(send)
-        shrink_pipe = shrink_sum(saved["active"][None], both(outer_low, outer_other))
+        shrink_pipe = shrink_sum(saved["active_act"], both(outer_low, outer_other))
         own = tick("P1", {"A": shrink_pipe}, own)
         delta_middle, branch_low, mod_b = middle_back_call(
             delta, own, received, saved["middle"], saved["branch"], saved["outer"], mod
         )
         branch_other = swap(branch_low)
-        paired = lambda v: v.reshape(2, -1, v.shape[-1])
-        expand_pipe = expand_sum(
-            paired(both(saved["second"], saved["second_other"])), paired(inner_low)
-        )
+        expand_pipe = expand_sum(saved["second_act"], inner_low)
         branch_low = tick("P2", {"B": expand_pipe}, branch_low)
         blocks = attend_back_call(
             branch_low, branch_other, self.args["proj"], layer, places, self.cells, self.width
@@ -1558,15 +1587,13 @@
             sent, self.qkv[layer], places, self.cells, self.width
         )
         received = swap(send)
-        mixed = both(saved["mixed"], saved["mixed_other"])
-
         def mixer(after):
             (value,) = passed_by([delta_project], after)
+            act = saved["mixer_act"]
             pipe, logits = mixer_sum(
-                mixed, value, saved["attend"], branch_low, branch_other, places,
-                self.width, self.size,
+                act, value, branch_low, branch_other, places, self.width, self.size
             )
-            return pipe, dot(logits, own_half(mixed), ((0,), (0,)))[: 2 * self.heads]
+            return pipe, dot(logits, act[0], ((0,), (1,)))[: 2 * self.heads]
 
         if not layer:
             mixer_pipe, grad_decay = mixer([])
@@ -1798,7 +1825,6 @@
     "tC0tS0gL0",
     "fAB1",
     "mS0",
-    "fC1",
     "fABC0",
 )
 
@@ -1972,8 +1998,11 @@
             if names[0] == "f":
                 kinds = names[1:-1]
                 layer = int(names[-1])
+                sums = [moving[kind + names[-1]] for kind in kinds]
+                if kinds[-1] == "C":
+                    kinds, sums = kinds + "C", sums + [moving["C1"]]
                 made, through = Gathered.finish(
-                    [moving[kind + names[-1]] for kind in kinds], kinds,
+                    sums, kinds,
                     None if layer else finished, layer, shapes, through,
                 )
                 finished = (finished or {}) | made

time: 900 us -> 831 us (0.923)
  local copies, waits for them, and re-layouts: 87.6 us -> 33.1 us
  other arithmetic: 19.8 us -> 9.3 us
  Pallas kernels: 231 us -> 222 us
    unnamed x350 -> x272, local copies, waits for them, and re-layouts: 56.1 us -> 24 us
    pallas_call x6 -> x0, local copies, waits for them, and re-layouts: 11.2 us -> none  [call(): pl.pallas_call(whole, in_specs=[pl.BlockSpec(memory_space=pltpu.SMEM)] *...]
    pallas_call x3 -> x2, Pallas kernels: 46.3 us -> 39.4 us  [finish(): pl.pallas_call(body, grid_spec=pltpu.PrefetchScalarGridSpec(num_scalar_pr...]
  transfers between devices with their start and end apart: 109 -> 109, of which waited for: 47 -> 51; matrix products, arithmetic and copies ran while one was open for 7% -> 4% of each run, Pallas kernels for 21% -> 23%
where the time goes in v3:
time: 831 us; the launch traced here: 824 us
  waiting for transfers between devices  385 us (46%)
  Pallas kernels  222 us (27%)
  starting transfers between devices  149 us (18%)
  local copies, waits for them, and re-layouts  33.1 us (4%)
  between operations  16.4 us (2%)
  other arithmetic  9.3 us (1%)
  matrix products  9.26 us (1%)
    ppermute x88, waiting for transfers between devices, swap(): return lax.ppermute(value, axis, [(i, i ^ bit) for i in range(count)])  233 us
    ppermute x88, starting transfers between devices, swap(): return lax.ppermute(value, axis, [(i, i ^ bit) for i in range(count)])  117 us
    all_gather x2, waiting for transfers between devices, collect(): whole = lax.all_gather(shares, GRID_AXES)  84.1 us
    pallas_call x25, Pallas kernels, call(): pl.pallas_call(whole, in_specs=[pl.BlockSpec(memory_space=pltpu.SMEM)] *...  61.4 us
    pallas_call x2, Pallas kernels, finish(): pl.pallas_call(body, grid_spec=pltpu.PrefetchScalarGridSpec(num_scalar_pr...  39.4 us
    pallas_call x8, Pallas kernels, call(): pl.pallas_call(body, grid_spec=pltpu.PrefetchScalarGridSpec(num_scalar_pr...  38 us
    ppermute x4, waiting for transfers between devices, halo_edges(): right = lax.ppermute(to_left, 'col', [(i + 1, i) for i in range(cols - 1)])  30.9 us
    ppermute x4, waiting for transfers between devices, halo_edges(): lax.ppermute(first_row, 'row', [(i + 1, i) for i in range(rows - 1)])  30.8 us
  transfers between devices with their start and end apart: 109, of which 51 were waited for; matrix products, arithmetic and copies ran while one was open for 4% of the time, Pallas kernels for 23%

profile of v3, /device:TPU:0, one launch (start us, length us, event | category | flops | bytes accessed | tf_op | source)
XLA Modules:
  0.0 823.7 jit_solution(8272221871096351663)
XLA Ops:
  60.8 7.9 collective-permute-done.7.refs_2_.two
  83.8 10.7 %collective-permute-done.13.refs_3_ = bf16[1,64,1920]{2,1,0:T(8,128)(2,1)S(1)} collective-permute-done((bf16[1,64,1920]{2,1,0:T(8,128)(2,1)S(1)}, bf16[1,64,1920]{2,1,0:T(8,128)(2,1)S(1)}, u32[]{:S(2)}, u32[]{:S(2)}) %collective-permute-start.13) | collective-permute-done | bytes 245792 | tf_op jit(solution)/shard_map/ppermute | solution.py:32
  112.0 11.0 %collective-permute-done.18.refs_2_ = bf16[128,1152]{1,0:T(8,128)(2,1)S(1)} collective-permute-done((bf16[128,1152]{1,0:T(8,128)(2,1)S(1)}, bf16[128,1152]{1,0:T(8,128)(2,1)S(1)}, u32[]{:S(2)}, u32[]{:S(2)}) %collective-permute-start.18) | collective-permute-done | bytes 294944 | tf_op jit(solution)/shard_map/ppermute | solution.py:32
  210.2 8.0 collective-permute-done.40.refs_2_
  220.8 7.7 collective-permute-done.41.refs_2_.five
  236.2 8.4 %shard_map.231 = (f32[128,1152]{1,0:T(8,128)S(1)}, bf16[128,1152]{1,0:T(8,128)(2,1)S(1)}, bf16[256,2304]{1,0:T(8,128)(2,1)S(1)}) custom-call(s32[3]{0:T(128)S(1)} %pad_add_fusion.2.refs_0_.places, bf16[128,1152]{1,0:T(8,128)(2,1)S(1)} %fusion.12.refs_1_, bf16[128,1152]{1,0:T(8,128)(2,1)S(1)} %collective-permute-done.47.refs_2_, ...), custom_call_target="tpu_custom_call" | custom-call | flops 1 | bytes 1 | tf_op jit(solution)/shard_map/pallas_call | solution.py:898
  247.7 8.2 shard_map.232
  264.4 8.5 %shard_map.234 = (bf16[16,2,144,1152]{3,2,1,0:T(8,128)(2,1)}, bf16[128,1152]{1,0:T(8,128)(2,1)S(1)}) custom-call(bf16[1,1152,256]{2,1,0:T(8,128)(2,1)S(1)} %bitcast.114, bf16[1,256,2304]{2,1,0:T(8,128)(2,1)S(1)} %bitcast.111, bf16[16,2,144,1152]{3,2,1,0:T(8,128)(2,1)} %get-tuple-element.280.refs_0_, ...), custom_call_target="tpu_custom_call", output_to_operand_aliasing={{0}: (2, {}), {1}: (3, {})} | custom-call | flops 1 | bytes 1 | tf_op jit(solution)/shard_map/pallas_call | solution.py:665
  308.4 8.3 %collective-permute-done.56.refs_1_ = bf16[128,1152]{1,0:T(8,128)(2,1)S(1)} collective-permute-done((bf16[128,1152]{1,0:T(8,128)(2,1)S(1)}, bf16[128,1152]{1,0:T(8,128)(2,1)S(1)}, u32[]{:S(2)}, u32[]{:S(2)}) %collective-permute-start.56) | collective-permute-done | bytes 294944 | tf_op jit(solution)/shard_map/ppermute | solution.py:32
  354.4 8.7 %shard_map.244 = (f32[128,1152]{1,0:T(8,128)S(1)}, bf16[128,1152]{1,0:T(8,128)(2,1)S(1)}, bf16[256,2304]{1,0:T(8,128)(2,1)S(1)}) custom-call(s32[3]{0:T(128)S(1)} %pad_add_fusion.refs_0_.places, bf16[128,1152]{1,0:T(8,128)(2,1)} %get-tuple-element.309.refs_1_, bf16[128,1152]{1,0:T(8,128)(2,1)} %collective-permute-done.63.refs_2_, ...), custom_call_target="tpu_custom_call" | custom-call | flops 1 | bytes 1 | tf_op jit(solution)/shard_map/pallas_call | solution.py:898
  377.5 8.0 collective-permute-done.66.refs_2_
  449.6 11.8 %collective-permute-done.67.refs_1_ = f32[32,1152]{1,0:T(8,128)S(1)} collective-permute-done((f32[32,1152]{1,0:T(8,128)S(1)}, f32[32,1152]{1,0:T(8,128)S(1)}, u32[]{:S(2)}, u32[]{:S(2)}) %collective-permute-start.67) | collective-permute-done | bytes 147488 | tf_op jit(solution)/shard_map/ppermute | solution.py:32
  462.8 11.5 %collective-permute-done.76.refs_3_ = bf16[1,64,1920]{2,1,0:T(8,128)(2,1)S(1)} collective-permute-done((bf16[1,64,1920]{2,1,0:T(8,128)(2,1)S(1)}, bf16[1,64,1920]{2,1,0:T(8,128)(2,1)S(1)}, u32[]{:S(2)}, u32[]{:S(2)}) %collective-permute-start.76) | collective-permute-done | bytes 245792 | tf_op jit(solution)/shard_map/ppermute | solution.py:32
  485.2 14.8 %collective-permute-done.74.refs_3_ = f32[32,1152]{1,0:T(8,128)S(1)} collective-permute-done((f32[32,1152]{1,0:T(8,128)S(1)}, f32[32,1152]{1,0:T(8,128)S(1)}, u32[]{:S(2)}, u32[]{:S(2)}) %collective-permute-start.74) | collective-permute-done | bytes 147488 | tf_op jit(solution)/shard_map/ppermute | solution.py:32
  508.2 28.1 %collective-permute-done.83.refs_6_ = bf16[2,8,1152]{2,1,0:T(8,128)(2,1)S(1)} collective-permute-done((bf16[2,8,1152]{2,1,0:T(8,128)(2,1)S(1)}, bf16[2,8,1152]{2,1,0:T(8,128)(2,1)S(1)}, u32[]{:S(2)}, u32[]{:S(2)}) %collective-permute-start.83) | collective-permute-done | bytes 36896 | tf_op jit(solution)/shard_map/ppermute | solution.py:930
  558.4 19.8 %collective-permute-done.89.refs_8_ = bf16[2,10,1152]{2,1,0:T(8,128)(2,1)S(1)} collective-permute-done((bf16[2,10,1152]{2,1,0:T(8,128)(2,1)S(1)}, bf16[2,10,1152]{2,1,0:T(8,128)(2,1)S(1)}, u32[]{:S(2)}, u32[]{:S(2)}) %collective-permute-start.89) | collective-permute-done | bytes 46112 | tf_op jit(solution)/shard_map/ppermute | solution.py:934
  601.8 11.1 %collective-permute-done.90.refs_1_ = bf16[1,144,1152]{2,1,0:T(8,128)(2,1)} collective-permute-done((bf16[1,144,1152]{2,1,0:T(8,128)(2,1)}, bf16[1,144,1152]{2,1,0:T(8,128)(2,1)}, u32[]{:S(2)}, u32[]{:S(2)}) %collective-permute-start.90) | collective-permute-done | bytes 331808 | tf_op jit(solution)/shard_map/ppermute | solution.py:32
  616.3 9.2 %shard_map.269 = (f32[2,576,6912]{2,1,0:T(8,128)}, bf16[128,1152]{1,0:T(8,128)(2,1)}) custom-call(f32[576,4]{1,0:T(8,128)S(1)} %copy-done.26, f32[4,6912]{1,0:T(4,128)S(1)} %get-tuple-element.493.values, bf16[128,1152]{1,0:T(8,128)(2,1)} %get-tuple-element.394.refs_0_), custom_call_target="tpu_custom_call", output_to_operand_aliasing={{1}: (2, {})} | custom-call | flops 1 | bytes 1 | tf_op jit(solution)/shard_map/pallas_call | solution.py:1789
  633.2 16.0 %collective-permute-done.99.refs_3_ = f32[32,1152]{1,0:T(8,128)S(1)} collective-permute-done((f32[32,1152]{1,0:T(8,128)S(1)}, f32[32,1152]{1,0:T(8,128)S(1)}, u32[]{:S(2)}, u32[]{:S(2)}) %collective-permute-start.99) | collective-permute-done | bytes 147488 | tf_op jit(solution)/shard_map/ppermute | solution.py:32
  652.9 20.8 %collective-permute-done.102.refs_3_ = f32[32,1152]{1,0:T(8,128)S(1)} collective-permute-done((f32[32,1152]{1,0:T(8,128)S(1)}, f32[32,1152]{1,0:T(8,128)S(1)}, u32[]{:S(2)}, u32[]{:S(2)}) %collective-permute-start.102) | collective-permute-done | bytes 147488 | tf_op jit(solution)/shard_map/ppermute | solution.py:32
  684.1 15.3 %shard_map.274 = (f32[2,2304,1152]{2,1,0:T(8,128)}, f32[2,576,4608]{2,1,0:T(8,128)}, bf16[128,1152]{1,0:T(8,128)(2,1)}) custom-call(s32[1]{0:T(128)} %bitcast.1.m, bf16[16,2,144,1152]{3,2,1,0:T(8,128)(2,1)} %bitcast.119, bf16[16,2,144,1152]{3,2,1,0:T(8,128)(2,1)} %bitcast.120, ...), custom_call_target="tpu_custom_call", output_to_operand_aliasing={{2}: (3, {})} | custom-call | flops 1 | bytes 1 | tf_op jit(solution)/shard_map/pallas_call | solution.py:625
  699.3 9.2 %shard_map.275 = (f32[2,576,6912]{2,1,0:T(8,128)}, bf16[128,1152]{1,0:T(8,128)(2,1)}) custom-call(f32[576,4]{1,0:T(8,128)S(1)} %copy-done.26, f32[4,6912]{1,0:T(4,128)S(1)} %get-tuple-element.491.values, f32[2,576,6912]{2,1,0:T(8,128)} %get-tuple-element.412.refs_0_, ...), custom_call_target="tpu_custom_call", output_to_operand_aliasing={{0}: (2, {}), {1}: (3, {})} | custom-call | flops 1 | bytes 1 | tf_op jit(solution)/shard_map/pallas_call | solution.py:1789
  708.5 84.1 %all-gather.5.cloned.1.call-done = bf16[64,144,1152]{2,1,0:T(8,128)(2,1)} async-done(((bf16[4,144,1152]{2,1,0:T(8,128)(2,1)}), bf16[64,144,1152]{2,1,0:T(8,128)(2,1)}) %all-gather.5.cloned.1.call-update) | async-done | bytes 21233680 | tf_op jit(solution)/shard_map/all_gather | solution.py:574
  792.6 24.1 %shard_map.276 = (f32[2,2304,1152]{2,1,0:T(8,128)}, f32[2,576,4608]{2,1,0:T(8,128)}, f32[2,576,3456]{2,1,0:T(8,128)}, f32[2,576,1152]{2,1,0:T(8,128)}, bf16[128,1152]{1,0:T(8,128)(2,1)}) custom-call(s32[1]{0:T(128)} %bitcast.1.m, bf16[16,4,144,1152]{3,2,1,0:T(8,128)(2,1)} %bitcast.115, ...), custom_call_target="tpu_custom_call", output_to_operand_aliasing={{0}: (5, {}), {1}: (6, {}), {4}: (7, {})} | custom-call | flops 1 | bytes 1 | tf_op jit(solution)/shard_map/pallas_call | solution.py:625
  (621 shorter events, 436.2 us)
Async XLA Ops:
  7.2 402.1 %reduce-scatter.2.cloned.1.call-start = ((), (), s32[]{:S(2)}) async-start(), calls=%async_computation.1 | async-start | bytes 11280384 | tf_op jit(solution)/shard_map/reduce_scatter | solution.py:686
  7.2 25.9 %collective-permute-start.1 = (bf16[2,3456]{1,0:T(2,128)(2,1)}, bf16[2,3456]{1,0:T(2,128)(2,1)S(1)}, u32[]{:S(2)}, u32[]{:S(2)}) collective-permute-start(bf16[2,3456]{1,0:T(2,128)(2,1)} %param.15), channel_id=1, source_target_pairs={{0,16},{16,0},{1,17},{17,1},{2,18},{18,2},{3,19},{19,3},{4,20},{20... | collective-permute-start | bytes 41480 | tf_op jit(solution)/shard_map/ppermute | solution.py:32
  82.3 48.3 %collective-permute-start.22 = (bf16[144,2304]{1,0:T(8,128)(2,1)S(1)}, bf16[144,2304]{1,0:T(8,128)(2,1)}, u32[]{:S(2)}, u32[]{:S(2)}) collective-permute-start(bf16[144,2304]{1,0:T(8,128)(2,1)S(1)} %get-tuple-element.237.refs_4_.refs_5_), channel_id=1, source_target_pairs={{0,4},{4,0},{8,12},{12,8},{1,5},{5,1},{9,13},{13,9},{2,6},{6,2},{1... | collective-permute-start | bytes 1990664 | tf_op jit(solution)/shard_map/ppermute | solution.py:32
  82.3 48.3 %collective-permute-start.23 = (bf16[144,2304]{1,0:T(8,128)(2,1)}, bf16[144,2304]{1,0:T(8,128)(2,1)}, u32[]{:S(2)}, u32[]{:S(2)}) collective-permute-start(bf16[144,2304]{1,0:T(8,128)(2,1)} %get-tuple-element.238.refs_5_.refs_6_), channel_id=1, source_target_pairs={{0,4},{4,0},{8,12},{12,8},{1,5},{5,1},{9,13},{13,9},{2,6},{6,2},{1... | collective-permute-start | bytes 1990664 | tf_op jit(solution)/shard_map/ppermute | solution.py:32
  150.2 28.9 %collective-permute-start.32 = (bf16[144,1920]{1,0:T(8,128)(2,1)}, bf16[144,1920]{1,0:T(8,128)(2,1)S(1)}, u32[]{:S(2)}, u32[]{:S(2)}) collective-permute-start(bf16[144,1920]{1,0:T(8,128)(2,1)} %get-tuple-element.252.refs_5_.refs_6_), channel_id=1, source_target_pairs={{0,4},{4,0},{8,12},{12,8},{1,5},{5,1},{9,13},{13,9},{2,6},{6,2},{1... | collective-permute-start | bytes 1658888 | tf_op jit(solution)/shard_map/ppermute | solution.py:32
  153.6 25.5 %collective-permute-start.33 = (bf16[144,1920]{1,0:T(8,128)(2,1)}, bf16[144,1920]{1,0:T(8,128)(2,1)S(1)}, u32[]{:S(2)}, u32[]{:S(2)}) collective-permute-start(bf16[144,1920]{1,0:T(8,128)(2,1)} %get-tuple-element.253.refs_6_.refs_7_), channel_id=1, source_target_pairs={{0,4},{4,0},{8,12},{12,8},{1,5},{5,1},{9,13},{13,9},{2,6},{6,2},{1... | collective-permute-start | bytes 1658888 | tf_op jit(solution)/shard_map/ppermute | solution.py:32
  168.6 34.7 %collective-permute-start.43 = (bf16[144,2304]{1,0:T(8,128)(2,1)S(1)}, bf16[144,2304]{1,0:T(8,128)(2,1)S(1)}, u32[]{:S(2)}, u32[]{:S(2)}) collective-permute-start(bf16[144,2304]{1,0:T(8,128)(2,1)S(1)} %shard_map.226.refs_0_), channel_id=1, source_target_pairs={{0,8},{4,12},{8,0},{12,4},{1,9},{5,13},{9,1},{13,5},{2,10},{6,14},... | collective-permute-start | bytes 1990664 | tf_op jit(solution)/shard_map/ppermute | solution.py:32
  203.3 25.3 %collective-permute-start.44 = (bf16[144,2304]{1,0:T(8,128)(2,1)S(1)}, bf16[144,2304]{1,0:T(8,128)(2,1)S(1)}, u32[]{:S(2)}, u32[]{:S(2)}) collective-permute-start(bf16[144,2304]{1,0:T(8,128)(2,1)S(1)} %get-tuple-element.267.refs_4_.refs_5_), channel_id=1, source_target_pairs={{0,4},{4,0},{8,12},{12,8},{1,5},{5,1},{9,13},{13,9},{2,6},{6,2},{1... | collective-permute-start | bytes 1990664 | tf_op jit(solution)/shard_map/ppermute | solution.py:32
  273.6 410.5 %all-gather.7.cloned.1.call-start = ((), (), s32[]{:S(2)}) async-start(), calls=%async_computation.3 | async-start | bytes 11280384 | tf_op jit(solution)/shard_map/all_gather | solution.py:574
  412.3 380.3 %all-gather.5.cloned.1.call-start = ((), (), s32[]{:S(2)}) async-start(), calls=%async_computation.2 | async-start | bytes 22560768 | tf_op jit(solution)/shard_map/all_gather | solution.py:574
  419.9 65.4 %collective-permute-start.64 = (bf16[4,144,1152]{2,1,0:T(8,128)(2,1)}, bf16[4,144,1152]{2,1,0:T(8,128)(2,1)S(1)}, u32[]{:S(2)}, u32[]{:S(2)}) collective-permute-start(bf16[4,144,1152]{2,1,0:T(8,128)(2,1)} %copy-done.122), channel_id=1, source_target_pairs={{0,8},{4,12},{8,0},{12,4},{1,9},{5,13},{9,1},{13,5},{2,10},{6,14},... | collective-permute-start | bytes 3981320 | tf_op jit(solution)/shard_map/ppermute | solution.py:32
  446.3 27.9 %collective-permute-start.76 = (bf16[1,64,1920]{2,1,0:T(8,128)(2,1)S(1)}, bf16[1,64,1920]{2,1,0:T(8,128)(2,1)S(1)}, u32[]{:S(2)}, u32[]{:S(2)}) collective-permute-start(bf16[1,64,1920]{2,1,0:T(8,128)(2,1)S(1)} %get-tuple-element.344), channel_id=1, source_target_pairs={{0,2},{1,3},{2,0},{3,1},{4,6},{5,7},{6,4},{7,5},{8,10},{9,11},{10,... | collective-permute-start | bytes 737288 | tf_op jit(solution)/shard_map/ppermute | solution.py:32
  448.2 26.0 %collective-permute-start.77 = (bf16[1,64,1920]{2,1,0:T(8,128)(2,1)S(1)}, bf16[1,64,1920]{2,1,0:T(8,128)(2,1)S(1)}, u32[]{:S(2)}, u32[]{:S(2)}) collective-permute-start(bf16[1,64,1920]{2,1,0:T(8,128)(2,1)S(1)} %get-tuple-element.345), channel_id=1, source_target_pairs={{0,3},{1,2},{2,1},{3,0},{4,7},{5,6},{6,5},{7,4},{8,11},{9,10},{10,... | collective-permute-start | bytes 737288 | tf_op jit(solution)/shard_map/ppermute | solution.py:32
  485.2 54.9 %collective-permute-start.79 = (bf16[4,144,1152]{2,1,0:T(8,128)(2,1)S(1)}, bf16[4,144,1152]{2,1,0:T(8,128)(2,1)S(1)}, u32[]{:S(2)}, u32[]{:S(2)}) collective-permute-start(bf16[4,144,1152]{2,1,0:T(8,128)(2,1)S(1)} %copy-done.121), channel_id=1, source_target_pairs={{0,8},{4,12},{8,0},{12,4},{1,9},{5,13},{9,1},{13,5},{2,10},{6,14},... | collective-permute-start | bytes 3981320 | tf_op jit(solution)/shard_map/ppermute | solution.py:32
  502.1 38.1 %collective-permute-start.80 = (f32[32,1152]{1,0:T(8,128)S(1)}, f32[32,1152]{1,0:T(8,128)S(1)}, u32[]{:S(2)}, u32[]{:S(2)}) collective-permute-start(f32[32,1152]{1,0:T(8,128)S(1)} %get-tuple-element.351.refs_4_), channel_id=1, source_target_pairs={{0,2},{1,3},{2,0},{3,1},{4,6},{5,7},{6,4},{7,5},{8,10},{9,11},{10,... | collective-permute-start | bytes 442376 | tf_op jit(solution)/shard_map/ppermute | solution.py:32
  502.2 40.9 %collective-permute-start.78 = (bf16[2,144,1152]{2,1,0:T(8,128)(2,1)S(1)}, bf16[2,144,1152]{2,1,0:T(8,128)(2,1)S(1)}, u32[]{:S(2)}, u32[]{:S(2)}) collective-permute-start(bf16[2,144,1152]{2,1,0:T(8,128)(2,1)S(1)} %get-tuple-element.348), channel_id=1, source_target_pairs={{0,1},{1,0},{2,3},{3,2},{4,5},{5,4},{6,7},{7,6},{8,9},{9,8},{10,11... | collective-permute-start | bytes 1990664 | tf_op jit(solution)/shard_map/ppermute | solution.py:32
  505.2 39.8 %collective-permute-start.88 = (bf16[256,1920]{1,0:T(8,128)(2,1)S(1)}, bf16[256,1920]{1,0:T(8,128)(2,1)S(1)}, u32[]{:S(2)}, u32[]{:S(2)}) collective-permute-start(bf16[256,1920]{1,0:T(8,128)(2,1)S(1)} %shard_map.260.mine), channel_id=1, source_target_pairs={{0,16},{16,0},{1,17},{17,1},{2,18},{18,2},{3,19},{19,3},{4,20},{20... | collective-permute-start | bytes 2949128 | tf_op jit(solution)/shard_map/ppermute | solution.py:32
  506.9 29.4 %collective-permute-start.83 = (bf16[2,8,1152]{2,1,0:T(8,128)(2,1)S(1)}, bf16[2,8,1152]{2,1,0:T(8,128)(2,1)S(1)}, u32[]{:S(2)}, u32[]{:S(2)}) collective-permute-start(bf16[2,8,1152]{2,1,0:T(8,128)(2,1)S(1)} %get-tuple-element.357), channel_id=1, source_target_pairs={{4,0},{8,4},{12,8},{5,1},{9,5},{13,9},{6,2},{10,6},{14,10},{7,3},{... | collective-permute-start | bytes 110600 | tf_op jit(solution)/shard_map/ppermute | solution.py:930
  549.4 38.1 %collective-permute-start.93 = (bf16[8,144,1152]{2,1,0:T(8,128)(2,1)S(1)}, bf16[8,144,1152]{2,1,0:T(8,128)(2,1)}, u32[]{:S(2)}, u32[]{:S(2)}) collective-permute-start(bf16[8,144,1152]{2,1,0:T(8,128)(2,1)S(1)} %get-tuple-element.384), channel_id=1, source_target_pairs={{0,4},{4,0},{8,12},{12,8},{1,5},{5,1},{9,13},{13,9},{2,6},{6,2},{1... | collective-permute-start | bytes 7962632 | tf_op jit(solution)/shard_map/ppermute | solution.py:32
  551.4 31.4 %collective-permute-start.87 = (bf16[4,144,1152]{2,1,0:T(8,128)(2,1)}, bf16[4,144,1152]{2,1,0:T(8,128)(2,1)}, u32[]{:S(2)}, u32[]{:S(2)}) collective-permute-start(bf16[4,144,1152]{2,1,0:T(8,128)(2,1)} %get-tuple-element.363), channel_id=1, source_target_pairs={{0,8},{4,12},{8,0},{12,4},{1,9},{5,13},{9,1},{13,5},{2,10},{6,14},... | collective-permute-start | bytes 3981320 | tf_op jit(solution)/shard_map/ppermute | solution.py:32
  551.9 30.9 %collective-permute-start.86 = (bf16[2,144,1152]{2,1,0:T(8,128)(2,1)S(1)}, bf16[2,144,1152]{2,1,0:T(8,128)(2,1)S(1)}, u32[]{:S(2)}, u32[]{:S(2)}) collective-permute-start(bf16[2,144,1152]{2,1,0:T(8,128)(2,1)S(1)} %get-tuple-element.361), channel_id=1, source_target_pairs={{0,1},{1,0},{2,3},{3,2},{4,5},{5,4},{6,7},{7,6},{8,9},{9,8},{10,11... | collective-permute-start | bytes 1990664 | tf_op jit(solution)/shard_map/ppermute | solution.py:32
  554.3 26.9 %collective-permute-start.85 = (bf16[1,144,1152]{2,1,0:T(8,128)(2,1)S(1)}, bf16[1,144,1152]{2,1,0:T(8,128)(2,1)S(1)}, u32[]{:S(2)}, u32[]{:S(2)}) collective-permute-start(bf16[1,144,1152]{2,1,0:T(8,128)(2,1)S(1)} %get-tuple-element.359), channel_id=1, source_target_pairs={{0,2},{1,3},{2,0},{3,1},{4,6},{5,7},{6,4},{7,5},{8,10},{9,11},{10,... | collective-permute-start | bytes 995336 | tf_op jit(solution)/shard_map/ppermute | solution.py:32
  585.4 27.5 %collective-permute-start.91 = (bf16[2,144,1152]{2,1,0:T(8,128)(2,1)}, bf16[2,144,1152]{2,1,0:T(8,128)(2,1)}, u32[]{:S(2)}, u32[]{:S(2)}) collective-permute-start(bf16[2,144,1152]{2,1,0:T(8,128)(2,1)} %get-tuple-element.378), channel_id=1, source_target_pairs={{0,1},{1,0},{2,3},{3,2},{4,5},{5,4},{6,7},{7,6},{8,9},{9,8},{10,11... | collective-permute-start | bytes 1990664 | tf_op jit(solution)/shard_map/ppermute | solution.py:32
  594.4 35.6 %collective-permute-start.95 = (bf16[4,144,1152]{2,1,0:T(8,128)(2,1)}, bf16[4,144,1152]{2,1,0:T(8,128)(2,1)S(1)}, u32[]{:S(2)}, u32[]{:S(2)}) collective-permute-start(bf16[4,144,1152]{2,1,0:T(8,128)(2,1)} %get-tuple-element.391), channel_id=1, source_target_pairs={{0,8},{4,12},{8,0},{12,4},{1,9},{5,13},{9,1},{13,5},{2,10},{6,14},... | collective-permute-start | bytes 3981320 | tf_op jit(solution)/shard_map/ppermute | solution.py:32
  (218 other events, 3138.4 us)
Sparse Core Ops, SparseCore 0:
  273.7 120.6 reduce-scatter.1
  412.4 135.6 all-gather.6
  675.2 117.2 all-gather.4

commit v4 on v3

--- a/solution.py
+++ b/solution.py
@@ -521,7 +521,7 @@
 
     works = ("halve", "halve", "add", "join", "join", "pass")
     own_state = 3
-    offload = False
+    offload = natural = False
 
     def advanced(self, outs):
         work = self.works[self.state]
@@ -580,16 +580,20 @@
         block = (1, SHARE_ROWS, D)
         scalar = lax.axis_index("batch").reshape(1).astype(jnp.int32)
 
-        def source(slot):
+        def source(one):
             def index(i, m):
                 core, y, low, high = i // 8, i // 4 % 2, i // 2 % 2, i % 2
-                return ((y * 2 + core) * 4 + high * 2 + low, slot, 0, 0)
+                device = i if one.natural else (y * 2 + core) * 4 + high * 2 + low
+                return (device, one.slot, 0, 0)
 
             return pl.BlockSpec((None,) + block, index)
 
+        natural = sums[0].natural
+
         def expand(i, m):
-            own = jnp.where(i // 8 == m[0], m[0], 1 - m[0])
-            return (layer, i % 4, own * 2 + i // 4 % 2)
+            core, y = (i // 4 % 2, i // 8) if natural else (i // 8, i // 4 % 2)
+            own = jnp.where(core == m[0], m[0], 1 - m[0])
+            return (layer, i % 4, own * 2 + y)
 
         indices = (
             lambda i, m: (layer, i, 0),
@@ -627,7 +631,7 @@
             grid_spec=pltpu.PrefetchScalarGridSpec(
                 num_scalar_prefetch=1,
                 grid=(SHARES,),
-                in_specs=[source(one.slot) for one in sums] + [ANYWHERE] * (count + 1),
+                in_specs=[source(one) for one in sums] + [ANYWHERE] * (count + 1),
                 out_specs=[pl.BlockSpec(blocks[k], indices[k]) for k in targets] + [ANYWHERE],
             ),
             out_shape=[jax.ShapeDtypeStruct(shapes[k], FLOAT) for k in targets]
@@ -646,31 +650,33 @@
 
     def add(self, one, through):
         slot, tokens, dim = len(self.group), one.act.shape[2], len(self.shares) % 2
-        one.offload = True
+        one.offload = one.natural = True
         earlier = [self.buffer] if slot else []
         self.sums.append(one)
         self.group.append(one)
         count = len(earlier)
-        width = 1 if dim else 2
-        place = lambda d: (slot, d, 0, 0) if dim else (d, slot, 0, 0)
-        shape = (width, SHARES) if dim else (SHARES, width)
-
-        def share(d):
-            row, col = d // 4, d % 4
-            return row % 2 * 8 + row // 2 * 4 + col % 2 * 2 + col // 2
+        shape = (1, SHARES) if dim else (SHARES, 2)
+        place = lambda j: (slot, j, 0, 0) if dim else (j, slot, 0, 0)
+        block = (1, 2) if dim else (2, 1)
+        cross = isinstance(one, CrossGradSum)
 
         def body(act, delta, *refs):
-            refs[count + 1][0, 0] = product(act[0], delta[0]).astype(BFLOAT)
+            value = product(act[0], delta[0]).astype(BFLOAT)
+            for k in range(2):
+                part = value[k * SHARE_ROWS : (k + 1) * SHARE_ROWS]
+                refs[count + 1][(0, k) if dim else (k, 0)] = part
 
         self.buffer, through = pl.pallas_call(
             body,
-            grid=(SHARES,),
+            grid=(SHARES // 2,),
             in_specs=[
-                pl.BlockSpec((1, SHARE_ROWS, tokens), lambda d: one.act_index(share(d))),
-                pl.BlockSpec((1, tokens, D), lambda d: one.delta_index(share(d))),
+                pl.BlockSpec(
+                    (1, 2 * SHARE_ROWS, tokens), lambda j: (0, j % 4 if cross else j, 0)
+                ),
+                pl.BlockSpec((1, tokens, D), lambda j: (0, 0, j // 4 if cross else 0)),
             ]
             + [ANYWHERE] * (count + 1),
-            out_specs=[pl.BlockSpec((1, 1, SHARE_ROWS, D), place), ANYWHERE],
+            out_specs=[pl.BlockSpec(block + (SHARE_ROWS, D), place), ANYWHERE],
             out_shape=[
                 jax.ShapeDtypeStruct(shape + (SHARE_ROWS, D), BFLOAT),
                 jax.ShapeDtypeStruct(through.shape, through.dtype),
@@ -1447,8 +1453,9 @@
 
 
 class Pair:
-    def __init__(self, args, modulations, taps, tile):
-        self.args, self.modulations, self.taps, self.tile = args, modulations, taps, tile
+    def __init__(self, args, taps, tile):
+        self.args, self.taps, self.tile = args, taps, tile
+        self.modulations = [None] * LAYERS
         self.cells = tile[0] * tile[1]
         self.width = args["proj"].shape[1]
         self.heads = self.width // HD
@@ -1461,29 +1468,48 @@
         ]
         self.qkv, self.expand, self.bias = [], [], []
         self.pieces = {}
+        self.quarter, self.batch = quarter, batch
+        self.modulate()
         for layer in range(LAYERS):
-            own, other = pack_call(
-                args["qkv"], args["decay"], layer, self.places[0], self.width
-            )
-            part = own.shape[0] // 4
-            piece = lax.dynamic_slice_in_dim(other, quarter * part, part, 0)
-            self.pieces["qkv", layer] = piece
-            self.qkv.append([own])
-            inner = args["shrink"].shape[1]
-            piece = lax.dynamic_slice(
-                args["expand"], (layer, quarter * part, (1 - batch) * inner), (1, part, inner)
-            )
-            self.pieces["expand", layer] = piece[0]
-            self.expand.append([args["expand"]])
-            start = self.width - self.width // LANES * LANES
-            self.bias.append(
-                jnp.pad(
-                    args["decay_bias"][layer].astype(FLOAT)[None],
-                    ((0, 0), (start, LANES - start - self.heads)),
-                )
-            )
+            self.prepare(layer)
         for stage in range(3):
             self.fetch("qkv", 0, stage, [])
+
+    def prepare(self, layer):
+        args = self.args
+        own, other = pack_call(args["qkv"], args["decay"], layer, self.places[0], self.width)
+        part = own.shape[0] // 4
+        self.pieces["qkv", layer] = lax.dynamic_slice_in_dim(other, self.quarter * part, part, 0)
+        self.qkv.append([own])
+        inner = args["shrink"].shape[1]
+        piece = lax.dynamic_slice(
+            args["expand"],
+            (layer, self.quarter * part, (1 - self.batch) * inner),
+            (1, part, inner),
+        )
+        self.pieces["expand", layer] = piece[0]
+        self.expand.append([args["expand"]])
+        start = self.width - self.width // LANES * LANES
+        self.bias.append(
+            jnp.pad(
+                args["decay_bias"][layer].astype(FLOAT)[None],
+                ((0, 0), (start, LANES - start - self.heads)),
+            )
+        )
+
+    def modulate(self):
+        cond = self.args["cond"]
+        partial = jnp.stack(
+            [
+                jnp.dot(cond, self.args["ada"][layer], preferred_element_type=FLOAT)
+                for layer in range(LAYERS)
+            ],
+            axis=1,
+        )
+        total = partial[:ITEMS] + swap(partial[ITEMS:])
+        for layer in range(LAYERS):
+            value = total[:, layer] + self.args["ada_bias"][layer]
+            self.modulations[layer] = value.reshape(ITEMS, 6, D)
 
     def fetch(self, name, layer, stage, after):
         held = self.pieces[name, layer]
@@ -1526,6 +1552,7 @@
         parts = project_call(
             mixed, mixed_other, self.qkv[layer], self.bias[layer], places, self.cells, self.width
         )
+        parts = list(parts)
         self.fetch("expand", layer, 2, [parts[0]])
         if layer + 1 < LAYERS:
             self.fetch("qkv", layer + 1, 0, [parts[0]])
@@ -1604,6 +1631,7 @@
         if layer:
             mixer_pipe, grad_decay = mixer([delta_conv])
         top, bottom, left, right = delta_sides
+        (left,) = passed_by([left], [right])
         left = tick("P8", {"C": mixer_pipe}, left)
         delta_sides = (top, bottom, left, right)
         delta_hidden, grad_taps = conv_backward(
@@ -1625,7 +1653,6 @@
     shape = (ITEMS, pair.cells, D)
     tokens = tokens_in.reshape(shape)
     delta = cotangent.reshape(shape)
-    outer_low = (pair.modulations[-1][:, 5:6] * delta.astype(FLOAT)).astype(BFLOAT)
     hidden, edges = enter_first(tokens, pair.modulations[0], tile)
     stored = []
     for layer in range(LAYERS):
@@ -1638,6 +1665,7 @@
             )
         else:
             block_out, saved["outer"] = leave(middle, own, received, mod)
+    outer_low = (pair.modulations[-1][:, 5:6] * delta.astype(FLOAT)).astype(BFLOAT)
     outer_low = outer_low.reshape(-1, D)
     outer_other = swap(outer_low)
     for layer in reversed(range(LAYERS)):
@@ -1808,21 +1836,20 @@
 SCHEDULE = {
     (1, "P1"): "aA1",
     (1, "P2"): "aB1rL1",
-    (1, "P7"): "sC1sS1",
+    (1, "P7"): "sC1",
     (0, "P1"): "kC1sA0",
-    (0, "P2"): "tS1kA0sB0",
+    (0, "P2"): "kA0sB0",
     (0, "P3"): "gL1kB0",
-    (0, "P4"): "tS1",
-    (0, "P5"): "tC1tS1",
-    (0, "P8"): "tC1tA0tS1sC0",
-    (0, "P7"): "tC1tA0tB0kC0sS0",
+    (0, "P5"): "tC1",
+    (0, "P8"): "sC0kC0tC1tA0",
+    (0, "P7"): "tC1tA0tB0sS0",
 }
 TAIL = (
-    "tA0tB0tS0",
+    "tA0tB0tC0tS0",
+    "tB0tC0tS0",
+    "tB0tC0tS0gL0",
+    "tS0",
     "mS1",
-    "tB0tC0tS0",
-    "tB0tC0tS0",
-    "tC0tS0gL0",
     "fAB1",
     "mS0",
     "fABC0",
@@ -1928,20 +1955,6 @@
         cond_first = cond_slice
     biases = gather_last(ada_bias).astype(FLOAT)
     taps_all = gather_last(conv_taps)
-    weights, modulations = [], []
-    partial = jnp.stack(
-        [
-            jnp.dot(cond_first, ada_weight[layer], preferred_element_type=FLOAT)
-            for layer in range(LAYERS)
-        ],
-        axis=1,
-    )
-    if count == 2:
-        total = partial[:items] + swap(partial[items:])
-    else:
-        total = lax.psum_scatter(partial, "batch", scatter_dimension=0, tiled=True)
-    for layer in range(LAYERS):
-        modulations.append((total[:, layer] + biases[layer]).reshape(items, 6, D))
     fast = pipelined(width) and count * items == 4 and tile == (8, 8)
     hidden_units = shrink_weight.shape[1]
     if fast:
@@ -1950,9 +1963,13 @@
 
         def act(names, through):
             names = [names[at : at + 3] for at in range(0, len(names), 3)]
-            steps = [moving[name[1:]] for name in names if name[0] == "t"]
-            through = tick(steps, through)
-            for name in names:
+            steps = []
+            for name in names + ["end"]:
+                if name[0] == "t":
+                    steps.append(moving[name[1:]])
+                    continue
+                through = tick(steps, through)
+                steps = []
                 one = moving.get(name[1:])
                 if name[0] == "s":
                     through = one.start(through)
@@ -1973,14 +1990,18 @@
                 moving[name if len(name) == 2 else name + str(layer)] = one
                 if name in "ABC":
                     one.offload = True
+            if "S" in fresh and not layer:
+                moving["S0"] = SmallSum(
+                    jnp.concatenate([moving["S0"].value, moving["S1"].value], axis=0)
+                )
             return act(SCHEDULE.get((layer, point), ""), through)
 
         pair = Pair(
             dict(
                 qkv=qkv_weight, decay=decay_weight, decay_bias=decay_bias, proj=proj_weight,
-                expand=expand_weight, shrink=shrink_weight,
+                expand=expand_weight, shrink=shrink_weight, cond=cond_first, ada=ada_weight,
+                ada_bias=biases,
             ),
-            modulations,
             taps_all,
             tile,
         )
@@ -2008,7 +2029,8 @@
                 finished = (finished or {}) | made
             elif names[0] == "m":
                 layer = int(names[2])
-                smalls[layer] = list(split_smalls(moving[names[1:]].keep, items, heads, width))
+                flat = moving["S0"].keep[layer * SMALL_ROWS : (layer + 1) * SMALL_ROWS]
+                smalls[layer] = list(split_smalls(flat, items, heads, width))
                 mods = gather_items(smalls[layer][0])
                 smalls[layer][0] = mods
                 grad_ada, through = ada_call(cond_first, mods, grad_ada, layer, through)
@@ -2016,6 +2038,20 @@
                 through = act(names, through)
         grad_tokens = through
     else:
+        partial = jnp.stack(
+            [
+                jnp.dot(cond_first, ada_weight[layer], preferred_element_type=FLOAT)
+                for layer in range(LAYERS)
+            ],
+            axis=1,
+        )
+        if count == 2:
+            total = partial[:items] + swap(partial[items:])
+        else:
+            total = lax.psum_scatter(partial, "batch", scatter_dimension=0, tiled=True)
+        modulations = [
+            (total[:, layer] + biases[layer]).reshape(items, 6, D) for layer in range(LAYERS)
+        ]
         block_out, grad_tokens, bigs, smalls = general_forward_backward(
             tokens_in, cotangent, modulations, taps_all, qkv_weight, decay_weight, decay_bias,
             proj_weight, expand_weight, shrink_weight,

time: 831 us -> 806 us (0.970)
  waiting for transfers between devices: 385 us -> 360 us
  Pallas kernels: 222 us -> 210 us
    ppermute x88 -> x84, waiting for transfers between devices: 233 us -> 269 us  [swap(): return lax.ppermute(value, axis, [(i, i ^ bit) for i in range(count)])]
    ppermute x4, waiting for transfers between devices: 30.8 us -> 4.78 us  [halo_edges(): lax.ppermute(first_row, 'row', [(i + 1, i) for i in range(rows - 1)])]
    all_gather x2, waiting for transfers between devices: 84.1 us -> 64.6 us  [collect(): whole = lax.all_gather(shares, GRID_AXES)]
    ppermute x4, waiting for transfers between devices: 30.9 us -> 16.5 us  [halo_edges(): right = lax.ppermute(to_left, 'col', [(i + 1, i) for i in range(cols - 1)])]
    unnamed x272 -> x270, local copies, waits for them, and re-layouts: 24 us -> 30.6 us
    ppermute x88 -> x84, starting transfers between devices: 117 us -> 119 us  [swap(): return lax.ppermute(value, axis, [(i, i ^ bit) for i in range(count)])]
  transfers between devices with their start and end apart: 109 -> 105, of which waited for: 51 -> 56; matrix products, arithmetic and copies ran while one was open for 4% -> 3% of each run, Pallas kernels for 23% -> 23%
where the time goes in v4:
time: 806 us; the launch traced here: 798 us
  waiting for transfers between devices  360 us (45%)
  Pallas kernels  210 us (26%)
  starting transfers between devices  156 us (19%)
  local copies, waits for them, and re-layouts  37.6 us (5%)
  between operations  16.3 us (2%)
  other arithmetic  9.3 us (1%)
  matrix products  9.25 us (1%)
    ppermute x84, waiting for transfers between devices, swap(): return lax.ppermute(value, axis, [(i, i ^ bit) for i in range(count)])  269 us
    ppermute x84, starting transfers between devices, swap(): return lax.ppermute(value, axis, [(i, i ^ bit) for i in range(count)])  119 us
    all_gather x2, waiting for transfers between devices, collect(): whole = lax.all_gather(shares, GRID_AXES)  64.6 us
    pallas_call x25, Pallas kernels, call(): pl.pallas_call(whole, in_specs=[pl.BlockSpec(memory_space=pltpu.SMEM)] *...  60.3 us
    pallas_call x2, Pallas kernels, finish(): pl.pallas_call(body, grid_spec=pltpu.PrefetchScalarGridSpec(num_scalar_pr...  39.3 us
    pallas_call x8, Pallas kernels, call(): pl.pallas_call(body, grid_spec=pltpu.PrefetchScalarGridSpec(num_scalar_pr...  34.8 us
    unnamed x270, local copies, waits for them, and re-layouts  30.6 us
    pallas_call x4, Pallas kernels, scan_call(): pl.pallas_call(body, grid_spec=pltpu.PrefetchScalarGridSpec(num_scalar_pr...  20.1 us
  transfers between devices with their start and end apart: 105, of which 56 were waited for; matrix products, arithmetic and copies ran while one was open for 3% of the time, Pallas kernels for 23%

profile of v4, /device:TPU:0, one launch (start us, length us, event | category | flops | bytes accessed | tf_op | source)
XLA Modules:
  0.0 797.8 jit_solution(12424359728068272131)
XLA Ops:
  83.2 10.7 %collective-permute-done.13.refs_3_ = bf16[1,64,1920]{2,1,0:T(8,128)(2,1)S(1)} collective-permute-done((bf16[1,64,1920]{2,1,0:T(8,128)(2,1)S(1)}, bf16[1,64,1920]{2,1,0:T(8,128)(2,1)S(1)}, u32[]{:S(2)}, u32[]{:S(2)}) %collective-permute-start.13) | collective-permute-done | bytes 245792 | tf_op jit(solution)/shard_map/ppermute | solution.py:32
  111.7 10.7 %collective-permute-done.18.refs_2_ = bf16[128,1152]{1,0:T(8,128)(2,1)S(1)} collective-permute-done((bf16[128,1152]{1,0:T(8,128)(2,1)S(1)}, bf16[128,1152]{1,0:T(8,128)(2,1)S(1)}, u32[]{:S(2)}, u32[]{:S(2)}) %collective-permute-start.18) | collective-permute-done | bytes 294944 | tf_op jit(solution)/shard_map/ppermute | solution.py:32
  208.1 8.3 %collective-permute-done.40.refs_2_ = bf16[128,1152]{1,0:T(8,128)(2,1)S(1)} collective-permute-done((bf16[128,1152]{1,0:T(8,128)(2,1)S(1)}, bf16[128,1152]{1,0:T(8,128)(2,1)S(1)}, u32[]{:S(2)}, u32[]{:S(2)}) %collective-permute-start.40) | collective-permute-done | bytes 294944 | tf_op jit(solution)/shard_map/ppermute | solution.py:32
  219.0 7.7 collective-permute-done.41.refs_2_.five
  234.1 8.4 %shard_map.231 = (f32[128,1152]{1,0:T(8,128)S(1)}, bf16[128,1152]{1,0:T(8,128)(2,1)S(1)}, bf16[256,2304]{1,0:T(8,128)(2,1)S(1)}) custom-call(s32[3]{0:T(128)S(1)} %pad_add_fusion.2.refs_0_.places, bf16[128,1152]{1,0:T(8,128)(2,1)S(1)} %fusion.12.refs_1_, bf16[128,1152]{1,0:T(8,128)(2,1)S(1)} %collective-permute-done.47.refs_2_, ...), custom_call_target="tpu_custom_call" | custom-call | flops 1 | bytes 1 | tf_op jit(solution)/shard_map/pallas_call | solution.py:904
  300.1 8.6 %collective-permute-done.56.refs_1_ = bf16[128,1152]{1,0:T(8,128)(2,1)S(1)} collective-permute-done((bf16[128,1152]{1,0:T(8,128)(2,1)S(1)}, bf16[128,1152]{1,0:T(8,128)(2,1)S(1)}, u32[]{:S(2)}, u32[]{:S(2)}) %collective-permute-start.56) | collective-permute-done | bytes 294944 | tf_op jit(solution)/shard_map/ppermute | solution.py:32
  346.6 8.7 %shard_map.245 = (f32[128,1152]{1,0:T(8,128)S(1)}, bf16[128,1152]{1,0:T(8,128)(2,1)S(1)}, bf16[256,2304]{1,0:T(8,128)(2,1)S(1)}) custom-call(s32[3]{0:T(128)S(1)} %pad_add_fusion.refs_0_.places, bf16[128,1152]{1,0:T(8,128)(2,1)} %get-tuple-element.303.refs_1_, bf16[128,1152]{1,0:T(8,128)(2,1)} %collective-permute-done.63.refs_2_, ...), custom_call_target="tpu_custom_call" | custom-call | flops 1 | bytes 1 | tf_op jit(solution)/shard_map/pallas_call | solution.py:904
  368.7 8.4 %collective-permute-done.66.refs_2_ = bf16[128,1152]{1,0:T(8,128)(2,1)S(1)} collective-permute-done((bf16[128,1152]{1,0:T(8,128)(2,1)S(1)}, bf16[128,1152]{1,0:T(8,128)(2,1)S(1)}, u32[]{:S(2)}, u32[]{:S(2)}) %collective-permute-start.66) | collective-permute-done | bytes 294944 | tf_op jit(solution)/shard_map/ppermute | solution.py:32
  379.4 7.9 collective-permute-done.68.refs_2_.low_other
  440.0 15.2 %collective-permute-done.72.refs_2_ = bf16[1,64,1920]{2,1,0:T(8,128)(2,1)S(1)} collective-permute-done((bf16[1,64,1920]{2,1,0:T(8,128)(2,1)S(1)}, bf16[1,64,1920]{2,1,0:T(8,128)(2,1)S(1)}, u32[]{:S(2)}, u32[]{:S(2)}) %collective-permute-start.72) | collective-permute-done | bytes 245792 | tf_op jit(solution)/shard_map/ppermute | solution.py:32
  455.3 9.1 %collective-permute-done.73.refs_3_ = bf16[1,64,1920]{2,1,0:T(8,128)(2,1)S(1)} collective-permute-done((bf16[1,64,1920]{2,1,0:T(8,128)(2,1)S(1)}, bf16[1,64,1920]{2,1,0:T(8,128)(2,1)S(1)}, u32[]{:S(2)}, u32[]{:S(2)}) %collective-permute-start.73) | collective-permute-done | bytes 245792 | tf_op jit(solution)/shard_map/ppermute | solution.py:32
  482.7 8.3 %collective-permute-start.81 = (bf16[2,10,1152]{2,1,0:T(8,128)(2,1)S(1)}, bf16[2,10,1152]{2,1,0:T(8,128)(2,1)S(1)}, u32[]{:S(2)}, u32[]{:S(2)}) collective-permute-start(bf16[2,10,1152]{2,1,0:T(8,128)(2,1)S(1)} %pad_maximum_fusion.14), channel_id=1, source_target_pairs={{0,1},{1,2},{2,3},{4,5},{5,6},{6,7},{8,9},{9,10},{10,11},{12,13},{... | collective-permute-start | bytes 138248 | tf_op jit(solution)/shard_map/ppermute | solution.py:939
  522.6 16.0 %collective-permute-done.76.refs_3_ = bf16[4,144,1152]{2,1,0:T(8,128)(2,1)S(1)} collective-permute-done((bf16[4,144,1152]{2,1,0:T(8,128)(2,1)S(1)}, bf16[4,144,1152]{2,1,0:T(8,128)(2,1)S(1)}, u32[]{:S(2)}, u32[]{:S(2)}) %collective-permute-start.76) | collective-permute-done | bytes 1327136 | tf_op jit(solution)/shard_map/ppermute | solution.py:32
  549.4 17.6 %collective-permute-done.86.refs_5_ = bf16[4,144,1152]{2,1,0:T(8,128)(2,1)S(1)} collective-permute-done((bf16[4,144,1152]{2,1,0:T(8,128)(2,1)}, bf16[4,144,1152]{2,1,0:T(8,128)(2,1)S(1)}, u32[]{:S(2)}, u32[]{:S(2)}) %collective-permute-start.86) | collective-permute-done | bytes 1327136 | tf_op jit(solution)/shard_map/ppermute | solution.py:32
  579.1 16.2 %collective-permute-done.87.refs_1_ = bf16[1,144,1152]{2,1,0:T(8,128)(2,1)S(1)} collective-permute-done((bf16[1,144,1152]{2,1,0:T(8,128)(2,1)S(1)}, bf16[1,144,1152]{2,1,0:T(8,128)(2,1)S(1)}, u32[]{:S(2)}, u32[]{:S(2)}) %collective-permute-start.87) | collective-permute-done | bytes 331808 | tf_op jit(solution)/shard_map/ppermute | solution.py:32
  605.8 8.0 %collective-permute-done.93.refs_5_ = f32[64,1152]{1,0:T(8,128)S(1)} collective-permute-done((f32[64,1152]{1,0:T(8,128)S(1)}, f32[64,1152]{1,0:T(8,128)S(1)}, u32[]{:S(2)}, u32[]{:S(2)}) %collective-permute-start.93) | collective-permute-done | bytes 294944 | tf_op jit(solution)/shard_map/ppermute | solution.py:32
  613.8 10.3 %collective-permute-done.91.refs_1_ = bf16[1,144,1152]{2,1,0:T(8,128)(2,1)S(1)} collective-permute-done((bf16[1,144,1152]{2,1,0:T(8,128)(2,1)S(1)}, bf16[1,144,1152]{2,1,0:T(8,128)(2,1)S(1)}, u32[]{:S(2)}, u32[]{:S(2)}) %collective-permute-start.91) | collective-permute-done | bytes 331808 | tf_op jit(solution)/shard_map/ppermute | solution.py:32
  630.4 9.4 %collective-permute-done.95.refs_3_ = f32[64,1152]{1,0:T(8,128)S(1)} collective-permute-done((f32[64,1152]{1,0:T(8,128)S(1)}, f32[64,1152]{1,0:T(8,128)S(1)}, u32[]{:S(2)}, u32[]{:S(2)}) %collective-permute-start.95) | collective-permute-done | bytes 294944 | tf_op jit(solution)/shard_map/ppermute | solution.py:32
  647.3 14.5 %collective-permute-done.98.refs_1_ = f32[64,1152]{1,0:T(8,128)S(1)} collective-permute-done((f32[64,1152]{1,0:T(8,128)S(1)}, f32[64,1152]{1,0:T(8,128)S(1)}, u32[]{:S(2)}, u32[]{:S(2)}) %collective-permute-start.98) | collective-permute-done | bytes 294944 | tf_op jit(solution)/shard_map/ppermute | solution.py:32
  667.8 9.1 %shard_map.273 = (f32[2,576,6912]{2,1,0:T(8,128)}, bf16[128,1152]{1,0:T(8,128)(2,1)}) custom-call(f32[576,4]{1,0:T(8,128)S(1)} %copy-done.27, f32[4,6912]{1,0:T(4,128)S(1)} %get-tuple-element.487.values, bf16[128,1152]{1,0:T(8,128)(2,1)} %get-tuple-element.396.refs_0_), custom_call_target="tpu_custom_call", output_to_operand_aliasing={{1}: (2, {})} | custom-call | flops 1 | bytes 1 | tf_op jit(solution)/shard_map/pallas_call | solution.py:1817
  677.7 15.2 %shard_map.274 = (f32[2,2304,1152]{2,1,0:T(8,128)}, f32[2,576,4608]{2,1,0:T(8,128)}, bf16[128,1152]{1,0:T(8,128)(2,1)}) custom-call(s32[1]{0:T(128)} %bitcast.1.m, bf16[16,2,144,1152]{3,2,1,0:T(8,128)(2,1)} %bitcast.119, bf16[16,2,144,1152]{3,2,1,0:T(8,128)(2,1)} %bitcast.120, ...), custom_call_target="tpu_custom_call", output_to_operand_aliasing={{2}: (3, {})} | custom-call | flops 1 | bytes 1 | tf_op jit(solution)/shard_map/pallas_call | solution.py:629
  692.9 9.1 %shard_map.275 = (f32[2,576,6912]{2,1,0:T(8,128)}, bf16[128,1152]{1,0:T(8,128)(2,1)}) custom-call(f32[576,4]{1,0:T(8,128)S(1)} %copy-done.27, f32[4,6912]{1,0:T(4,128)S(1)} %get-tuple-element.485.values, f32[2,576,6912]{2,1,0:T(8,128)} %get-tuple-element.400.refs_0_, ...), custom_call_target="tpu_custom_call", output_to_operand_aliasing={{0}: (2, {}), {1}: (3, {})} | custom-call | flops 1 | bytes 1 | tf_op jit(solution)/shard_map/pallas_call | solution.py:1817
  702.1 64.6 %all-gather.5.cloned.1.call-done = bf16[64,144,1152]{2,1,0:T(8,128)(2,1)} async-done(((bf16[4,144,1152]{2,1,0:T(8,128)(2,1)}), bf16[64,144,1152]{2,1,0:T(8,128)(2,1)}) %all-gather.5.cloned.1.call-update) | async-done | bytes 21233680 | tf_op jit(solution)/shard_map/all_gather | solution.py:574
  766.7 24.1 %shard_map.276 = (f32[2,2304,1152]{2,1,0:T(8,128)}, f32[2,576,4608]{2,1,0:T(8,128)}, f32[2,576,3456]{2,1,0:T(8,128)}, f32[2,576,1152]{2,1,0:T(8,128)}, bf16[128,1152]{1,0:T(8,128)(2,1)}) custom-call(s32[1]{0:T(128)} %bitcast.1.m, bf16[16,4,144,1152]{3,2,1,0:T(8,128)(2,1)} %bitcast.115, ...), custom_call_target="tpu_custom_call", output_to_operand_aliasing={{0}: (5, {}), {1}: (6, {}), {4}: (7, {})} | custom-call | flops 1 | bytes 1 | tf_op jit(solution)/shard_map/pallas_call | solution.py:629
  (608 shorter events, 455.3 us)
Async XLA Ops:
  7.2 392.9 %reduce-scatter.2.cloned.1.call-start = ((), (), s32[]{:S(2)}) async-start(), calls=%async_computation.1 | async-start | bytes 11280384 | tf_op jit(solution)/shard_map/reduce_scatter | solution.py:692
  7.2 25.3 %collective-permute-start.1 = (bf16[2,3456]{1,0:T(2,128)(2,1)}, bf16[2,3456]{1,0:T(2,128)(2,1)S(1)}, u32[]{:S(2)}, u32[]{:S(2)}) collective-permute-start(bf16[2,3456]{1,0:T(2,128)(2,1)} %param.15), channel_id=1, source_target_pairs={{0,16},{16,0},{1,17},{17,1},{2,18},{18,2},{3,19},{19,3},{4,20},{20... | collective-permute-start | bytes 41480 | tf_op jit(solution)/shard_map/ppermute | solution.py:32
  81.7 46.5 %collective-permute-start.22 = (bf16[144,2304]{1,0:T(8,128)(2,1)S(1)}, bf16[144,2304]{1,0:T(8,128)(2,1)}, u32[]{:S(2)}, u32[]{:S(2)}) collective-permute-start(bf16[144,2304]{1,0:T(8,128)(2,1)S(1)} %get-tuple-element.231.refs_4_.refs_5_), channel_id=1, source_target_pairs={{0,4},{4,0},{8,12},{12,8},{1,5},{5,1},{9,13},{13,9},{2,6},{6,2},{1... | collective-permute-start | bytes 1990664 | tf_op jit(solution)/shard_map/ppermute | solution.py:32
  81.7 46.5 %collective-permute-start.23 = (bf16[144,2304]{1,0:T(8,128)(2,1)}, bf16[144,2304]{1,0:T(8,128)(2,1)}, u32[]{:S(2)}, u32[]{:S(2)}) collective-permute-start(bf16[144,2304]{1,0:T(8,128)(2,1)} %get-tuple-element.232.refs_5_.refs_6_), channel_id=1, source_target_pairs={{0,4},{4,0},{8,12},{12,8},{1,5},{5,1},{9,13},{13,9},{2,6},{6,2},{1... | collective-permute-start | bytes 1990664 | tf_op jit(solution)/shard_map/ppermute | solution.py:32
  125.6 24.2 %collective-permute-start.31 = (bf16[144,1920]{1,0:T(8,128)(2,1)}, bf16[144,1920]{1,0:T(8,128)(2,1)}, u32[]{:S(2)}, u32[]{:S(2)}) collective-permute-start(bf16[144,1920]{1,0:T(8,128)(2,1)} %shard_map.219.refs_0_), channel_id=1, source_target_pairs={{0,8},{4,12},{8,0},{12,4},{1,9},{5,13},{9,1},{13,5},{2,10},{6,14},... | collective-permute-start | bytes 1658888 | tf_op jit(solution)/shard_map/ppermute | solution.py:32
  149.8 27.7 %collective-permute-start.32 = (bf16[144,1920]{1,0:T(8,128)(2,1)}, bf16[144,1920]{1,0:T(8,128)(2,1)S(1)}, u32[]{:S(2)}, u32[]{:S(2)}) collective-permute-start(bf16[144,1920]{1,0:T(8,128)(2,1)} %get-tuple-element.246.refs_5_.refs_6_), channel_id=1, source_target_pairs={{0,4},{4,0},{8,12},{12,8},{1,5},{5,1},{9,13},{13,9},{2,6},{6,2},{1... | collective-permute-start | bytes 1658888 | tf_op jit(solution)/shard_map/ppermute | solution.py:32
  151.9 25.6 %collective-permute-start.33 = (bf16[144,1920]{1,0:T(8,128)(2,1)}, bf16[144,1920]{1,0:T(8,128)(2,1)S(1)}, u32[]{:S(2)}, u32[]{:S(2)}) collective-permute-start(bf16[144,1920]{1,0:T(8,128)(2,1)} %get-tuple-element.247.refs_6_.refs_7_), channel_id=1, source_target_pairs={{0,4},{4,0},{8,12},{12,8},{1,5},{5,1},{9,13},{13,9},{2,6},{6,2},{1... | collective-permute-start | bytes 1658888 | tf_op jit(solution)/shard_map/ppermute | solution.py:32
  166.8 34.7 %collective-permute-start.43 = (bf16[144,2304]{1,0:T(8,128)(2,1)S(1)}, bf16[144,2304]{1,0:T(8,128)(2,1)S(1)}, u32[]{:S(2)}, u32[]{:S(2)}) collective-permute-start(bf16[144,2304]{1,0:T(8,128)(2,1)S(1)} %shard_map.226.refs_0_), channel_id=1, source_target_pairs={{0,8},{4,12},{8,0},{12,4},{1,9},{5,13},{9,1},{13,5},{2,10},{6,14},... | collective-permute-start | bytes 1990664 | tf_op jit(solution)/shard_map/ppermute | solution.py:32
  201.5 25.3 %collective-permute-start.44 = (bf16[144,2304]{1,0:T(8,128)(2,1)S(1)}, bf16[144,2304]{1,0:T(8,128)(2,1)S(1)}, u32[]{:S(2)}, u32[]{:S(2)}) collective-permute-start(bf16[144,2304]{1,0:T(8,128)(2,1)S(1)} %get-tuple-element.261.refs_4_.refs_5_), channel_id=1, source_target_pairs={{0,4},{4,0},{8,12},{12,8},{1,5},{5,1},{9,13},{13,9},{2,6},{6,2},{1... | collective-permute-start | bytes 1990664 | tf_op jit(solution)/shard_map/ppermute | solution.py:32
  201.9 24.9 %collective-permute-start.45 = (bf16[144,2304]{1,0:T(8,128)(2,1)S(1)}, bf16[144,2304]{1,0:T(8,128)(2,1)S(1)}, u32[]{:S(2)}, u32[]{:S(2)}) collective-permute-start(bf16[144,2304]{1,0:T(8,128)(2,1)S(1)} %get-tuple-element.262.refs_5_.refs_6_), channel_id=1, source_target_pairs={{0,4},{4,0},{8,12},{12,8},{1,5},{5,1},{9,13},{13,9},{2,6},{6,2},{1... | collective-permute-start | bytes 1990664 | tf_op jit(solution)/shard_map/ppermute | solution.py:32
  265.6 412.1 %all-gather.7.cloned.1.call-start = ((), (), s32[]{:S(2)}) async-start(), calls=%async_computation.3 | async-start | bytes 11280384 | tf_op jit(solution)/shard_map/all_gather | solution.py:574
  312.1 24.5 %collective-permute-start.57 = (bf16[256,1920]{1,0:T(8,128)(2,1)}, bf16[256,1920]{1,0:T(8,128)(2,1)}, u32[]{:S(2)}, u32[]{:S(2)}) collective-permute-start(bf16[256,1920]{1,0:T(8,128)(2,1)} %shard_map.239.mine), channel_id=1, source_target_pairs={{0,16},{16,0},{1,17},{17,1},{2,18},{18,2},{3,19},{19,3},{4,20},{20... | collective-permute-start | bytes 2949128 | tf_op jit(solution)/shard_map/ppermute | solution.py:32
  403.1 363.6 %all-gather.5.cloned.1.call-start = ((), (), s32[]{:S(2)}) async-start(), calls=%async_computation.2 | async-start | bytes 22560768 | tf_op jit(solution)/shard_map/all_gather | solution.py:574
  409.9 61.3 %collective-permute-start.64 = (bf16[4,144,1152]{2,1,0:T(8,128)(2,1)}, bf16[4,144,1152]{2,1,0:T(8,128)(2,1)S(1)}, u32[]{:S(2)}, u32[]{:S(2)}) collective-permute-start(bf16[4,144,1152]{2,1,0:T(8,128)(2,1)} %copy-done.118), channel_id=1, source_target_pairs={{0,8},{4,12},{8,0},{12,4},{1,9},{5,13},{9,1},{13,5},{2,10},{6,14},... | collective-permute-start | bytes 3981320 | tf_op jit(solution)/shard_map/ppermute | solution.py:32
  435.5 28.8 %collective-permute-start.73 = (bf16[1,64,1920]{2,1,0:T(8,128)(2,1)S(1)}, bf16[1,64,1920]{2,1,0:T(8,128)(2,1)S(1)}, u32[]{:S(2)}, u32[]{:S(2)}) collective-permute-start(bf16[1,64,1920]{2,1,0:T(8,128)(2,1)S(1)} %get-tuple-element.329), channel_id=1, source_target_pairs={{0,2},{1,3},{2,0},{3,1},{4,6},{5,7},{6,4},{7,5},{8,10},{9,11},{10,... | collective-permute-start | bytes 737288 | tf_op jit(solution)/shard_map/ppermute | solution.py:32
  438.7 25.7 %collective-permute-start.74 = (bf16[1,64,1920]{2,1,0:T(8,128)(2,1)S(1)}, bf16[1,64,1920]{2,1,0:T(8,128)(2,1)S(1)}, u32[]{:S(2)}, u32[]{:S(2)}) collective-permute-start(bf16[1,64,1920]{2,1,0:T(8,128)(2,1)S(1)} %get-tuple-element.330), channel_id=1, source_target_pairs={{0,3},{1,2},{2,1},{3,0},{4,7},{5,6},{6,5},{7,4},{8,11},{9,10},{10,... | collective-permute-start | bytes 737288 | tf_op jit(solution)/shard_map/ppermute | solution.py:32
  477.5 24.4 %collective-permute-start.77 = (bf16[256,1920]{1,0:T(8,128)(2,1)S(1)}, bf16[256,1920]{1,0:T(8,128)(2,1)S(1)}, u32[]{:S(2)}, u32[]{:S(2)}) collective-permute-start(bf16[256,1920]{1,0:T(8,128)(2,1)S(1)} %shard_map.256.mine), channel_id=1, source_target_pairs={{0,16},{16,0},{1,17},{17,1},{2,18},{18,2},{3,19},{19,3},{4,20},{20... | collective-permute-start | bytes 2949128 | tf_op jit(solution)/shard_map/ppermute | solution.py:32
  506.7 32.0 %collective-permute-start.76 = (bf16[4,144,1152]{2,1,0:T(8,128)(2,1)S(1)}, bf16[4,144,1152]{2,1,0:T(8,128)(2,1)S(1)}, u32[]{:S(2)}, u32[]{:S(2)}) collective-permute-start(bf16[4,144,1152]{2,1,0:T(8,128)(2,1)S(1)} %copy-done.117), channel_id=1, source_target_pairs={{0,8},{4,12},{8,0},{12,4},{1,9},{5,13},{9,1},{13,5},{2,10},{6,14},... | collective-permute-start | bytes 3981320 | tf_op jit(solution)/shard_map/ppermute | solution.py:32
  506.7 32.0 %collective-permute-start.75 = (bf16[2,144,1152]{2,1,0:T(8,128)(2,1)S(1)}, bf16[2,144,1152]{2,1,0:T(8,128)(2,1)S(1)}, u32[]{:S(2)}, u32[]{:S(2)}) collective-permute-start(bf16[2,144,1152]{2,1,0:T(8,128)(2,1)S(1)} %get-tuple-element.333), channel_id=1, source_target_pairs={{0,1},{1,0},{2,3},{3,2},{4,5},{5,4},{6,7},{7,6},{8,9},{9,8},{10,11... | collective-permute-start | bytes 1990664 | tf_op jit(solution)/shard_map/ppermute | solution.py:32
  512.1 55.0 %collective-permute-start.86 = (bf16[4,144,1152]{2,1,0:T(8,128)(2,1)}, bf16[4,144,1152]{2,1,0:T(8,128)(2,1)S(1)}, u32[]{:S(2)}, u32[]{:S(2)}) collective-permute-start(bf16[4,144,1152]{2,1,0:T(8,128)(2,1)} %get-tuple-element.354), channel_id=1, source_target_pairs={{0,8},{4,12},{8,0},{12,4},{1,9},{5,13},{9,1},{13,5},{2,10},{6,14},... | collective-permute-start | bytes 3981320 | tf_op jit(solution)/shard_map/ppermute | solution.py:32
  539.2 27.9 %collective-permute-start.85 = (bf16[2,144,1152]{2,1,0:T(8,128)(2,1)S(1)}, bf16[2,144,1152]{2,1,0:T(8,128)(2,1)S(1)}, u32[]{:S(2)}, u32[]{:S(2)}) collective-permute-start(bf16[2,144,1152]{2,1,0:T(8,128)(2,1)S(1)} %get-tuple-element.352), channel_id=1, source_target_pairs={{0,1},{1,0},{2,3},{3,2},{4,5},{5,4},{6,7},{7,6},{8,9},{9,8},{10,11... | collective-permute-start | bytes 1990664 | tf_op jit(solution)/shard_map/ppermute | solution.py:32
  544.7 51.4 %collective-permute-start.89 = (bf16[4,144,1152]{2,1,0:T(8,128)(2,1)S(1)}, bf16[4,144,1152]{2,1,0:T(8,128)(2,1)S(1)}, u32[]{:S(2)}, u32[]{:S(2)}) collective-permute-start(bf16[4,144,1152]{2,1,0:T(8,128)(2,1)S(1)} %get-tuple-element.366), channel_id=1, source_target_pairs={{0,8},{4,12},{8,0},{12,4},{1,9},{5,13},{9,1},{13,5},{2,10},{6,14},... | collective-permute-start | bytes 3981320 | tf_op jit(solution)/shard_map/ppermute | solution.py:32
  570.0 26.0 %collective-permute-start.88 = (bf16[2,144,1152]{2,1,0:T(8,128)(2,1)S(1)}, bf16[2,144,1152]{2,1,0:T(8,128)(2,1)S(1)}, u32[]{:S(2)}, u32[]{:S(2)}) collective-permute-start(bf16[2,144,1152]{2,1,0:T(8,128)(2,1)S(1)} %get-tuple-element.364), channel_id=1, source_target_pairs={{0,1},{1,0},{2,3},{3,2},{4,5},{5,4},{6,7},{7,6},{8,9},{9,8},{10,11... | collective-permute-start | bytes 1990664 | tf_op jit(solution)/shard_map/ppermute | solution.py:32
  599.4 25.5 %collective-permute-start.92 = (bf16[2,144,1152]{2,1,0:T(8,128)(2,1)S(1)}, bf16[2,144,1152]{2,1,0:T(8,128)(2,1)S(1)}, u32[]{:S(2)}, u32[]{:S(2)}) collective-permute-start(bf16[2,144,1152]{2,1,0:T(8,128)(2,1)S(1)} %get-tuple-element.382), channel_id=1, source_target_pairs={{0,1},{1,0},{2,3},{3,2},{4,5},{5,4},{6,7},{7,6},{8,9},{9,8},{10,11... | collective-permute-start | bytes 1990664 | tf_op jit(solution)/shard_map/ppermute | solution.py:32
  (213 other events, 2726.5 us)
Sparse Core Ops, SparseCore 0:
  265.7 120.5 reduce-scatter.1
  403.2 116.5 all-gather.6
  644.3 122.2 all-gather.4

commit v5 on v4

--- a/solution.py
+++ b/solution.py
@@ -1838,8 +1838,8 @@
     (1, "P2"): "aB1rL1",
     (1, "P7"): "sC1",
     (0, "P1"): "kC1sA0",
-    (0, "P2"): "kA0sB0",
-    (0, "P3"): "gL1kB0",
+    (0, "P2"): "kA0sB0gL1",
+    (0, "P3"): "kB0",
     (0, "P5"): "tC1",
     (0, "P8"): "sC0kC0tC1tA0",
     (0, "P7"): "tC1tA0tB0sS0",

time: 806 us -> 815 us (1.011)
    unnamed x270 -> x260, local copies, waits for them, and re-layouts: 30.6 us -> 29 us
  transfers between devices with their start and end apart: 105 -> 105, of which waited for: 56 -> 52; matrix products, arithmetic and copies ran while one was open for 3% -> 4% of each run, Pallas kernels for 23% -> 23%
where the time goes in v5:
time: 815 us; the launch traced here: 807 us
  waiting for transfers between devices  360 us (44%)
  Pallas kernels  215 us (26%)
  starting transfers between devices  155 us (19%)
  local copies, waits for them, and re-layouts  39.1 us (5%)
  between operations  16.3 us (2%)
  other arithmetic  12.6 us (2%)
  matrix products  9.3 us (1%)
    ppermute x84, waiting for transfers between devices, swap(): return lax.ppermute(value, axis, [(i, i ^ bit) for i in range(count)])  274 us
    ppermute x84, starting transfers between devices, swap(): return lax.ppermute(value, axis, [(i, i ^ bit) for i in range(count)])  117 us
    pallas_call x25, Pallas kernels, call(): pl.pallas_call(whole, in_specs=[pl.BlockSpec(memory_space=pltpu.SMEM)] *...  61 us
    all_gather x2, waiting for transfers between devices, collect(): whole = lax.all_gather(shares, GRID_AXES)  59.7 us
    pallas_call x2, Pallas kernels, finish(): pl.pallas_call(body, grid_spec=pltpu.PrefetchScalarGridSpec(num_scalar_pr...  39.4 us
    pallas_call x8, Pallas kernels, call(): pl.pallas_call(body, grid_spec=pltpu.PrefetchScalarGridSpec(num_scalar_pr...  38 us
    unnamed x260, local copies, waits for them, and re-layouts  29 us
    pallas_call x4, Pallas kernels, scan_call(): pl.pallas_call(body, grid_spec=pltpu.PrefetchScalarGridSpec(num_scalar_pr...  20.3 us
  transfers between devices with their start and end apart: 105, of which 52 were waited for; matrix products, arithmetic and copies ran while one was open for 4% of the time, Pallas kernels for 23%

profile of v5, /device:TPU:0, one launch (start us, length us, event | category | flops | bytes accessed | tf_op | source)
XLA Modules:
  0.0 807.2 jit_solution(14708413767530385808)
XLA Ops:
  89.8 10.2 %collective-permute-done.13.refs_3_ = bf16[1,64,1920]{2,1,0:T(8,128)(2,1)S(1)} collective-permute-done((bf16[1,64,1920]{2,1,0:T(8,128)(2,1)S(1)}, bf16[1,64,1920]{2,1,0:T(8,128)(2,1)S(1)}, u32[]{:S(2)}, u32[]{:S(2)}) %collective-permute-start.13) | collective-permute-done | bytes 245792 | tf_op jit(solution)/shard_map/ppermute | solution.py:32
  117.9 11.3 %collective-permute-done.18.refs_2_ = bf16[128,1152]{1,0:T(8,128)(2,1)S(1)} collective-permute-done((bf16[128,1152]{1,0:T(8,128)(2,1)S(1)}, bf16[128,1152]{1,0:T(8,128)(2,1)S(1)}, u32[]{:S(2)}, u32[]{:S(2)}) %collective-permute-start.18) | collective-permute-done | bytes 294944 | tf_op jit(solution)/shard_map/ppermute | solution.py:32
  216.1 7.7 collective-permute-done.40.refs_2_
  226.4 7.7 collective-permute-done.41.refs_2_.five
  242.1 8.4 %shard_map.231 = (f32[128,1152]{1,0:T(8,128)S(1)}, bf16[128,1152]{1,0:T(8,128)(2,1)S(1)}, bf16[256,2304]{1,0:T(8,128)(2,1)S(1)}) custom-call(s32[3]{0:T(128)S(1)} %pad_add_fusion.2.refs_0_.places, bf16[128,1152]{1,0:T(8,128)(2,1)S(1)} %fusion.12.refs_1_, bf16[128,1152]{1,0:T(8,128)(2,1)S(1)} %collective-permute-done.47.refs_2_, ...), custom_call_target="tpu_custom_call" | custom-call | flops 1 | bytes 1 | tf_op jit(solution)/shard_map/pallas_call | solution.py:904
  308.1 8.0 collective-permute-done.56.refs_1_
  354.1 8.7 %shard_map.245 = (f32[128,1152]{1,0:T(8,128)S(1)}, bf16[128,1152]{1,0:T(8,128)(2,1)S(1)}, bf16[256,2304]{1,0:T(8,128)(2,1)S(1)}) custom-call(s32[3]{0:T(128)S(1)} %pad_add_fusion.refs_0_.places, bf16[128,1152]{1,0:T(8,128)(2,1)} %get-tuple-element.303.refs_1_, bf16[128,1152]{1,0:T(8,128)(2,1)} %collective-permute-done.63.refs_2_, ...), custom_call_target="tpu_custom_call" | custom-call | flops 1 | bytes 1 | tf_op jit(solution)/shard_map/pallas_call | solution.py:904
  377.3 7.8 collective-permute-done.66.refs_2_
  410.3 7.8 collective-permute-start.67
  451.5 13.5 %collective-permute-done.72.refs_2_ = bf16[1,64,1920]{2,1,0:T(8,128)(2,1)S(1)} collective-permute-done((bf16[1,64,1920]{2,1,0:T(8,128)(2,1)S(1)}, bf16[1,64,1920]{2,1,0:T(8,128)(2,1)S(1)}, u32[]{:S(2)}, u32[]{:S(2)}) %collective-permute-start.72) | collective-permute-done | bytes 245792 | tf_op jit(solution)/shard_map/ppermute | solution.py:32
  465.1 8.5 %collective-permute-done.73.refs_3_ = bf16[1,64,1920]{2,1,0:T(8,128)(2,1)S(1)} collective-permute-done((bf16[1,64,1920]{2,1,0:T(8,128)(2,1)S(1)}, bf16[1,64,1920]{2,1,0:T(8,128)(2,1)S(1)}, u32[]{:S(2)}, u32[]{:S(2)}) %collective-permute-start.73) | collective-permute-done | bytes 245792 | tf_op jit(solution)/shard_map/ppermute | solution.py:32
  492.9 9.6 %collective-permute-start.81 = (bf16[2,10,1152]{2,1,0:T(8,128)(2,1)S(1)}, bf16[2,10,1152]{2,1,0:T(8,128)(2,1)S(1)}, u32[]{:S(2)}, u32[]{:S(2)}) collective-permute-start(bf16[2,10,1152]{2,1,0:T(8,128)(2,1)S(1)} %pad_maximum_fusion.14), channel_id=1, source_target_pairs={{0,1},{1,2},{2,3},{4,5},{5,6},{6,7},{8,9},{9,10},{10,11},{12,13},{... | collective-permute-start | bytes 138248 | tf_op jit(solution)/shard_map/ppermute | solution.py:939
  532.7 16.5 %collective-permute-done.76.refs_3_ = bf16[4,144,1152]{2,1,0:T(8,128)(2,1)S(1)} collective-permute-done((bf16[4,144,1152]{2,1,0:T(8,128)(2,1)}, bf16[4,144,1152]{2,1,0:T(8,128)(2,1)S(1)}, u32[]{:S(2)}, u32[]{:S(2)}) %collective-permute-start.76) | collective-permute-done | bytes 1327136 | tf_op jit(solution)/shard_map/ppermute | solution.py:32
  558.4 19.3 %collective-permute-done.86.refs_5_ = bf16[4,144,1152]{2,1,0:T(8,128)(2,1)} collective-permute-done((bf16[4,144,1152]{2,1,0:T(8,128)(2,1)}, bf16[4,144,1152]{2,1,0:T(8,128)(2,1)}, u32[]{:S(2)}, u32[]{:S(2)}) %collective-permute-start.86) | collective-permute-done | bytes 1327136 | tf_op jit(solution)/shard_map/ppermute | solution.py:32
  587.1 18.3 %collective-permute-done.87.refs_1_ = bf16[1,144,1152]{2,1,0:T(8,128)(2,1)S(1)} collective-permute-done((bf16[1,144,1152]{2,1,0:T(8,128)(2,1)S(1)}, bf16[1,144,1152]{2,1,0:T(8,128)(2,1)S(1)}, u32[]{:S(2)}, u32[]{:S(2)}) %collective-permute-start.87) | collective-permute-done | bytes 331808 | tf_op jit(solution)/shard_map/ppermute | solution.py:32
  614.8 8.0 collective-permute-done.93.refs_5_
  622.9 12.4 %collective-permute-done.91.refs_1_ = bf16[1,144,1152]{2,1,0:T(8,128)(2,1)S(1)} collective-permute-done((bf16[1,144,1152]{2,1,0:T(8,128)(2,1)S(1)}, bf16[1,144,1152]{2,1,0:T(8,128)(2,1)S(1)}, u32[]{:S(2)}, u32[]{:S(2)}) %collective-permute-start.91) | collective-permute-done | bytes 331808 | tf_op jit(solution)/shard_map/ppermute | solution.py:32
  639.8 13.5 %collective-permute-done.95.refs_3_ = f32[64,1152]{1,0:T(8,128)S(1)} collective-permute-done((f32[64,1152]{1,0:T(8,128)S(1)}, f32[64,1152]{1,0:T(8,128)S(1)}, u32[]{:S(2)}, u32[]{:S(2)}) %collective-permute-start.95) | collective-permute-done | bytes 294944 | tf_op jit(solution)/shard_map/ppermute | solution.py:32
  655.6 19.2 %collective-permute-done.98.refs_1_ = f32[64,1152]{1,0:T(8,128)S(1)} collective-permute-done((f32[64,1152]{1,0:T(8,128)S(1)}, f32[64,1152]{1,0:T(8,128)S(1)}, u32[]{:S(2)}, u32[]{:S(2)}) %collective-permute-start.98) | collective-permute-done | bytes 294944 | tf_op jit(solution)/shard_map/ppermute | solution.py:32
  681.9 9.2 %shard_map.273 = (f32[2,576,6912]{2,1,0:T(8,128)}, bf16[128,1152]{1,0:T(8,128)(2,1)}) custom-call(f32[576,4]{1,0:T(8,128)S(1)} %copy-done.28, f32[4,6912]{1,0:T(4,128)S(1)} %get-tuple-element.487.values, bf16[128,1152]{1,0:T(8,128)(2,1)} %get-tuple-element.396.refs_0_), custom_call_target="tpu_custom_call", output_to_operand_aliasing={{1}: (2, {})} | custom-call | flops 1 | bytes 1 | tf_op jit(solution)/shard_map/pallas_call | solution.py:1817
  691.8 15.3 %shard_map.274 = (f32[2,2304,1152]{2,1,0:T(8,128)}, f32[2,576,4608]{2,1,0:T(8,128)}, bf16[128,1152]{1,0:T(8,128)(2,1)}) custom-call(s32[1]{0:T(128)} %bitcast.1.m, bf16[16,2,144,1152]{3,2,1,0:T(8,128)(2,1)} %bitcast.119, bf16[16,2,144,1152]{3,2,1,0:T(8,128)(2,1)} %bitcast.120, ...), custom_call_target="tpu_custom_call", output_to_operand_aliasing={{2}: (3, {})} | custom-call | flops 1 | bytes 1 | tf_op jit(solution)/shard_map/pallas_call | solution.py:629
  707.1 9.2 %shard_map.275 = (f32[2,576,6912]{2,1,0:T(8,128)}, bf16[128,1152]{1,0:T(8,128)(2,1)}) custom-call(f32[576,4]{1,0:T(8,128)S(1)} %copy-done.28, f32[4,6912]{1,0:T(4,128)S(1)} %get-tuple-element.485.values, f32[2,576,6912]{2,1,0:T(8,128)} %get-tuple-element.400.refs_0_, ...), custom_call_target="tpu_custom_call", output_to_operand_aliasing={{0}: (2, {}), {1}: (3, {})} | custom-call | flops 1 | bytes 1 | tf_op jit(solution)/shard_map/pallas_call | solution.py:1817
  716.3 59.7 %all-gather.5.cloned.1.call-done = bf16[64,144,1152]{2,1,0:T(8,128)(2,1)} async-done(((bf16[4,144,1152]{2,1,0:T(8,128)(2,1)}), bf16[64,144,1152]{2,1,0:T(8,128)(2,1)}) %all-gather.5.cloned.1.call-update) | async-done | bytes 21233680 | tf_op jit(solution)/shard_map/all_gather | solution.py:574
  776.0 24.1 %shard_map.276 = (f32[2,2304,1152]{2,1,0:T(8,128)}, f32[2,576,4608]{2,1,0:T(8,128)}, f32[2,576,3456]{2,1,0:T(8,128)}, f32[2,576,1152]{2,1,0:T(8,128)}, bf16[128,1152]{1,0:T(8,128)(2,1)}) custom-call(s32[1]{0:T(128)} %bitcast.1.m, bf16[16,4,144,1152]{3,2,1,0:T(8,128)(2,1)} %bitcast.115, ...), custom_call_target="tpu_custom_call", output_to_operand_aliasing={{0}: (5, {}), {1}: (6, {}), {4}: (7, {})} | custom-call | flops 1 | bytes 1 | tf_op jit(solution)/shard_map/pallas_call | solution.py:629
  (598 shorter events, 456.8 us)
Async XLA Ops:
  7.2 400.2 %reduce-scatter.2.cloned.1.call-start = ((), (), s32[]{:S(2)}) async-start(), calls=%async_computation.1 | async-start | bytes 11280384 | tf_op jit(solution)/shard_map/reduce_scatter | solution.py:692
  7.2 26.3 %collective-permute-start.1 = (bf16[2,3456]{1,0:T(2,128)(2,1)}, bf16[2,3456]{1,0:T(2,128)(2,1)}, u32[]{:S(2)}, u32[]{:S(2)}) collective-permute-start(bf16[2,3456]{1,0:T(2,128)(2,1)} %param.15), channel_id=1, source_target_pairs={{0,16},{16,0},{1,17},{17,1},{2,18},{18,2},{3,19},{19,3},{4,20},{20... | collective-permute-start | bytes 41480 | tf_op jit(solution)/shard_map/ppermute | solution.py:32
  11.6 29.9 %collective-permute-start.6 = (bf16[2,9,576]{2,1,0:T(8,128)(2,1)}, bf16[2,9,576]{2,1,0:T(8,128)(2,1)}, u32[]{:S(2)}, u32[]{:S(2)}) collective-permute-start(bf16[2,9,576]{2,1,0:T(8,128)(2,1)} %copy.107), channel_id=1, source_target_pairs={{0,16},{16,0},{1,17},{17,1},{2,18},{18,2},{3,19},{19,3},{4,20},{20... | collective-permute-start | bytes 62216 | tf_op jit(solution)/shard_map/ppermute | solution.py:32
  87.8 48.3 %collective-permute-start.22 = (bf16[144,2304]{1,0:T(8,128)(2,1)S(1)}, bf16[144,2304]{1,0:T(8,128)(2,1)}, u32[]{:S(2)}, u32[]{:S(2)}) collective-permute-start(bf16[144,2304]{1,0:T(8,128)(2,1)S(1)} %get-tuple-element.231.refs_4_.refs_5_), channel_id=1, source_target_pairs={{0,4},{4,0},{8,12},{12,8},{1,5},{5,1},{9,13},{13,9},{2,6},{6,2},{1... | collective-permute-start | bytes 1990664 | tf_op jit(solution)/shard_map/ppermute | solution.py:32
  87.8 48.3 %collective-permute-start.23 = (bf16[144,2304]{1,0:T(8,128)(2,1)}, bf16[144,2304]{1,0:T(8,128)(2,1)}, u32[]{:S(2)}, u32[]{:S(2)}) collective-permute-start(bf16[144,2304]{1,0:T(8,128)(2,1)} %get-tuple-element.232.refs_5_.refs_6_), channel_id=1, source_target_pairs={{0,4},{4,0},{8,12},{12,8},{1,5},{5,1},{9,13},{13,9},{2,6},{6,2},{1... | collective-permute-start | bytes 1990664 | tf_op jit(solution)/shard_map/ppermute | solution.py:32
  132.1 24.3 %collective-permute-start.31 = (bf16[144,1920]{1,0:T(8,128)(2,1)}, bf16[144,1920]{1,0:T(8,128)(2,1)}, u32[]{:S(2)}, u32[]{:S(2)}) collective-permute-start(bf16[144,1920]{1,0:T(8,128)(2,1)} %shard_map.219.refs_0_), channel_id=1, source_target_pairs={{0,8},{4,12},{8,0},{12,4},{1,9},{5,13},{9,1},{13,5},{2,10},{6,14},... | collective-permute-start | bytes 1658888 | tf_op jit(solution)/shard_map/ppermute | solution.py:32
  156.5 28.3 %collective-permute-start.32 = (bf16[144,1920]{1,0:T(8,128)(2,1)}, bf16[144,1920]{1,0:T(8,128)(2,1)S(1)}, u32[]{:S(2)}, u32[]{:S(2)}) collective-permute-start(bf16[144,1920]{1,0:T(8,128)(2,1)} %get-tuple-element.246.refs_5_.refs_6_), channel_id=1, source_target_pairs={{0,4},{4,0},{8,12},{12,8},{1,5},{5,1},{9,13},{13,9},{2,6},{6,2},{1... | collective-permute-start | bytes 1658888 | tf_op jit(solution)/shard_map/ppermute | solution.py:32
  159.2 25.5 %collective-permute-start.33 = (bf16[144,1920]{1,0:T(8,128)(2,1)}, bf16[144,1920]{1,0:T(8,128)(2,1)S(1)}, u32[]{:S(2)}, u32[]{:S(2)}) collective-permute-start(bf16[144,1920]{1,0:T(8,128)(2,1)} %get-tuple-element.247.refs_6_.refs_7_), channel_id=1, source_target_pairs={{0,4},{4,0},{8,12},{12,8},{1,5},{5,1},{9,13},{13,9},{2,6},{6,2},{1... | collective-permute-start | bytes 1658888 | tf_op jit(solution)/shard_map/ppermute | solution.py:32
  174.1 34.7 %collective-permute-start.43 = (bf16[144,2304]{1,0:T(8,128)(2,1)S(1)}, bf16[144,2304]{1,0:T(8,128)(2,1)S(1)}, u32[]{:S(2)}, u32[]{:S(2)}) collective-permute-start(bf16[144,2304]{1,0:T(8,128)(2,1)S(1)} %shard_map.226.refs_0_), channel_id=1, source_target_pairs={{0,8},{4,12},{8,0},{12,4},{1,9},{5,13},{9,1},{13,5},{2,10},{6,14},... | collective-permute-start | bytes 1990664 | tf_op jit(solution)/shard_map/ppermute | solution.py:32
  208.9 25.3 %collective-permute-start.44 = (bf16[144,2304]{1,0:T(8,128)(2,1)S(1)}, bf16[144,2304]{1,0:T(8,128)(2,1)S(1)}, u32[]{:S(2)}, u32[]{:S(2)}) collective-permute-start(bf16[144,2304]{1,0:T(8,128)(2,1)S(1)} %get-tuple-element.261.refs_4_.refs_5_), channel_id=1, source_target_pairs={{0,4},{4,0},{8,12},{12,8},{1,5},{5,1},{9,13},{13,9},{2,6},{6,2},{1... | collective-permute-start | bytes 1990664 | tf_op jit(solution)/shard_map/ppermute | solution.py:32
  209.3 24.9 %collective-permute-start.45 = (bf16[144,2304]{1,0:T(8,128)(2,1)S(1)}, bf16[144,2304]{1,0:T(8,128)(2,1)S(1)}, u32[]{:S(2)}, u32[]{:S(2)}) collective-permute-start(bf16[144,2304]{1,0:T(8,128)(2,1)S(1)} %get-tuple-element.262.refs_5_.refs_6_), channel_id=1, source_target_pairs={{0,4},{4,0},{8,12},{12,8},{1,5},{5,1},{9,13},{13,9},{2,6},{6,2},{1... | collective-permute-start | bytes 1990664 | tf_op jit(solution)/shard_map/ppermute | solution.py:32
  273.0 418.8 %all-gather.7.cloned.1.call-start = ((), (), s32[]{:S(2)}) async-start(), calls=%async_computation.3 | async-start | bytes 11280384 | tf_op jit(solution)/shard_map/all_gather | solution.py:574
  319.6 24.5 %collective-permute-start.57 = (bf16[256,1920]{1,0:T(8,128)(2,1)}, bf16[256,1920]{1,0:T(8,128)(2,1)}, u32[]{:S(2)}, u32[]{:S(2)}) collective-permute-start(bf16[256,1920]{1,0:T(8,128)(2,1)} %shard_map.239.mine), channel_id=1, source_target_pairs={{0,16},{16,0},{1,17},{17,1},{2,18},{18,2},{3,19},{19,3},{4,20},{20... | collective-permute-start | bytes 2949128 | tf_op jit(solution)/shard_map/ppermute | solution.py:32
  410.2 365.8 %all-gather.5.cloned.1.call-start = ((), (), s32[]{:S(2)}) async-start(), calls=%async_computation.2 | async-start | bytes 22560768 | tf_op jit(solution)/shard_map/all_gather | solution.py:574
  418.1 61.8 %collective-permute-start.64 = (bf16[4,144,1152]{2,1,0:T(8,128)(2,1)}, bf16[4,144,1152]{2,1,0:T(8,128)(2,1)S(1)}, u32[]{:S(2)}, u32[]{:S(2)}) collective-permute-start(bf16[4,144,1152]{2,1,0:T(8,128)(2,1)} %copy-done.115), channel_id=1, source_target_pairs={{0,8},{4,12},{8,0},{12,4},{1,9},{5,13},{9,1},{13,5},{2,10},{6,14},... | collective-permute-start | bytes 3981320 | tf_op jit(solution)/shard_map/ppermute | solution.py:32
  448.2 25.4 %collective-permute-start.73 = (bf16[1,64,1920]{2,1,0:T(8,128)(2,1)S(1)}, bf16[1,64,1920]{2,1,0:T(8,128)(2,1)S(1)}, u32[]{:S(2)}, u32[]{:S(2)}) collective-permute-start(bf16[1,64,1920]{2,1,0:T(8,128)(2,1)S(1)} %get-tuple-element.329), channel_id=1, source_target_pairs={{0,2},{1,3},{2,0},{3,1},{4,6},{5,7},{6,4},{7,5},{8,10},{9,11},{10,... | collective-permute-start | bytes 737288 | tf_op jit(solution)/shard_map/ppermute | solution.py:32
  488.0 24.4 %collective-permute-start.77 = (bf16[256,1920]{1,0:T(8,128)(2,1)S(1)}, bf16[256,1920]{1,0:T(8,128)(2,1)S(1)}, u32[]{:S(2)}, u32[]{:S(2)}) collective-permute-start(bf16[256,1920]{1,0:T(8,128)(2,1)S(1)} %shard_map.256.mine), channel_id=1, source_target_pairs={{0,16},{16,0},{1,17},{17,1},{2,18},{18,2},{3,19},{19,3},{4,20},{20... | collective-permute-start | bytes 2949128 | tf_op jit(solution)/shard_map/ppermute | solution.py:32
  517.0 32.2 %collective-permute-start.76 = (bf16[4,144,1152]{2,1,0:T(8,128)(2,1)}, bf16[4,144,1152]{2,1,0:T(8,128)(2,1)S(1)}, u32[]{:S(2)}, u32[]{:S(2)}) collective-permute-start(bf16[4,144,1152]{2,1,0:T(8,128)(2,1)} %get-tuple-element.335), channel_id=1, source_target_pairs={{0,8},{4,12},{8,0},{12,4},{1,9},{5,13},{9,1},{13,5},{2,10},{6,14},... | collective-permute-start | bytes 3981320 | tf_op jit(solution)/shard_map/ppermute | solution.py:32
  517.1 32.1 %collective-permute-start.75 = (bf16[2,144,1152]{2,1,0:T(8,128)(2,1)}, bf16[2,144,1152]{2,1,0:T(8,128)(2,1)S(1)}, u32[]{:S(2)}, u32[]{:S(2)}) collective-permute-start(bf16[2,144,1152]{2,1,0:T(8,128)(2,1)} %get-tuple-element.333), channel_id=1, source_target_pairs={{0,1},{1,0},{2,3},{3,2},{4,5},{5,4},{6,7},{7,6},{8,9},{9,8},{10,11... | collective-permute-start | bytes 1990664 | tf_op jit(solution)/shard_map/ppermute | solution.py:32
  522.3 55.5 %collective-permute-start.86 = (bf16[4,144,1152]{2,1,0:T(8,128)(2,1)}, bf16[4,144,1152]{2,1,0:T(8,128)(2,1)}, u32[]{:S(2)}, u32[]{:S(2)}) collective-permute-start(bf16[4,144,1152]{2,1,0:T(8,128)(2,1)} %get-tuple-element.354), channel_id=1, source_target_pairs={{0,8},{4,12},{8,0},{12,4},{1,9},{5,13},{9,1},{13,5},{2,10},{6,14},... | collective-permute-start | bytes 3981320 | tf_op jit(solution)/shard_map/ppermute | solution.py:32
  549.8 28.0 %collective-permute-start.85 = (bf16[2,144,1152]{2,1,0:T(8,128)(2,1)S(1)}, bf16[2,144,1152]{2,1,0:T(8,128)(2,1)S(1)}, u32[]{:S(2)}, u32[]{:S(2)}) collective-permute-start(bf16[2,144,1152]{2,1,0:T(8,128)(2,1)S(1)} %get-tuple-element.352), channel_id=1, source_target_pairs={{0,1},{1,0},{2,3},{3,2},{4,5},{5,4},{6,7},{7,6},{8,9},{9,8},{10,11... | collective-permute-start | bytes 1990664 | tf_op jit(solution)/shard_map/ppermute | solution.py:32
  554.9 51.3 %collective-permute-start.89 = (bf16[4,144,1152]{2,1,0:T(8,128)(2,1)S(1)}, bf16[4,144,1152]{2,1,0:T(8,128)(2,1)S(1)}, u32[]{:S(2)}, u32[]{:S(2)}) collective-permute-start(bf16[4,144,1152]{2,1,0:T(8,128)(2,1)S(1)} %get-tuple-element.366), channel_id=1, source_target_pairs={{0,8},{4,12},{8,0},{12,4},{1,9},{5,13},{9,1},{13,5},{2,10},{6,14},... | collective-permute-start | bytes 3981320 | tf_op jit(solution)/shard_map/ppermute | solution.py:32
  579.6 26.6 %collective-permute-start.88 = (bf16[2,144,1152]{2,1,0:T(8,128)(2,1)S(1)}, bf16[2,144,1152]{2,1,0:T(8,128)(2,1)S(1)}, u32[]{:S(2)}, u32[]{:S(2)}) collective-permute-start(bf16[2,144,1152]{2,1,0:T(8,128)(2,1)S(1)} %get-tuple-element.364), channel_id=1, source_target_pairs={{0,1},{1,0},{2,3},{3,2},{4,5},{5,4},{6,7},{7,6},{8,9},{9,8},{10,11... | collective-permute-start | bytes 1990664 | tf_op jit(solution)/shard_map/ppermute | solution.py:32
  609.6 26.5 %collective-permute-start.92 = (bf16[2,144,1152]{2,1,0:T(8,128)(2,1)S(1)}, bf16[2,144,1152]{2,1,0:T(8,128)(2,1)S(1)}, u32[]{:S(2)}, u32[]{:S(2)}) collective-permute-start(bf16[2,144,1152]{2,1,0:T(8,128)(2,1)S(1)} %get-tuple-element.382), channel_id=1, source_target_pairs={{0,1},{1,0},{2,3},{3,2},{4,5},{5,4},{6,7},{7,6},{8,9},{9,8},{10,11... | collective-permute-start | bytes 1990664 | tf_op jit(solution)/shard_map/ppermute | solution.py:32
  (208 other events, 2648.0 us)
Sparse Core Ops, SparseCore 0:
  273.1 120.8 reduce-scatter.1
  410.3 115.5 all-gather.6
  654.8 121.1 all-gather.4

commit v6 on v5

--- a/solution.py
+++ b/solution.py
@@ -1838,8 +1838,8 @@
     (1, "P2"): "aB1rL1",
     (1, "P7"): "sC1",
     (0, "P1"): "kC1sA0",
-    (0, "P2"): "kA0sB0gL1",
-    (0, "P3"): "kB0",
+    (0, "P3"): "gL1kA0",
+    (0, "P4"): "sB0kB0",
     (0, "P5"): "tC1",
     (0, "P8"): "sC0kC0tC1tA0",
     (0, "P7"): "tC1tA0tB0sS0",

time: 815 us -> 806 us (0.989)
  waiting for transfers between devices: 360 us -> 340 us
  starting transfers between devices: 155 us -> 174 us
    ppermute x84, waiting for transfers between devices: 274 us -> 247 us  [swap(): return lax.ppermute(value, axis, [(i, i ^ bit) for i in range(count)])]
    ppermute x4, starting transfers between devices: 19.5 us -> 31 us  [halo_edges(): left = lax.ppermute(to_right, 'col', [(i, i + 1) for i in range(cols - 1)])]
    unnamed x260 -> x278, local copies, waits for them, and re-layouts: 29 us -> 31.8 us
  transfers between devices with their start and end apart: 105 -> 105, of which waited for: 52 -> 55; matrix products, arithmetic and copies ran while one was open for 4% -> 4% of each run, Pallas kernels for 23% -> 23%
where the time goes in v6:
time: 806 us; the launch traced here: 799 us
  waiting for transfers between devices  340 us (42%)
  Pallas kernels  211 us (26%)
  starting transfers between devices  174 us (22%)
  local copies, waits for them, and re-layouts  40.2 us (5%)
  between operations  16.3 us (2%)
  matrix products  9.27 us (1%)
  other arithmetic  8.88 us (1%)
    ppermute x84, waiting for transfers between devices, swap(): return lax.ppermute(value, axis, [(i, i ^ bit) for i in range(count)])  247 us
    ppermute x84, starting transfers between devices, swap(): return lax.ppermute(value, axis, [(i, i ^ bit) for i in range(count)])  124 us
    all_gather x2, waiting for transfers between devices, collect(): whole = lax.all_gather(shares, GRID_AXES)  64.1 us
    pallas_call x25, Pallas kernels, call(): pl.pallas_call(whole, in_specs=[pl.BlockSpec(memory_space=pltpu.SMEM)] *...  60.5 us
    pallas_call x2, Pallas kernels, finish(): pl.pallas_call(body, grid_spec=pltpu.PrefetchScalarGridSpec(num_scalar_pr...  39.1 us
    pallas_call x8, Pallas kernels, call(): pl.pallas_call(body, grid_spec=pltpu.PrefetchScalarGridSpec(num_scalar_pr...  35.7 us
    unnamed x278, local copies, waits for them, and re-layouts  31.8 us
    ppermute x4, starting transfers between devices, halo_edges(): left = lax.ppermute(to_right, 'col', [(i, i + 1) for i in range(cols - 1)])  31 us
  transfers between devices with their start and end apart: 105, of which 55 were waited for; matrix products, arithmetic and copies ran while one was open for 4% of the time, Pallas kernels for 23%

profile of v6, /device:TPU:0, one launch (start us, length us, event | category | flops | bytes accessed | tf_op | source)
XLA Modules:
  0.0 799.3 jit_solution(2663915439129801843)
XLA Ops:
  60.8 7.9 collective-permute-done.7.refs_2_.two
  83.8 10.7 %collective-permute-done.13.refs_3_ = bf16[1,64,1920]{2,1,0:T(8,128)(2,1)S(1)} collective-permute-done((bf16[1,64,1920]{2,1,0:T(8,128)(2,1)S(1)}, bf16[1,64,1920]{2,1,0:T(8,128)(2,1)S(1)}, u32[]{:S(2)}, u32[]{:S(2)}) %collective-permute-start.13) | collective-permute-done | bytes 245792 | tf_op jit(solution)/shard_map/ppermute | solution.py:32
  112.0 11.0 %collective-permute-done.18.refs_2_ = bf16[128,1152]{1,0:T(8,128)(2,1)S(1)} collective-permute-done((bf16[128,1152]{1,0:T(8,128)(2,1)S(1)}, bf16[128,1152]{1,0:T(8,128)(2,1)S(1)}, u32[]{:S(2)}, u32[]{:S(2)}) %collective-permute-start.18) | collective-permute-done | bytes 294944 | tf_op jit(solution)/shard_map/ppermute | solution.py:32
  132.7 7.6 shard_map.213
  210.3 8.0 collective-permute-done.40.refs_2_
  220.8 7.7 collective-permute-done.41.refs_2_.five
  236.2 8.4 %shard_map.231 = (f32[128,1152]{1,0:T(8,128)S(1)}, bf16[128,1152]{1,0:T(8,128)(2,1)S(1)}, bf16[256,2304]{1,0:T(8,128)(2,1)S(1)}) custom-call(s32[3]{0:T(128)S(1)} %pad_add_fusion.2.refs_0_.places, bf16[128,1152]{1,0:T(8,128)(2,1)S(1)} %fusion.12.refs_1_, bf16[128,1152]{1,0:T(8,128)(2,1)S(1)} %collective-permute-done.47.refs_2_, ...), custom_call_target="tpu_custom_call" | custom-call | flops 1 | bytes 1 | tf_op jit(solution)/shard_map/pallas_call | solution.py:904
  302.3 8.2 %collective-permute-done.56.refs_1_ = bf16[128,1152]{1,0:T(8,128)(2,1)S(1)} collective-permute-done((bf16[128,1152]{1,0:T(8,128)(2,1)S(1)}, bf16[128,1152]{1,0:T(8,128)(2,1)S(1)}, u32[]{:S(2)}, u32[]{:S(2)}) %collective-permute-start.56) | collective-permute-done | bytes 294944 | tf_op jit(solution)/shard_map/ppermute | solution.py:32
  348.5 8.7 %shard_map.245 = (f32[128,1152]{1,0:T(8,128)S(1)}, bf16[128,1152]{1,0:T(8,128)(2,1)S(1)}, bf16[256,2304]{1,0:T(8,128)(2,1)S(1)}) custom-call(s32[3]{0:T(128)S(1)} %pad_add_fusion.refs_0_.places, bf16[128,1152]{1,0:T(8,128)(2,1)} %get-tuple-element.303.refs_1_, bf16[128,1152]{1,0:T(8,128)(2,1)} %collective-permute-done.63.refs_2_, ...), custom_call_target="tpu_custom_call" | custom-call | flops 1 | bytes 1 | tf_op jit(solution)/shard_map/pallas_call | solution.py:904
  372.8 7.9 collective-permute-done.67.refs_2_.low_other
  391.2 7.7 collective-permute-start.65
  441.8 9.1 %collective-permute-done.74.refs_4_ = bf16[1,64,1920]{2,1,0:T(8,128)(2,1)S(1)} collective-permute-done((bf16[1,64,1920]{2,1,0:T(8,128)(2,1)S(1)}, bf16[1,64,1920]{2,1,0:T(8,128)(2,1)S(1)}, u32[]{:S(2)}, u32[]{:S(2)}) %collective-permute-start.74) | collective-permute-done | bytes 245792 | tf_op jit(solution)/shard_map/ppermute | solution.py:32
  471.3 21.0 %collective-permute-start.81 = (bf16[2,10,1152]{2,1,0:T(8,128)(2,1)S(1)}, bf16[2,10,1152]{2,1,0:T(8,128)(2,1)S(1)}, u32[]{:S(2)}, u32[]{:S(2)}) collective-permute-start(bf16[2,10,1152]{2,1,0:T(8,128)(2,1)S(1)} %pad_maximum_fusion.14), channel_id=1, source_target_pairs={{0,1},{1,2},{2,3},{4,5},{5,6},{6,7},{8,9},{9,10},{10,11},{12,13},{... | collective-permute-start | bytes 138248 | tf_op jit(solution)/shard_map/ppermute | solution.py:939
  524.5 13.5 %collective-permute-done.76.refs_3_ = bf16[4,144,1152]{2,1,0:T(8,128)(2,1)S(1)} collective-permute-done((bf16[4,144,1152]{2,1,0:T(8,128)(2,1)}, bf16[4,144,1152]{2,1,0:T(8,128)(2,1)S(1)}, u32[]{:S(2)}, u32[]{:S(2)}) %collective-permute-start.76) | collective-permute-done | bytes 1327136 | tf_op jit(solution)/shard_map/ppermute | solution.py:32
  551.1 15.5 %collective-permute-done.86.refs_5_ = bf16[4,144,1152]{2,1,0:T(8,128)(2,1)} collective-permute-done((bf16[4,144,1152]{2,1,0:T(8,128)(2,1)S(1)}, bf16[4,144,1152]{2,1,0:T(8,128)(2,1)}, u32[]{:S(2)}, u32[]{:S(2)}) %collective-permute-start.86) | collective-permute-done | bytes 1327136 | tf_op jit(solution)/shard_map/ppermute | solution.py:32
  579.7 15.8 %collective-permute-done.87.refs_1_ = bf16[1,144,1152]{2,1,0:T(8,128)(2,1)S(1)} collective-permute-done((bf16[1,144,1152]{2,1,0:T(8,128)(2,1)S(1)}, bf16[1,144,1152]{2,1,0:T(8,128)(2,1)S(1)}, u32[]{:S(2)}, u32[]{:S(2)}) %collective-permute-start.87) | collective-permute-done | bytes 331808 | tf_op jit(solution)/shard_map/ppermute | solution.py:32
  614.6 10.7 %collective-permute-done.91.refs_1_ = bf16[1,144,1152]{2,1,0:T(8,128)(2,1)S(1)} collective-permute-done((bf16[1,144,1152]{2,1,0:T(8,128)(2,1)S(1)}, bf16[1,144,1152]{2,1,0:T(8,128)(2,1)S(1)}, u32[]{:S(2)}, u32[]{:S(2)}) %collective-permute-start.91) | collective-permute-done | bytes 331808 | tf_op jit(solution)/shard_map/ppermute | solution.py:32
  631.2 9.7 %collective-permute-done.95.refs_3_ = f32[64,1152]{1,0:T(8,128)S(1)} collective-permute-done((f32[64,1152]{1,0:T(8,128)S(1)}, f32[64,1152]{1,0:T(8,128)S(1)}, u32[]{:S(2)}, u32[]{:S(2)}) %collective-permute-start.95) | collective-permute-done | bytes 294944 | tf_op jit(solution)/shard_map/ppermute | solution.py:32
  647.5 15.1 %collective-permute-done.98.refs_1_ = f32[64,1152]{1,0:T(8,128)S(1)} collective-permute-done((f32[64,1152]{1,0:T(8,128)S(1)}, f32[64,1152]{1,0:T(8,128)S(1)}, u32[]{:S(2)}, u32[]{:S(2)}) %collective-permute-start.98) | collective-permute-done | bytes 294944 | tf_op jit(solution)/shard_map/ppermute | solution.py:32
  669.9 9.2 %shard_map.273 = (f32[2,576,6912]{2,1,0:T(8,128)}, bf16[128,1152]{1,0:T(8,128)(2,1)}) custom-call(f32[576,4]{1,0:T(8,128)S(1)} %copy-done.28, f32[4,6912]{1,0:T(4,128)S(1)} %get-tuple-element.487.values, bf16[128,1152]{1,0:T(8,128)(2,1)} %get-tuple-element.396.refs_0_), custom_call_target="tpu_custom_call", output_to_operand_aliasing={{1}: (2, {})} | custom-call | flops 1 | bytes 1 | tf_op jit(solution)/shard_map/pallas_call | solution.py:1817
  679.9 15.0 %shard_map.274 = (f32[2,2304,1152]{2,1,0:T(8,128)}, f32[2,576,4608]{2,1,0:T(8,128)}, bf16[128,1152]{1,0:T(8,128)(2,1)}) custom-call(s32[1]{0:T(128)} %bitcast.1.m, bf16[16,2,144,1152]{3,2,1,0:T(8,128)(2,1)} %bitcast.119, bf16[16,2,144,1152]{3,2,1,0:T(8,128)(2,1)} %bitcast.120, ...), custom_call_target="tpu_custom_call", output_to_operand_aliasing={{2}: (3, {})} | custom-call | flops 1 | bytes 1 | tf_op jit(solution)/shard_map/pallas_call | solution.py:629
  694.9 9.2 %shard_map.275 = (f32[2,576,6912]{2,1,0:T(8,128)}, bf16[128,1152]{1,0:T(8,128)(2,1)}) custom-call(f32[576,4]{1,0:T(8,128)S(1)} %copy-done.28, f32[4,6912]{1,0:T(4,128)S(1)} %get-tuple-element.485.values, f32[2,576,6912]{2,1,0:T(8,128)} %get-tuple-element.400.refs_0_, ...), custom_call_target="tpu_custom_call", output_to_operand_aliasing={{0}: (2, {}), {1}: (3, {})} | custom-call | flops 1 | bytes 1 | tf_op jit(solution)/shard_map/pallas_call | solution.py:1817
  704.1 64.0 %all-gather.5.cloned.1.call-done = bf16[64,144,1152]{2,1,0:T(8,128)(2,1)} async-done(((bf16[4,144,1152]{2,1,0:T(8,128)(2,1)}), bf16[64,144,1152]{2,1,0:T(8,128)(2,1)}) %all-gather.5.cloned.1.call-update) | async-done | bytes 21233680 | tf_op jit(solution)/shard_map/all_gather | solution.py:574
  768.2 24.1 %shard_map.276 = (f32[2,2304,1152]{2,1,0:T(8,128)}, f32[2,576,4608]{2,1,0:T(8,128)}, f32[2,576,3456]{2,1,0:T(8,128)}, f32[2,576,1152]{2,1,0:T(8,128)}, bf16[128,1152]{1,0:T(8,128)(2,1)}) custom-call(s32[1]{0:T(128)} %bitcast.1.m, bf16[16,4,144,1152]{3,2,1,0:T(8,128)(2,1)} %bitcast.115, ...), custom_call_target="tpu_custom_call", output_to_operand_aliasing={{0}: (5, {}), {1}: (6, {}), {4}: (7, {})} | custom-call | flops 1 | bytes 1 | tf_op jit(solution)/shard_map/pallas_call | solution.py:629
  (616 shorter events, 457.0 us)
Async XLA Ops:
  7.2 381.0 %reduce-scatter.2.cloned.1.call-start = ((), (), s32[]{:S(2)}) async-start(), calls=%async_computation.1 | async-start | bytes 11280384 | tf_op jit(solution)/shard_map/reduce_scatter | solution.py:692
  7.2 25.9 %collective-permute-start.1 = (bf16[2,3456]{1,0:T(2,128)(2,1)}, bf16[2,3456]{1,0:T(2,128)(2,1)S(1)}, u32[]{:S(2)}, u32[]{:S(2)}) collective-permute-start(bf16[2,3456]{1,0:T(2,128)(2,1)} %param.15), channel_id=1, source_target_pairs={{0,16},{16,0},{1,17},{17,1},{2,18},{18,2},{3,19},{19,3},{4,20},{20... | collective-permute-start | bytes 41480 | tf_op jit(solution)/shard_map/ppermute | solution.py:32
  11.6 24.8 %collective-permute-start.6 = (bf16[2,9,576]{2,1,0:T(8,128)(2,1)}, bf16[2,9,576]{2,1,0:T(8,128)(2,1)}, u32[]{:S(2)}, u32[]{:S(2)}) collective-permute-start(bf16[2,9,576]{2,1,0:T(8,128)(2,1)} %copy.107), channel_id=1, source_target_pairs={{0,16},{16,0},{1,17},{17,1},{2,18},{18,2},{3,19},{19,3},{4,20},{20... | collective-permute-start | bytes 62216 | tf_op jit(solution)/shard_map/ppermute | solution.py:32
  82.3 48.3 %collective-permute-start.22 = (bf16[144,2304]{1,0:T(8,128)(2,1)S(1)}, bf16[144,2304]{1,0:T(8,128)(2,1)}, u32[]{:S(2)}, u32[]{:S(2)}) collective-permute-start(bf16[144,2304]{1,0:T(8,128)(2,1)S(1)} %get-tuple-element.231.refs_4_.refs_5_), channel_id=1, source_target_pairs={{0,4},{4,0},{8,12},{12,8},{1,5},{5,1},{9,13},{13,9},{2,6},{6,2},{1... | collective-permute-start | bytes 1990664 | tf_op jit(solution)/shard_map/ppermute | solution.py:32
  82.3 48.3 %collective-permute-start.23 = (bf16[144,2304]{1,0:T(8,128)(2,1)}, bf16[144,2304]{1,0:T(8,128)(2,1)}, u32[]{:S(2)}, u32[]{:S(2)}) collective-permute-start(bf16[144,2304]{1,0:T(8,128)(2,1)} %get-tuple-element.232.refs_5_.refs_6_), channel_id=1, source_target_pairs={{0,4},{4,0},{8,12},{12,8},{1,5},{5,1},{9,13},{13,9},{2,6},{6,2},{1... | collective-permute-start | bytes 1990664 | tf_op jit(solution)/shard_map/ppermute | solution.py:32
  150.2 28.9 %collective-permute-start.32 = (bf16[144,1920]{1,0:T(8,128)(2,1)}, bf16[144,1920]{1,0:T(8,128)(2,1)S(1)}, u32[]{:S(2)}, u32[]{:S(2)}) collective-permute-start(bf16[144,1920]{1,0:T(8,128)(2,1)} %get-tuple-element.246.refs_5_.refs_6_), channel_id=1, source_target_pairs={{0,4},{4,0},{8,12},{12,8},{1,5},{5,1},{9,13},{13,9},{2,6},{6,2},{1... | collective-permute-start | bytes 1658888 | tf_op jit(solution)/shard_map/ppermute | solution.py:32
  153.7 25.5 %collective-permute-start.33 = (bf16[144,1920]{1,0:T(8,128)(2,1)}, bf16[144,1920]{1,0:T(8,128)(2,1)S(1)}, u32[]{:S(2)}, u32[]{:S(2)}) collective-permute-start(bf16[144,1920]{1,0:T(8,128)(2,1)} %get-tuple-element.247.refs_6_.refs_7_), channel_id=1, source_target_pairs={{0,4},{4,0},{8,12},{12,8},{1,5},{5,1},{9,13},{13,9},{2,6},{6,2},{1... | collective-permute-start | bytes 1658888 | tf_op jit(solution)/shard_map/ppermute | solution.py:32
  168.6 34.7 %collective-permute-start.43 = (bf16[144,2304]{1,0:T(8,128)(2,1)S(1)}, bf16[144,2304]{1,0:T(8,128)(2,1)S(1)}, u32[]{:S(2)}, u32[]{:S(2)}) collective-permute-start(bf16[144,2304]{1,0:T(8,128)(2,1)S(1)} %shard_map.226.refs_0_), channel_id=1, source_target_pairs={{0,8},{4,12},{8,0},{12,4},{1,9},{5,13},{9,1},{13,5},{2,10},{6,14},... | collective-permute-start | bytes 1990664 | tf_op jit(solution)/shard_map/ppermute | solution.py:32
  203.3 25.3 %collective-permute-start.44 = (bf16[144,2304]{1,0:T(8,128)(2,1)S(1)}, bf16[144,2304]{1,0:T(8,128)(2,1)S(1)}, u32[]{:S(2)}, u32[]{:S(2)}) collective-permute-start(bf16[144,2304]{1,0:T(8,128)(2,1)S(1)} %get-tuple-element.261.refs_4_.refs_5_), channel_id=1, source_target_pairs={{0,4},{4,0},{8,12},{12,8},{1,5},{5,1},{9,13},{13,9},{2,6},{6,2},{1... | collective-permute-start | bytes 1990664 | tf_op jit(solution)/shard_map/ppermute | solution.py:32
  203.7 24.9 %collective-permute-start.45 = (bf16[144,2304]{1,0:T(8,128)(2,1)S(1)}, bf16[144,2304]{1,0:T(8,128)(2,1)S(1)}, u32[]{:S(2)}, u32[]{:S(2)}) collective-permute-start(bf16[144,2304]{1,0:T(8,128)(2,1)S(1)} %get-tuple-element.262.refs_5_.refs_6_), channel_id=1, source_target_pairs={{0,4},{4,0},{8,12},{12,8},{1,5},{5,1},{9,13},{13,9},{2,6},{6,2},{1... | collective-permute-start | bytes 1990664 | tf_op jit(solution)/shard_map/ppermute | solution.py:32
  267.4 412.5 %all-gather.7.cloned.1.call-start = ((), (), s32[]{:S(2)}) async-start(), calls=%async_computation.3 | async-start | bytes 11280384 | tf_op jit(solution)/shard_map/all_gather | solution.py:574
  314.0 24.5 %collective-permute-start.57 = (bf16[256,1920]{1,0:T(8,128)(2,1)}, bf16[256,1920]{1,0:T(8,128)(2,1)}, u32[]{:S(2)}, u32[]{:S(2)}) collective-permute-start(bf16[256,1920]{1,0:T(8,128)(2,1)} %shard_map.239.mine), channel_id=1, source_target_pairs={{0,16},{16,0},{1,17},{17,1},{2,18},{18,2},{3,19},{19,3},{4,20},{20... | collective-permute-start | bytes 2949128 | tf_op jit(solution)/shard_map/ppermute | solution.py:32
  391.2 377.0 %all-gather.5.cloned.1.call-start = ((), (), s32[]{:S(2)}) async-start(), calls=%async_computation.2 | async-start | bytes 22560768 | tf_op jit(solution)/shard_map/all_gather | solution.py:574
  421.5 39.9 %collective-permute-start.64 = (bf16[4,144,1152]{2,1,0:T(8,128)(2,1)}, bf16[4,144,1152]{2,1,0:T(8,128)(2,1)S(1)}, u32[]{:S(2)}, u32[]{:S(2)}) collective-permute-start(bf16[4,144,1152]{2,1,0:T(8,128)(2,1)} %get-tuple-element.307), channel_id=1, source_target_pairs={{0,8},{4,12},{8,0},{12,4},{1,9},{5,13},{9,1},{13,5},{2,10},{6,14},... | collective-permute-start | bytes 3981320 | tf_op jit(solution)/shard_map/ppermute | solution.py:32
  425.9 25.1 %collective-permute-start.74 = (bf16[1,64,1920]{2,1,0:T(8,128)(2,1)S(1)}, bf16[1,64,1920]{2,1,0:T(8,128)(2,1)S(1)}, u32[]{:S(2)}, u32[]{:S(2)}) collective-permute-start(bf16[1,64,1920]{2,1,0:T(8,128)(2,1)S(1)} %get-tuple-element.330), channel_id=1, source_target_pairs={{0,3},{1,2},{2,1},{3,0},{4,7},{5,6},{6,5},{7,4},{8,11},{9,10},{10,... | collective-permute-start | bytes 737288 | tf_op jit(solution)/shard_map/ppermute | solution.py:32
  465.1 35.3 %collective-permute-start.77 = (bf16[256,1920]{1,0:T(8,128)(2,1)S(1)}, bf16[256,1920]{1,0:T(8,128)(2,1)S(1)}, u32[]{:S(2)}, u32[]{:S(2)}) collective-permute-start(bf16[256,1920]{1,0:T(8,128)(2,1)S(1)} %shard_map.256.mine), channel_id=1, source_target_pairs={{0,16},{16,0},{1,17},{17,1},{2,18},{18,2},{3,19},{19,3},{4,20},{20... | collective-permute-start | bytes 2949128 | tf_op jit(solution)/shard_map/ppermute | solution.py:32
  471.3 24.6 %collective-permute-start.81 = (bf16[2,10,1152]{2,1,0:T(8,128)(2,1)S(1)}, bf16[2,10,1152]{2,1,0:T(8,128)(2,1)S(1)}, u32[]{:S(2)}, u32[]{:S(2)}) collective-permute-start(bf16[2,10,1152]{2,1,0:T(8,128)(2,1)S(1)} %pad_maximum_fusion.14), channel_id=1, source_target_pairs={{0,1},{1,2},{2,3},{4,5},{5,6},{6,7},{8,9},{9,10},{10,11},{12,13},{... | collective-permute-start | bytes 138248 | tf_op jit(solution)/shard_map/ppermute | solution.py:939
  505.8 32.2 %collective-permute-start.76 = (bf16[4,144,1152]{2,1,0:T(8,128)(2,1)}, bf16[4,144,1152]{2,1,0:T(8,128)(2,1)S(1)}, u32[]{:S(2)}, u32[]{:S(2)}) collective-permute-start(bf16[4,144,1152]{2,1,0:T(8,128)(2,1)} %copy-done.116), channel_id=1, source_target_pairs={{0,8},{4,12},{8,0},{12,4},{1,9},{5,13},{9,1},{13,5},{2,10},{6,14},... | collective-permute-start | bytes 3981320 | tf_op jit(solution)/shard_map/ppermute | solution.py:32
  507.1 30.9 %collective-permute-start.75 = (bf16[2,144,1152]{2,1,0:T(8,128)(2,1)S(1)}, bf16[2,144,1152]{2,1,0:T(8,128)(2,1)S(1)}, u32[]{:S(2)}, u32[]{:S(2)}) collective-permute-start(bf16[2,144,1152]{2,1,0:T(8,128)(2,1)S(1)} %copy-done.118), channel_id=1, source_target_pairs={{0,1},{1,0},{2,3},{3,2},{4,5},{5,4},{6,7},{7,6},{8,9},{9,8},{10,11... | collective-permute-start | bytes 1990664 | tf_op jit(solution)/shard_map/ppermute | solution.py:32
  513.1 53.5 %collective-permute-start.86 = (bf16[4,144,1152]{2,1,0:T(8,128)(2,1)S(1)}, bf16[4,144,1152]{2,1,0:T(8,128)(2,1)}, u32[]{:S(2)}, u32[]{:S(2)}) collective-permute-start(bf16[4,144,1152]{2,1,0:T(8,128)(2,1)S(1)} %get-tuple-element.354), channel_id=1, source_target_pairs={{0,8},{4,12},{8,0},{12,4},{1,9},{5,13},{9,1},{13,5},{2,10},{6,14},... | collective-permute-start | bytes 3981320 | tf_op jit(solution)/shard_map/ppermute | solution.py:32
  538.6 28.0 %collective-permute-start.85 = (bf16[2,144,1152]{2,1,0:T(8,128)(2,1)S(1)}, bf16[2,144,1152]{2,1,0:T(8,128)(2,1)S(1)}, u32[]{:S(2)}, u32[]{:S(2)}) collective-permute-start(bf16[2,144,1152]{2,1,0:T(8,128)(2,1)S(1)} %get-tuple-element.352), channel_id=1, source_target_pairs={{0,1},{1,0},{2,3},{3,2},{4,5},{5,4},{6,7},{7,6},{8,9},{9,8},{10,11... | collective-permute-start | bytes 1990664 | tf_op jit(solution)/shard_map/ppermute | solution.py:32
  545.9 50.4 %collective-permute-start.89 = (bf16[4,144,1152]{2,1,0:T(8,128)(2,1)}, bf16[4,144,1152]{2,1,0:T(8,128)(2,1)S(1)}, u32[]{:S(2)}, u32[]{:S(2)}) collective-permute-start(bf16[4,144,1152]{2,1,0:T(8,128)(2,1)} %get-tuple-element.366), channel_id=1, source_target_pairs={{0,8},{4,12},{8,0},{12,4},{1,9},{5,13},{9,1},{13,5},{2,10},{6,14},... | collective-permute-start | bytes 3981320 | tf_op jit(solution)/shard_map/ppermute | solution.py:32
  568.4 27.8 %collective-permute-start.88 = (bf16[2,144,1152]{2,1,0:T(8,128)(2,1)S(1)}, bf16[2,144,1152]{2,1,0:T(8,128)(2,1)S(1)}, u32[]{:S(2)}, u32[]{:S(2)}) collective-permute-start(bf16[2,144,1152]{2,1,0:T(8,128)(2,1)S(1)} %get-tuple-element.364), channel_id=1, source_target_pairs={{0,1},{1,0},{2,3},{3,2},{4,5},{5,4},{6,7},{7,6},{8,9},{9,8},{10,11... | collective-permute-start | bytes 1990664 | tf_op jit(solution)/shard_map/ppermute | solution.py:32
  599.6 26.5 %collective-permute-start.92 = (bf16[2,144,1152]{2,1,0:T(8,128)(2,1)S(1)}, bf16[2,144,1152]{2,1,0:T(8,128)(2,1)S(1)}, u32[]{:S(2)}, u32[]{:S(2)}) collective-permute-start(bf16[2,144,1152]{2,1,0:T(8,128)(2,1)S(1)} %get-tuple-element.382), channel_id=1, source_target_pairs={{0,1},{1,0},{2,3},{3,2},{4,5},{5,4},{6,7},{7,6},{8,9},{9,8},{10,11... | collective-permute-start | bytes 1990664 | tf_op jit(solution)/shard_map/ppermute | solution.py:32
  (217 other events, 2680.3 us)
Sparse Core Ops, SparseCore 0:
  267.5 120.5 reduce-scatter.1
  391.3 110.4 all-gather.6
  645.1 122.9 all-gather.4
